TPU v7x, 32 devices: a whole 2x2x4 slice. The times are simulated.
32 devices in a mesh: dp: 16 (over z, x, core), mp: 2 (over y).
Axes of the slice: x: 2, y: 2, z: 4, core: 2. Of those that a mesh axis runs over, the one named last changes fastest.
Arguments:
- tokens: bfloat16 [18464, 1024], P(('dp', 'mp')), may hold values from -6 to 6
- ln1_gain: bfloat16 [1024], P(('dp', 'mp')), may hold values from 0.099609375 to 1.8984375
- ln1_bias: bfloat16 [1024], P(('dp', 'mp')), may hold values from -3 to 3
- qkv_weight: bfloat16 [1024, 3, 1024], P('dp', None, 'mp'), may hold values from -1 to 1
- qv_bias: bfloat16 [2, 16, 64], P(None, 'mp', 'dp'), may hold values from -3 to 3
- proj_weight: bfloat16 [1024, 1024], P('mp', 'dp'), may hold values from -1 to 1
- proj_bias: bfloat16 [1024], P(('dp', 'mp')), may hold values from -3 to 3
- ln2_gain: bfloat16 [1024], P(('dp', 'mp')), may hold values from 0.099609375 to 1.8984375
- ln2_bias: bfloat16 [1024], P(('dp', 'mp')), may hold values from -3 to 3
- fc1_weight: bfloat16 [1024, 4096], P('dp', 'mp'), may hold values from -0.1875 to 0.1875
- fc1_bias: bfloat16 [64, 64], P('mp', 'dp'), may hold values from -3 to 3
- fc2_weight: bfloat16 [4096, 1024], P('mp', 'dp'), may hold values from -0.09375 to 0.09375
- fc2_bias: bfloat16 [1024], P(('dp', 'mp')), may hold values from -3 to 3
- cotangent: bfloat16 [18464, 1024], P(('dp', 'mp')), may hold values from -6 to 6
Outputs:
- output: bfloat16 [18464, 1024], P(('dp', 'mp'))
- grad_tokens: float32 [18464, 1024], P(('dp', 'mp'))
- grad_ln1_gain: float32 [1024], P(('dp', 'mp'))
- grad_ln1_bias: float32 [1024], P(('dp', 'mp'))
- grad_qkv_weight: float32 [1024, 3, 1024], P('dp', None, 'mp')
- grad_qv_bias: float32 [2, 16, 64], P(None, 'mp', 'dp')
- grad_proj_weight: float32 [1024, 1024], P('mp', 'dp')
- grad_proj_bias: float32 [1024], P(('dp', 'mp'))
- grad_ln2_gain: float32 [1024], P(('dp', 'mp'))
- grad_ln2_bias: float32 [1024], P(('dp', 'mp'))
- grad_fc1_weight: float32 [1024, 4096], P('dp', 'mp')
- grad_fc1_bias: float32 [64, 64], P('mp', 'dp')
- grad_fc2_weight: float32 [4096, 1024], P('mp', 'dp')
- grad_fc2_bias: float32 [1024], P(('dp', 'mp'))
All inputs are finite; a program needn't handle non-finite values.
Results may differ from a plain program's by a relative error of at most 0.017.
Values may be sent and summed in bfloat16 or wider, within the bound.
No kernel may reach another device: no remote copies, remote signals or barrier semaphores. Data moves between devices by JAX's collectives and lax.ppermute only.
A program may use at most 192 MiB of HBM per device.

v0:
```python
import math

import jax
import jax.numpy as jnp
from jax import lax
from jax.sharding import PartitionSpec as P

SEQ = 577


EPS = 1e-06
SCALE = 0.125


def norm_rows(inputs, scale_vec, shift_vec):
    row_mean = jnp.mean(inputs, axis=-1, keepdims=True)
    centered = inputs - row_mean
    inv_scale = lax.rsqrt(jnp.mean(jnp.square(centered), axis=-1, keepdims=True) + EPS)
    normed = centered * inv_scale
    return (normed * scale_vec + shift_vec, normed, inv_scale)


def norm_back(upstream, normed, inv_scale, scale_vec):
    scaled = upstream * scale_vec
    first = jnp.mean(scaled, axis=-1, keepdims=True)
    second = jnp.mean(scaled * normed, axis=-1, keepdims=True)
    return inv_scale * (scaled - first - normed * second)


def gelu_slope(values):
    normal_cdf = 0.5 * (1.0 + lax.erf(values * (1.0 / math.sqrt(2.0))))
    density = jnp.exp(-0.5 * values * values) * (1.0 / math.sqrt(2.0 * math.pi))
    return normal_cdf + values * density


def attend(queries, key_heads, value_heads):
    scores = (
        jnp.einsum("qhe,khe->hqk", queries, key_heads, preferred_element_type=jnp.float32) * SCALE
    )
    row_max = jnp.max(scores, axis=-1, keepdims=True)
    shifted = jnp.exp(scores - row_max)
    row_total = jnp.sum(shifted, axis=-1, keepdims=True)
    probs = (shifted / row_total).astype(jnp.bfloat16)
    mixed = jnp.einsum("hqk,khe->qhe", probs, value_heads, preferred_element_type=jnp.float32)
    return (mixed.astype(jnp.bfloat16), (row_max + jnp.log(row_total))[..., 0])


def attend_back(queries, key_heads, value_heads, mixed_grad, log_total):
    scores = (
        jnp.einsum("qhe,khe->hqk", queries, key_heads, preferred_element_type=jnp.float32) * SCALE
    )
    probs = jnp.exp(scores - log_total[..., None])
    value_grad = jnp.einsum(
        "hqk,qhe->khe", probs.astype(jnp.bfloat16), mixed_grad, preferred_element_type=jnp.float32
    )
    prob_grad = jnp.einsum(
        "qhe,khe->hqk", mixed_grad, value_heads, preferred_element_type=jnp.float32
    )
    weighted = jnp.sum(prob_grad * probs, axis=-1, keepdims=True)
    score_grad = (probs * (prob_grad - weighted) * SCALE).astype(jnp.bfloat16)
    query_grad = jnp.einsum(
        "hqk,khe->qhe", score_grad, key_heads, preferred_element_type=jnp.float32
    )
    key_grad = jnp.einsum("hqk,qhe->khe", score_grad, queries, preferred_element_type=jnp.float32)
    return (
        query_grad.astype(jnp.bfloat16),
        key_grad.astype(jnp.bfloat16),
        value_grad.astype(jnp.bfloat16),
    )


def all_rows(member):
    return lax.all_gather(member, "mp", axis=0, tiled=True)


def rows_product(left, product):
    return lax.psum_scatter(
        product(left).astype(jnp.bfloat16), "mp", scatter_dimension=0, tiled=True
    ).astype(jnp.float32)


def on_device(
    tokens,
    ln1_gain,
    ln1_bias,
    qkv_weight,
    qv_bias,
    proj_weight,
    proj_bias,
    ln2_gain,
    ln2_bias,
    fc1_weight,
    fc1_bias,
    fc2_weight,
    fc2_bias,
    cotangent,
):
    vectors = (
        lax.all_gather(ln1_gain, ("dp", "mp"), axis=0, tiled=True),
        lax.all_gather(ln1_bias, ("dp", "mp"), axis=0, tiled=True),
        lax.all_gather(ln2_gain, ("dp", "mp"), axis=0, tiled=True),
        lax.all_gather(ln2_bias, ("dp", "mp"), axis=0, tiled=True),
        lax.all_gather(proj_bias, ("dp", "mp"), axis=0, tiled=True),
        lax.all_gather(fc2_bias, ("dp", "mp"), axis=0, tiled=True),
    )
    gain_one, shift_one, gain_two, shift_two, proj_shift, out_shift = [
        member.astype(jnp.float32) for member in vectors
    ]
    qkv_full, qv_full, proj_full = (
        lax.all_gather(qkv_weight, "dp", axis=0, tiled=True),
        lax.all_gather(qv_bias, "dp", axis=2, tiled=True),
        lax.all_gather(proj_weight, "dp", axis=1, tiled=True),
    )
    local_width = qkv_full.shape[2]
    heads_here = qv_full.shape[1]
    head_size = qv_full.shape[2]
    inputs = tokens.astype(jnp.float32)
    normed_one, hat_one, inv_one = norm_rows(inputs, gain_one, shift_one)
    rows_one = all_rows(normed_one.astype(jnp.bfloat16))
    total_rows = rows_one.shape[0]
    images = total_rows // SEQ
    projected = jnp.einsum("td,dcf->tcf", rows_one, qkv_full, preferred_element_type=jnp.float32)
    qv_flat = qv_full.astype(jnp.float32).reshape(2, local_width)
    head_shape = (images, SEQ, heads_here, head_size)
    queries = (projected[:, 0] + qv_flat[0]).astype(jnp.bfloat16).reshape(head_shape)
    key_heads = projected[:, 1].astype(jnp.bfloat16).reshape(head_shape)
    value_heads = (projected[:, 2] + qv_flat[1]).astype(jnp.bfloat16).reshape(head_shape)
    mixed, log_total = lax.map(
        lambda image_set: attend(*image_set), (queries, key_heads, value_heads)
    )
    mixed_rows = mixed.reshape(total_rows, local_width)
    branch_one = rows_product(
        mixed_rows, lambda block: jnp.dot(block, proj_full, preferred_element_type=jnp.float32)
    )
    residual = inputs + branch_one + proj_shift
    normed_two, hat_two, inv_two = norm_rows(residual, gain_two, shift_two)
    rows_two = all_rows(normed_two.astype(jnp.bfloat16))
    fc1_full, fc1_bias_full, fc2_full = (
        lax.all_gather(fc1_weight, "dp", axis=0, tiled=True),
        lax.all_gather(fc1_bias, "dp", axis=1, tiled=True),
        lax.all_gather(fc2_weight, "dp", axis=1, tiled=True),
    )
    hidden_pre = jnp.dot(
        rows_two, fc1_full, preferred_element_type=jnp.float32
    ) + fc1_bias_full.astype(jnp.float32).reshape(-1)
    hidden = (0.5 * hidden_pre * (1.0 + lax.erf(hidden_pre * (1.0 / math.sqrt(2.0))))).astype(
        jnp.bfloat16
    )
    branch_two = rows_product(
        hidden, lambda block: jnp.dot(block, fc2_full, preferred_element_type=jnp.float32)
    )
    output = (residual + branch_two + out_shift).astype(jnp.bfloat16)
    upstream = cotangent.astype(jnp.float32)
    grad_out_shift = jnp.sum(upstream, axis=0)
    down_rows = all_rows(upstream.astype(jnp.bfloat16))
    fc1_back, fc2_back = (
        lax.all_gather(fc1_weight, "dp", axis=0, tiled=True),
        lax.all_gather(fc2_weight, "dp", axis=1, tiled=True),
    )
    grad_fc2 = jnp.einsum("tf,td->fd", hidden, down_rows, preferred_element_type=jnp.float32)
    hidden_grad = (
        jnp.einsum("td,fd->tf", down_rows, fc2_back, preferred_element_type=jnp.float32)
        * gelu_slope(hidden_pre)
    ).astype(jnp.bfloat16)
    grad_fc1_shift = jnp.sum(hidden_grad.astype(jnp.float32), axis=0).reshape(fc1_bias_full.shape)
    grad_fc1 = jnp.einsum("td,tf->df", rows_two, hidden_grad, preferred_element_type=jnp.float32)
    back_two = rows_product(
        hidden_grad,
        lambda block: jnp.einsum("tf,df->td", block, fc1_back, preferred_element_type=jnp.float32),
    )
    grad_gain_two = jnp.sum(back_two * hat_two, axis=0)
    grad_shift_two = jnp.sum(back_two, axis=0)
    resid_grad = upstream + norm_back(back_two, hat_two, inv_two, gain_two)
    grad_proj_shift = jnp.sum(resid_grad, axis=0)
    attn_rows = all_rows(resid_grad.astype(jnp.bfloat16))
    qkv_back, proj_back = (
        lax.all_gather(qkv_weight, "dp", axis=0, tiled=True),
        lax.all_gather(proj_weight, "dp", axis=1, tiled=True),
    )
    grad_proj = jnp.einsum("tf,td->fd", mixed_rows, attn_rows, preferred_element_type=jnp.float32)
    mixed_grad = (
        jnp.einsum("td,fd->tf", attn_rows, proj_back, preferred_element_type=jnp.float32)
        .astype(jnp.bfloat16)
        .reshape(head_shape)
    )
    query_grad, key_grad, value_grad = lax.map(
        lambda image_set: attend_back(*image_set),
        (queries, key_heads, value_heads, mixed_grad, log_total),
    )
    stacked = jnp.stack(
        [
            query_grad.reshape(total_rows, local_width),
            key_grad.reshape(total_rows, local_width),
            value_grad.reshape(total_rows, local_width),
        ],
        axis=1,
    )
    grad_qkv = jnp.einsum("td,tcf->dcf", rows_one, stacked, preferred_element_type=jnp.float32)
    grad_qv = jnp.sum(stacked[:, 0::2].astype(jnp.float32), axis=0).reshape(qv_full.shape)
    back_one = rows_product(
        stacked,
        lambda block: jnp.einsum(
            "tcf,dcf->td", block, qkv_back, preferred_element_type=jnp.float32
        ),
    )
    grad_gain_one = jnp.sum(back_one * hat_one, axis=0)
    grad_shift_one = jnp.sum(back_one, axis=0)
    grad_tokens = resid_grad + norm_back(back_one, hat_one, inv_one, gain_one)
    grad_fc1_own, grad_fc1_shift_own, grad_fc2_own = (
        lax.psum_scatter(grad_fc1, "dp", scatter_dimension=0, tiled=True),
        lax.psum_scatter(grad_fc1_shift, "dp", scatter_dimension=1, tiled=True),
        lax.psum_scatter(grad_fc2, "dp", scatter_dimension=1, tiled=True),
    )
    grad_qkv_own, grad_qv_own, grad_proj_own = (
        lax.psum_scatter(grad_qkv, "dp", scatter_dimension=0, tiled=True),
        lax.psum_scatter(grad_qv, "dp", scatter_dimension=2, tiled=True),
        lax.psum_scatter(grad_proj, "dp", scatter_dimension=1, tiled=True),
    )
    (
        grad_gain_one_own,
        grad_shift_one_own,
        grad_gain_two_own,
        grad_shift_two_own,
        grad_proj_shift_own,
        grad_out_shift_own,
    ) = (
        lax.psum_scatter(grad_gain_one, ("dp", "mp"), scatter_dimension=0, tiled=True),
        lax.psum_scatter(grad_shift_one, ("dp", "mp"), scatter_dimension=0, tiled=True),
        lax.psum_scatter(grad_gain_two, ("dp", "mp"), scatter_dimension=0, tiled=True),
        lax.psum_scatter(grad_shift_two, ("dp", "mp"), scatter_dimension=0, tiled=True),
        lax.psum_scatter(grad_proj_shift, ("dp", "mp"), scatter_dimension=0, tiled=True),
        lax.psum_scatter(grad_out_shift, ("dp", "mp"), scatter_dimension=0, tiled=True),
    )
    return (
        output,
        grad_tokens,
        grad_gain_one_own,
        grad_shift_one_own,
        grad_qkv_own,
        grad_qv_own,
        grad_proj_own,
        grad_proj_shift_own,
        grad_gain_two_own,
        grad_shift_two_own,
        grad_fc1_own,
        grad_fc1_shift_own,
        grad_fc2_own,
        grad_out_shift_own,
    )


def solution(mesh):
    return jax.shard_map(
        on_device,
        mesh=mesh,
        in_specs=(
            P(("dp", "mp"), None),
            P(("dp", "mp")),
            P(("dp", "mp")),
            P("dp", None, "mp"),
            P(None, "mp", "dp"),
            P("mp", "dp"),
            P(("dp", "mp")),
            P(("dp", "mp")),
            P(("dp", "mp")),
            P("dp", "mp"),
            P("mp", "dp"),
            P("mp", "dp"),
            P(("dp", "mp")),
            P(("dp", "mp"), None),
        ),
        out_specs=(
            P(("dp", "mp"), None),
            P(("dp", "mp"), None),
            P(("dp", "mp")),
            P(("dp", "mp")),
            P("dp", None, "mp"),
            P(None, "mp", "dp"),
            P("mp", "dp"),
            P(("dp", "mp")),
            P(("dp", "mp")),
            P(("dp", "mp")),
            P("dp", "mp"),
            P("mp", "dp"),
            P("mp", "dp"),
            P(("dp", "mp")),
        ),
        check_vma=False,
    )
```

profile of v0, /device:TPU:1, one launch (start us, length us, event | category | flops | bytes accessed | tf_op | source)
XLA Modules:
  0.0 996.4 jit_solution(9959881547775632615)
XLA Ops:
  12.4 41.2 %all-reduce.24 = (bf16[1024]{0:T(1024)(128)(2,1)S(1)}, bf16[1024]{0:T(1024)(128)(2,1)S(1)}, bf16[1024]{0:T(1024)(128)(2,1)S(1)}, bf16[1024]{0:T(1024)(128)(2,1)S...) all-reduce(bf16[1024]{0:T(1024)(128)(2,1)S(1)} %dynamic-update-slic, ...), channel_id=1, replica_groups=mesh['dp'=16,'mp'=2] {'dp','mp'}, use_global_device_ids=true, to_apply=%add.4 | all-reduce | flops 6144 | bytes 24576
  61.1 22.5 %all_gather.56 = bf16[2,8,64]{1,0,2:T(2,128)(2,1)S(1)} all-gather(bf16[2,8,4]{1,0,2:T(2,128)(2,1)S(1)} %copy.74), channel_id=1, replica_groups=mesh['dp'=16,'mp'=2] {'dp'}, dimensions={2}, use_global_device_ids=true | all-gather | bytes 2176 | tf_op jit(solution)/shard_map/all_gather | solution.py:111
  83.8 12.4 %all-gather.22.cloned.1.call-done = bf16[2,577,1024]{2,1,0:T(8,128)(2,1)} async-done(((bf16[1,577,1024]{2,1,0:T(8,128)(2,1)}), bf16[2,577,1024]{2,1,0:T(8,128)(2,1)}) %all-gather.22.cloned.1.call-update) | async-done | bytes 2363408 | tf_op jit(solution)/shard_map/all_gather | solution.py:73
  99.8 44.3 %all-gather.14.cloned.1.call-done = bf16[1024,3,512]{2,0,1:T(8,128)(2,1)} async-done(((bf16[64,3,512]{2,0,1:T(8,128)(2,1)}), bf16[1024,3,512]{2,0,1:T(8,128)(2,1)}) %all-gather.14.cloned.1.call-update) | async-done | bytes 3145744 | tf_op jit(solution)/shard_map/all_gather | solution.py:110
  186.7 18.7 %while.26 = (s32[]{:T(128)}, bf16[2,577,8,64]{1,3,2,0:T(8,128)(2,1)}, f32[2,8,577]{2,1,0:T(8,128)S(1)}, bf16[2,577,8,64]{1,3,2,0:T(8,128)(2,1)}, bf16[2,577,8,64...) while((s32[]{:T(128)}, bf16[2,577,8,64]{1,3,2,0:T(8,128)(2,1)}, ...), condition=%wide.region_5.6_spmd, body=%wide.region_2.5_spmd.sunk | while | flops 706100224 | bytes 50229580 | solution.py:128
  218.3 31.9 %fusion = bf16[584,1024]{1,0:T(8,128)(2,1)S(1)} fusion(bf16[1154,1024]{1,0:T(8,128)(2,1)} %convolution_convert_fusion.2), kind=kCustom, calls=%all-reduce-scatter | all-reduce-scatter fusion | flops 1196033 | bytes 3559936
  264.3 20.8 %all-gather.2 = bf16[16,4,32]{2,1,0:T(4,128)(2,1)S(1)} all-gather(bf16[1,4,32]{2,1,0:T(4,128)(2,1)S(1)} %bitcast.164), channel_id=1, replica_groups=mesh['dp'=16,'mp'=2] {'dp'}, dimensions={0}, use_global_device_ids=true | all-gather | bytes 4352 | tf_op jit(solution)/shard_map/all_gather | solution.py:140
  288.9 11.4 %all-gather.24.cloned.1.call-done = bf16[2,577,1024]{2,1,0:T(8,128)(2,1)} async-done(((bf16[1,577,1024]{2,1,0:T(8,128)(2,1)}), bf16[2,577,1024]{2,1,0:T(8,128)(2,1)}) %all-gather.24.cloned.1.call-update) | async-done | bytes 2363408 | tf_op jit(solution)/shard_map/all_gather | solution.py:73
  303.8 49.5 %all-gather.18.cloned.1.call-done = bf16[1024,2048]{1,0:T(8,128)(2,1)} async-done(((bf16[64,2048]{1,0:T(8,128)(2,1)}), bf16[1024,2048]{1,0:T(8,128)(2,1)}) %all-gather.18.cloned.1.call-update) | async-done | bytes 4194320 | tf_op jit(solution)/shard_map/all_gather | solution.py:139
  353.3 11.5 %multiply_convert_fusion.1 = (bf16[1154,2048]{1,0:T(8,128)(2,1)}, f32[1154,2048]{1,0:T(8,128)}) fusion(f32[2048]{0:T(1024)S(1)} %reshape.139, bf16[1154,1024]{1,0:T(8,128)(2,1)} %reshape.155, bf16[1024,2048]{1,0:T(8,128)(2,1)} %all-gather.18.cloned.1.call-done), kind=kOutput, calls=%fused_computation.77 | convolution fusion | flops 4854407168 | bytes 20746240 | tf_op jit(solution)/shard_map/dot_general | solution.py:143
  364.8 39.8 %all-gather.20.cloned.1.call-done = bf16[2048,1024]{0,1:T(8,128)(2,1)} async-done(((bf16[2048,64]{0,1:T(8,128)(2,1)}), bf16[2048,1024]{0,1:T(8,128)(2,1)}) %all-gather.20.cloned.1.call-update) | async-done | bytes 4194320 | tf_op jit(solution)/shard_map/all_gather | solution.py:141
  404.6 12.4 %convert_reduce_fusion = (f32[2048]{0:T(1024)}, bf16[1154,2048]{1,0:T(8,128)(2,1)S(1)}) fusion(f32[1154,2048]{1,0:T(8,128)} %get-tuple-element.242, bf16[1154,1024]{1,0:T(8,128)(2,1)} %reshape.159, bf16[2048,1024]{0,1:T(8,128)(2,1)} %all-gather.20.cloned.1.call-done), kind=kOutput, calls=%fused_computation.76 | convolution fusion | flops 4868585472 | bytes 20746240 | tf_op jit(solution)/shard_map/td,fd->tf/dot_general | solution.py:162
  425.6 32.6 %fusion.2 = bf16[584,1024]{1,0:T(8,128)(2,1)} fusion(bf16[1154,1024]{1,0:T(8,128)(2,1)} %convolution_convert_fusion), kind=kCustom, calls=%all-reduce-scatter.2 | all-reduce-scatter fusion | flops 1196033 | bytes 3559936
  479.1 37.5 %all-gather.28.cloned.1.call-done = bf16[2,577,1024]{2,1,0:T(8,128)(2,1)} async-done(((bf16[1,577,1024]{2,1,0:T(8,128)(2,1)}), bf16[2,577,1024]{2,1,0:T(8,128)(2,1)}) %all-gather.28.cloned.1.call-update) | async-done | bytes 2363408 | tf_op jit(solution)/shard_map/all_gather | solution.py:73
  538.6 113.9 %while.27 = (s32[]{:T(128)}, bf16[2,577,8,64]{1,3,2,0:T(8,128)(2,1)}, bf16[2,577,8,64]{1,3,2,0:T(8,128)(2,1)}, bf16[2,577,8,64]{1,3,2,0:T(8,128)(2,1)}, bf16[2,5...) while((s32[]{:T(128)}, ...), condition=%wide.region_15.16_spmd, body=%wide.region_13.15_spmd.sunk | while | flops 1761425152 | bytes 187717072 | solution.py:186
  553.2 21.1 %fusion.195 = bf16[2,577,8,64]{1,3,2,0:T(8,128)(2,1)} fusion(bf16[2,577,8,64]{1,3,2,0:T(8,128)(2,1)} %get-tuple-element.376, s32[]{:T(128)S(6)} %copy.137, f32[8,577,577]{1,2,0:T(8,128)} %fusion.192, f32[8,577,577]{1,2,0:T(8,128)} %copy-done, f32[8,577]{1,0:T(8,128)S(1)} %dynamic-slice_bitcast_fusion.2, ...), kind=kOutput, calls=%fused_computation.40.clone.1 | convolution fusion | flops 365190784 | bytes 49193984 | tf_op jit(solution)/shard_map/while/body/eval_jaxpr/hqk,qhe->khe/dot_general | solution.py:64
  574.2 21.4 %fusion.194 = bf16[2,577,8,64]{1,3,2,0:T(8,128)(2,1)} fusion(bf16[2,577,8,64]{1,3,2,0:T(8,128)(2,1)} %get-tuple-element.375, s32[]{:T(128)S(6)} %copy.137, f32[8,577,577]{1,2,0:T(8,128)} %fusion.192, f32[8,577,577]{1,2,0:T(8,128)} %copy-done, f32[8,577]{1,0:T(8,128)S(1)} %dynamic-slice_bitcast_fusion.2, bf16[2,577,8,64]{1,3,2,0:T(8,128)(2,1)} %get-tuple-element.388), kind=kOutput, calls=%fused_computation.42.clone.1 | convolution fusion | flops 365190784 | bytes 49193984 | tf_op jit(solution)/shard_map/while/body/eval_jaxpr/hqk,khe->qhe/dot_general | solution.py:61
  610.0 21.1 %fusion.195 = bf16[2,577,8,64]{1,3,2,0:T(8,128)(2,1)} fusion(bf16[2,577,8,64]{1,3,2,0:T(8,128)(2,1)} %get-tuple-element.376, s32[]{:T(128)S(6)} %copy.137, f32[8,577,577]{1,2,0:T(8,128)} %fusion.192, f32[8,577,577]{1,2,0:T(8,128)} %copy-done, f32[8,577]{1,0:T(8,128)S(1)} %dynamic-slice_bitcast_fusion.2, ...), kind=kOutput, calls=%fused_computation.40.clone.1 | convolution fusion | flops 365190784 | bytes 49193984 | tf_op jit(solution)/shard_map/while/body/eval_jaxpr/hqk,qhe->khe/dot_general | solution.py:64
  631.0 21.4 %fusion.194 = bf16[2,577,8,64]{1,3,2,0:T(8,128)(2,1)} fusion(bf16[2,577,8,64]{1,3,2,0:T(8,128)(2,1)} %get-tuple-element.375, s32[]{:T(128)S(6)} %copy.137, f32[8,577,577]{1,2,0:T(8,128)} %fusion.192, f32[8,577,577]{1,2,0:T(8,128)} %copy-done, f32[8,577]{1,0:T(8,128)S(1)} %dynamic-slice_bitcast_fusion.2, bf16[2,577,8,64]{1,3,2,0:T(8,128)(2,1)} %get-tuple-element.388), kind=kOutput, calls=%fused_computation.42.clone.1 | convolution fusion | flops 365190784 | bytes 49193984 | tf_op jit(solution)/shard_map/while/body/eval_jaxpr/hqk,khe->qhe/dot_general | solution.py:61
  695.5 10.8 %fusion.135 = f32[1024,2048]{1,0:T(8,128)} fusion(bf16[1154,1024]{1,0:T(8,128)(2,1)} %reshape.155, bf16[1154,2048]{1,0:T(8,128)(2,1)} %copy-done.44), kind=kOutput, calls=%fused_computation.151 | convolution fusion | flops 4840226816 | bytes 15478784 | tf_op jit(solution)/shard_map/td,tf->df/dot_general | solution.py:166
  726.8 57.8 %fusion.128 = (bf16[584,1024]{1,0:T(8,128)(2,1)S(1)}, bf16[584,1024]{1,0:T(8,128)(2,1)}) fusion(bf16[1154,1024]{1,0:T(8,128)(2,1)} %convolution_convert_fusion.1, bf16[1154,1024]{1,0:T(8,128)(2,1)} %bitcast_convert_fusion), kind=kCustom, calls=%all-reduce-scatter.4 | all-reduce-scatter fusion | flops 2392065 | bytes 7119360
  789.4 60.7 %all-reduce.23 = (f32[2,8,64]{1,0,2:T(2,128)S(1)}, f32[32,64]{1,0:T(8,128)S(1)}) all-reduce(f32[2,8,64]{1,0,2:T(2,128)S(1)} %copy.95, f32[32,64]{1,0:T(8,128)S(1)} %reshape.138), channel_id=9, replica_groups=mesh['dp'=16,'mp'=2] {'dp'}, use_global_device_ids=true, to_apply=%region_25.26.clone | all-reduce | flops 3072 | bytes 24576
  861.5 41.1 %all-reduce.22 = (f32[1024]{0:T(1024)S(1)}, f32[1024]{0:T(1024)S(1)}, f32[1024]{0:T(1024)S(1)}, f32[1024]{0:T(1024)S(1)}, f32[1024]{0:T(1024)S(1)}, /*index=5*/f32[1024]{0:T(1024)S(1)}) all-reduce(f32[1024]{0:T(1024)S(1)} %get-tuple-element.176, f32[1024]{0:T(1024)S(1)} %get-tuple-element.181, ...), channel_id=6, replica_groups=mesh['dp'=16,'mp'=2] {'dp','mp'}, use_global_device_ids=true, to_apply=%region_20.21.clone | all-reduce | flops 6144 | bytes 49152
  918.7 70.4 %reduce-scatter.18.cloned.1.call-done = f32[64,2048]{1,0:T(8,128)} async-done(((f32[1024,2048]{1,0:T(8,128)}), f32[64,2048]{1,0:T(8,128)}) %reduce-scatter.18.cloned.1.call-update) | async-done | bytes 524304 | tf_op jit(solution)/shard_map/reduce_scatter | solution.py:210
  (264 shorter events, 285.9 us)
Async XLA Ops:
  7.2 89.0 %all-gather.22.cloned.1.call-start = ((), (), s32[]{:S(2)}) async-start(), calls=%async_computation.12 | async-start | bytes 3588096 | tf_op jit(solution)/shard_map/all_gather | solution.py:73
  59.0 85.1 %all-gather.14.cloned.1.call-start = ((), (), s32[]{:S(2)}) async-start(), calls=%async_computation.4 | async-start | bytes 3342336 | tf_op jit(solution)/shard_map/all_gather | solution.py:110
  59.7 153.9 %all-gather.16.cloned.1.call-start = ((), (), s32[]{:S(2)}) async-start(), calls=%async_computation.5 | async-start | bytes 1114112 | tf_op jit(solution)/shard_map/all_gather | solution.py:112
  60.5 224.8 %all-gather.26.cloned.1.call-start = ((), (), s32[]{:S(2)}) async-start(), calls=%async_computation.14 | async-start | bytes 3588096 | tf_op jit(solution)/shard_map/all_gather | solution.py:73
  61.0 239.2 %all-gather.24.cloned.1.call-start = ((), (), s32[]{:S(2)}) async-start(), calls=%async_computation.13 | async-start | bytes 3588096 | tf_op jit(solution)/shard_map/all_gather | solution.py:73
  250.2 3.5 collective-permute-start
  253.7 219.7 %copy-start.25 = (f32[1024]{0:T(1024)}, f32[1024]{0:T(1024)S(1)}, u32[]{:S(2)}) copy-start(f32[1024]{0:T(1024)S(1)} %convert_element_type.136) | copy-start | bytes 12292
  259.3 214.1 %copy-start.3 = (bf16[591,1024]{1,0:T(8,128)(2,1)}, bf16[591,1024]{1,0:T(8,128)(2,1)S(1)}, u32[]{:S(2)}) copy-start(bf16[591,1024]{1,0:T(8,128)(2,1)S(1)} %concatenate) | copy-start | bytes 3631108
  262.9 90.4 %all-gather.18.cloned.1.call-start = ((), (), s32[]{:S(2)}) async-start(), calls=%async_computation.6 | async-start | bytes 4456448 | tf_op jit(solution)/shard_map/all_gather | solution.py:139
  263.5 141.1 %all-gather.20.cloned.1.call-start = ((), (), s32[]{:S(2)}) async-start(), calls=%async_computation.7 | async-start | bytes 4456448 | tf_op jit(solution)/shard_map/all_gather | solution.py:141
  264.3 252.3 %all-gather.28.cloned.1.call-start = ((), (), s32[]{:S(2)}) async-start(), calls=%async_computation.15 | async-start | bytes 3588096 | tf_op jit(solution)/shard_map/all_gather | solution.py:73
  458.9 3.0 collective-permute-start.2
  479.0 439.6 %reduce-scatter.16.cloned.1.call-start = ((), (), s32[]{:S(2)}) async-start(), calls=%async_computation.9 | async-start | bytes 2228224 | tf_op jit(solution)/shard_map/reduce_scatter | solution.py:217
  524.7 393.9 %reduce-scatter.14.cloned.1.call-start = ((), (), s32[]{:S(2)}) async-start(), calls=%async_computation.8 | async-start | bytes 6684672 | tf_op jit(solution)/shard_map/reduce_scatter | solution.py:215
  685.2 233.5 %reduce-scatter.20.cloned.1.call-start = ((), (), s32[]{:S(2)}) async-start(), calls=%async_computation.11 | async-start | bytes 8912896 | tf_op jit(solution)/shard_map/reduce_scatter | solution.py:212
  695.5 293.6 %reduce-scatter.18.cloned.1.call-start = ((), (), s32[]{:S(2)}) async-start(), calls=%async_computation.10 | async-start | bytes 8912896 | tf_op jit(solution)/shard_map/reduce_scatter | solution.py:210
  784.6 66.8 %copy-start.16 = (bf16[584,1024]{1,0:T(8,128)(2,1)}, bf16[584,1024]{1,0:T(8,128)(2,1)S(1)}, u32[]{:S(2)}) copy-start(bf16[584,1024]{1,0:T(8,128)(2,1)S(1)} %get-tuple-element.228) | copy-start | bytes 3588100
  784.6 74.1 %copy-start.2 = (bf16[577,1024]{1,0:T(8,128)(2,1)S(1)}, bf16[577,1024]{1,0:T(8,128)(2,1)}, u32[]{:S(2)}) copy-start(bf16[577,1024]{1,0:T(8,128)(2,1)} %param.18) | copy-start | bytes 3545092
  784.6 74.1 %copy-start.28 = (f32[577]{0:T(1024)S(1)}, f32[577]{0:T(1024)}, u32[]{:S(2)}) copy-start(f32[577]{0:T(1024)} %copy-done.27) | copy-start | bytes 6928
  784.6 74.1 %copy-start.30 = (f32[1024]{0:T(1024)S(1)}, f32[1024]{0:T(1024)}, u32[]{:S(2)}) copy-start(f32[1024]{0:T(1024)} %copy-done.29) | copy-start | bytes 12292
  784.6 74.1 %copy-start.32 = (f32[577]{0:T(1024)S(1)}, f32[577]{0:T(1024)}, u32[]{:S(2)}) copy-start(f32[577]{0:T(1024)} %copy-done.31) | copy-start | bytes 6928
  785.5 65.9 %collective-permute-start.3 = (bf16[7,1024]{1,0:T(8,128)(2,1)S(1)}, bf16[7,1024]{1,0:T(8,128)(2,1)S(1)}, u32[]{:S(2)}, u32[]{:S(2)}) collective-permute-start(bf16[7,1024]{1,0:T(8,128)(2,1)S(1)} %slice.35), channel_id=1, source_target_pairs={{0,1},{2,3},{4,5},{6,7},{8,9},{10,11},{12,13},{14,15},{16,17},{18,... | collective-permute-start | bytes 43016
  787.9 118.2 %collective-permute-start.1 = (bf16[7,1024]{1,0:T(8,128)(2,1)S(1)}, bf16[7,1024]{1,0:T(8,128)(2,1)S(1)}, u32[]{:S(2)}, u32[]{:S(2)}) collective-permute-start(bf16[7,1024]{1,0:T(8,128)(2,1)S(1)} %slice.33), channel_id=1, source_target_pairs={{0,1},{2,3},{4,5},{6,7},{8,9},{10,11},{12,13},{14,15},{16,17},{18,... | collective-permute-start | bytes 43016
  858.7 54.7 %copy-start.4 = (bf16[591,1024]{1,0:T(8,128)(2,1)S(1)}, bf16[591,1024]{1,0:T(8,128)(2,1)}, u32[]{:S(2)}) copy-start(bf16[591,1024]{1,0:T(8,128)(2,1)} %copy-done.3) | copy-start | bytes 3631108
  (43 other events, 342.7 us)
Sparse Core Ops, SparseCore 0:
  59.1 37.0 all-gather.21
  98.4 45.6 all-gather.13
  146.2 36.7 all-gather.15
  184.4 34.9 all-gather.25
  263.0 37.1 all-gather.23
  302.3 50.9 all-gather.17
  355.5 49.0 all-gather.19
  479.1 37.3 all-gather.27
  524.8 60.0 reduce-scatter.15
  685.3 84.6 reduce-scatter.13
  774.6 105.4 reduce-scatter.19
  884.6 104.3 reduce-scatter.17
where the time goes:
time: 1000 us; the launch traced here: 996 us
  blocking collectives  309 us (31%)
  waiting for transfers between devices  269 us (27%)
  matrix products  219 us (22%)
  local copies, waits for them, and re-layouts  140 us (14%)
  other arithmetic  34.6 us (3%)
  between operations  16.6 us (2%)
    unnamed x6, blocking collectives  265 us
    reduce_scatter x1, waiting for transfers between devices, on_device(): lax.psum_scatter(grad_fc1, 'dp', scatter_dimension=0, tiled=True)  70.4 us
    unnamed x117, local copies, waits for them, and re-layouts  63.7 us
    all_gather x4, waiting for transfers between devices, all_rows(): return lax.all_gather(member, 'mp', axis=0, tiled=True)  61.3 us
    all_gather x1, waiting for transfers between devices, on_device(): lax.all_gather(fc1_weight, 'dp', axis=0, tiled=True)  49.5 us
    all_gather x1, waiting for transfers between devices, on_device(): lax.all_gather(qkv_weight, 'dp', axis=0, tiled=True)  44.3 us
    dot_general x2, matrix products, attend_back(): jnp.einsum('hqk,khe->qhe', score_grad, key_heads, preferred_element_type=...  42.8 us
    dot_general x2, matrix products, attend_back(): jnp.einsum('hqk,qhe->khe', score_grad, queries, preferred_element_type=jn...  42.1 us
  transfers between devices with their start and end apart: 16, of which 8 were waited for; matrix products, arithmetic and copies ran while one was open for 42% of the time, Pallas kernels for 0%

commit v1 on v0

v1 whole, which is shorter than its diff:
```python
import functools
import itertools
import math

import jax
import jax.numpy as jnp
import numpy as np
from jax import lax
from jax.experimental import pallas as pl
from jax.experimental.pallas import tpu as pltpu
from jax.sharding import Mesh
from jax.sharding import PartitionSpec as P

SEQ = 577
ROWS = 592
HEAD = 64
EPS = 1e-06
ALL = ("z", "x", "c", "y")
F32 = jnp.float32
BF16 = jnp.bfloat16

NN = (((1,), (0,)), ((), ()))
NT = (((1,), (1,)), ((), ()))
TN = (((0,), (0,)), ((), ()))
VMEM_LIMIT = 48 * 2**20


def dot(left, right, dims=NN):
    return lax.dot_general(left, right, dims, preferred_element_type=F32)


def attend_kernel(heads, qkv_ref, mixed_ref, probs_ref):
    width = heads * HEAD
    for pair in range(heads // 2):
        at = pair * 128
        queries = qkv_ref[:, at : at + 128]
        keys = qkv_ref[:, width + at : width + at + 128]
        values = qkv_ref[:, 2 * width + at : 2 * width + at + 128]
        lane = lax.broadcasted_iota(jnp.int32, (ROWS, 128), 1)
        row = lax.broadcasted_iota(jnp.int32, (ROWS, ROWS), 0)
        mixed = []
        for half in range(2):
            inside = (lane < HEAD) if half == 0 else (lane >= HEAD)
            own_keys = jnp.where(inside, keys, jnp.zeros_like(keys)) * BF16(0.125)
            scores = dot(own_keys, queries, NT)
            scores = jnp.where(row < SEQ, scores, -1e30)
            shifted = jnp.exp(scores - jnp.max(scores, axis=0, keepdims=True))
            total = jnp.sum(shifted, axis=0, keepdims=True)
            probs = (shifted * (1.0 / total)).astype(BF16)
            probs_ref[0, 2 * pair + half] = probs
            mixed.append(dot(probs, values, TN))
        mixed_ref[:, at : at + 128] = jnp.where(lane < HEAD, mixed[0], mixed[1]).astype(BF16)


def attend(projected, heads):
    width = heads * HEAD
    return pl.pallas_call(
        functools.partial(attend_kernel, heads),
        grid=(2,),
        in_specs=[pl.BlockSpec((ROWS, 3 * width), lambda i: (i, 0))],
        out_specs=[
            pl.BlockSpec((ROWS, width), lambda i: (i, 0)),
            pl.BlockSpec((1, heads, ROWS, ROWS), lambda i: (i, 0, 0, 0)),
        ],
        out_shape=[
            jax.ShapeDtypeStruct((2 * ROWS, width), BF16),
            jax.ShapeDtypeStruct((2, heads, ROWS, ROWS), BF16),
        ],
        compiler_params=pltpu.CompilerParams(vmem_limit_bytes=VMEM_LIMIT),
        cost_estimate=pl.CostEstimate(
            flops=12 * heads * ROWS * ROWS * 256,
            bytes_accessed=2 * 2 * heads * ROWS * (ROWS + 256),
            transcendentals=2 * heads * ROWS * ROWS,
        ),
    )(projected)


def attend_back_kernel(heads, qkv_ref, probs_ref, grad_ref, out_ref):
    width = heads * HEAD
    for pair in range(heads // 2):
        at = pair * 128
        queries = qkv_ref[:, at : at + 128]
        keys = qkv_ref[:, width + at : width + at + 128]
        values = qkv_ref[:, 2 * width + at : 2 * width + at + 128]
        grad = grad_ref[:, at : at + 128]
        lane = lax.broadcasted_iota(jnp.int32, (ROWS, 128), 1)
        keys_t = (keys * BF16(0.125)).T
        queries_s = queries * BF16(0.125)
        d_query, d_key, d_value = [], [], []
        for half in range(2):
            inside = (lane < HEAD) if half == 0 else (lane >= HEAD)
            own_values = jnp.where(inside, values, jnp.zeros_like(values))
            low_probs = probs_ref[0, 2 * pair + half]
            prob_grad = dot(own_values, grad, NT)
            probs = low_probs.astype(F32)
            product = prob_grad * probs
            weighted = jnp.sum(product, axis=0, keepdims=True)
            score_grad = (product - probs * weighted).astype(BF16)
            d_value.append(dot(low_probs, grad))
            d_key.append(dot(score_grad, queries_s))
            d_query.append(dot(keys_t[half * HEAD : (half + 1) * HEAD], score_grad))
        out_ref[:, at : at + 128] = jnp.concatenate(d_query, 0).T.astype(BF16)
        out_ref[:, width + at : width + at + 128] = jnp.where(
            lane < HEAD, d_key[0], d_key[1]
        ).astype(BF16)
        out_ref[:, 2 * width + at : 2 * width + at + 128] = jnp.where(
            lane < HEAD, d_value[0], d_value[1]
        ).astype(BF16)


def attend_back(projected, probs, mixed_grad, heads):
    width = heads * HEAD
    return pl.pallas_call(
        functools.partial(attend_back_kernel, heads),
        grid=(2,),
        in_specs=[
            pl.BlockSpec((ROWS, 3 * width), lambda i: (i, 0)),
            pl.BlockSpec((1, heads, ROWS, ROWS), lambda i: (i, 0, 0, 0)),
            pl.BlockSpec((ROWS, width), lambda i: (i, 0)),
        ],
        out_specs=pl.BlockSpec((ROWS, 3 * width), lambda i: (i, 0)),
        out_shape=jax.ShapeDtypeStruct((2 * ROWS, 3 * width), BF16),
        compiler_params=pltpu.CompilerParams(vmem_limit_bytes=VMEM_LIMIT),
        cost_estimate=pl.CostEstimate(
            flops=20 * heads * ROWS * ROWS * 256,
            bytes_accessed=2 * 2 * heads * ROWS * (ROWS + 448),
            transcendentals=0,
        ),
    )(projected, probs, mixed_grad)


def place(parts, spots, shape, block):
    def kernel(spot_ref, *refs):
        out_ref, sems = refs[-2], refs[-1]
        copies = []
        for n in range(len(parts)):
            copies.append(
                pltpu.make_async_copy(refs[n], block(out_ref, spot_ref[n]), sems.at[n])
            )
        for copy in copies:
            copy.start()
        for copy in copies:
            copy.wait()

    size = math.prod(shape) * 2
    return pl.pallas_call(
        kernel,
        grid_spec=pltpu.PrefetchScalarGridSpec(
            num_scalar_prefetch=1,
            grid=(1,),
            in_specs=[pl.BlockSpec(memory_space=pl.ANY)] * len(parts),
            out_specs=pl.BlockSpec(memory_space=pl.ANY),
            scratch_shapes=[pltpu.SemaphoreType.DMA((len(parts),))],
        ),
        out_shape=jax.ShapeDtypeStruct(shape, parts[0].dtype),
        compiler_params=pltpu.CompilerParams(vmem_limit_bytes=2**20),
        cost_estimate=pl.CostEstimate(flops=0, bytes_accessed=2 * size, transcendentals=0),
    )(spots, *parts)


def row_stats(values):
    mean = jnp.mean(values, axis=-1, keepdims=True)
    centered = values - mean
    inv = lax.rsqrt(jnp.mean(jnp.square(centered), axis=-1, keepdims=True) + EPS)
    return mean, inv


def norm_back(upstream, normed, inv_scale, gain):
    scaled = upstream * gain
    first = jnp.mean(scaled, axis=-1, keepdims=True)
    second = jnp.mean(scaled * normed, axis=-1, keepdims=True)
    return inv_scale * (scaled - first - normed * second)


def build(n_z, n_x):
    sizes = dict(z=n_z, x=n_x, c=2, y=2)

    def pairs(move, only=None):
        found = []
        names = ALL
        spots = list(itertools.product(*[range(sizes[a]) for a in names]))
        index = {spot: n for n, spot in enumerate(spots)}
        for spot in spots:
            here = dict(zip(names, spot))
            if only is not None and not only(here):
                continue
            there = dict(here)
            move(there)
            found.append((index[spot], index[tuple(there[a] for a in names)]))
        return found

    def shift(axis, by, only=None):
        def move(spot):
            spot[axis] = (spot[axis] + by) % sizes[axis]

        return pairs(move, only)

    def send(value, perm):
        return lax.ppermute(value, ALL, perm)

    def is_owner(spot):
        return spot["c"] == spot["y"]

    def not_owner(spot):
        return spot["c"] != spot["y"]

    def on_device(
        tokens,
        ln1_gain,
        ln1_bias,
        qkv_weight,
        qv_bias,
        proj_weight,
        proj_bias,
        ln2_gain,
        ln2_bias,
        fc1_weight,
        fc1_bias,
        fc2_weight,
        fc2_bias,
        cotangent,
    ):
        z, x, c, y = [lax.axis_index(a) for a in ALL]
        owner = c == y
        width = tokens.shape[1]
        depth = fc1_weight.shape[0]
        pair = 2 * depth
        heads = qv_bias.shape[1] // 2

        def swap(value):
            return send(value, shift("c", 1))

        def chunks(arrays):
            own = jnp.concatenate(arrays, axis=1)
            other = swap(own)
            both = jnp.where(c == 0, jnp.stack([own, other]), jnp.stack([other, own]))
            both = both.reshape(pair, own.shape[1])
            return both

        quarter = proj_weight.shape[0] // 2
        proj_t = proj_weight.T
        fc2_t = fc2_weight.T
        parts = []
        for colour in range(2):
            cut = slice(colour * quarter, (colour + 1) * quarter)
            parts += [qkv_weight[:, n, cut] for n in range(3)] + [proj_t[:, cut]]
        first = chunks(parts)
        span = 4 * quarter
        rest = chunks([fc1_weight, fc2_t])
        hidden_half = fc1_weight.shape[1] // 2
        groups = [
            (first[:, :span], first[:, span:]),
            (rest[:, :hidden_half], rest[:, hidden_half : 2 * hidden_half]),
            (rest[:, 2 * hidden_half : 3 * hidden_half], rest[:, 3 * hidden_half :]),
        ]

        z_spots = (z + jnp.arange(n_z, dtype=jnp.int32)) % n_z
        x_spots = (x + jnp.arange(n_x, dtype=jnp.int32)) % n_x

        def gather_a(chunk):
            wide = chunk.shape[1]
            moved = send(chunk, shift("y", 1, is_owner))
            chunk = jnp.where(owner, chunk, moved)
            bufs = [chunk]
            for _ in range(n_z - 1):
                bufs.append(send(bufs[-1], shift("z", -1)))
            column = place(bufs, z_spots, (n_z, pair, wide), lambda ref, n: ref.at[n])
            bufs = [column]
            for _ in range(n_x - 1):
                bufs.append(send(bufs[-1], shift("x", -1)))
            whole = place(bufs, x_spots, (n_z, n_x, pair, wide), lambda ref, n: ref.at[:, n])
            return whole.reshape(width, wide)

        def gather_b(chunk):
            wide = chunk.shape[1]
            bufs = [chunk]
            for _ in range(n_x - 1):
                bufs.append(send(bufs[-1], shift("x", -1, is_owner)))
            line = place(bufs, x_spots, (n_x, pair, wide), lambda ref, n: ref.at[n])
            bufs = [line]
            for _ in range(n_z - 1):
                bufs.append(send(bufs[-1], shift("z", -1, is_owner)))
            plane = place(bufs, z_spots, (n_z, n_x, pair, wide), lambda ref, n: ref.at[n])
            moved = send(plane, shift("y", 1, is_owner))
            return jnp.where(owner, plane, moved).reshape(width, wide)

        def add(left, right):
            return (left.astype(F32) + right.astype(F32)).astype(BF16)

        def finish(total):
            first, second = total[:depth], total[depth:]
            moved = swap(jnp.where(c == 0, second, first))
            kept = jnp.where(c == 0, first, second)
            return jnp.where(owner, kept, moved).astype(F32)

        def pick(array, axis, index):
            return lax.dynamic_index_in_dim(array, index, axis, keepdims=False)

        def scatter_a(grad):
            grad = grad.reshape(n_z, n_x, pair, grad.shape[1])
            total = pick(grad, 1, (x + n_x - 1) % n_x)
            for k in range(n_x - 2, -1, -1):
                total = add(send(total, shift("x", 1)), pick(grad, 1, (x + k) % n_x))
            lines = total
            total = pick(lines, 0, (z + n_z - 1) % n_z)
            for k in range(n_z - 2, -1, -1):
                total = add(send(total, shift("z", 1)), pick(lines, 0, (z + k) % n_z))
            return finish(add(send(total, shift("y", 1, not_owner)), total))

        def scatter_b(grad):
            grad = add(send(grad, shift("y", 1, not_owner)), grad)
            grad = grad.reshape(n_z, n_x, pair, grad.shape[1])
            total = pick(grad, 0, (z + n_z - 1) % n_z)
            for k in range(n_z - 2, -1, -1):
                total = add(send(total, shift("z", 1, is_owner)), pick(grad, 0, (z + k) % n_z))
            lines = total
            total = pick(lines, 0, (x + n_x - 1) % n_x)
            for k in range(n_x - 2, -1, -1):
                total = add(send(total, shift("x", 1, is_owner)), pick(lines, 0, (x + k) % n_x))
            return finish(total)

        small = jnp.concatenate(
            [ln1_gain, ln1_bias, ln2_gain, ln2_bias, proj_bias, fc2_bias]
            + [qv_bias.reshape(-1), fc1_bias.reshape(-1)]
        )[None]
        where_am_i = dict(z=z, x=x, c=c, y=y)
        for axis in ("c", "y", "x", "z"):
            count = sizes[axis]
            stacked = jnp.stack([small] + [send(small, shift(axis, -k)) for k in range(1, count)])
            start = (count - where_am_i[axis]) % count
            small = lax.dynamic_slice_in_dim(jnp.concatenate([stacked] * 2), start, count, 0)
        share = ln1_gain.shape[0]
        small = small.reshape(n_z, n_x, 2, 2, -1)
        small = small.transpose(0, 1, 3, 2, 4)
        vectors = small[..., : 6 * share].reshape(-1, 6, share).transpose(1, 0, 2).reshape(6, -1)
        gain_one, shift_one, gain_two, shift_two, proj_shift, out_shift = vectors.astype(F32)
        mine = pick(small[..., 6 * share :], 3, c).astype(F32)
        per_qv = qv_bias.shape[2]
        n_qv = qv_bias.size
        qv_half = mine[..., :n_qv].reshape((-1,) + qv_bias.shape)
        qv_half = qv_half.transpose(1, 2, 0, 3).reshape(2, -1)
        per_fc1 = fc1_bias.shape[1]
        fc1_half = mine[..., n_qv:].reshape((-1,) + fc1_bias.shape)
        fc1_half = fc1_half.transpose(1, 0, 2).reshape(-1)

        def both_images(value):
            value = jnp.pad(value, ((0, ROWS - SEQ), (0, 0)))
            return jnp.concatenate([value, swap(value)])

        inputs = both_images(tokens)
        down = both_images(cotangent)

        def own(value):
            return value[:ROWS]

        def exchanged(partial):
            moved = swap(partial.astype(BF16)).astype(F32)
            return partial + jnp.concatenate([moved[ROWS:], moved[:ROWS]])

        def exchanged_own(partial):
            return partial[:ROWS] + swap(partial[ROWS:].astype(BF16)).astype(F32)

        attn_a, attn_b = gather_a(groups[0][0]), gather_b(groups[0][1])
        fc1_a, fc1_b = gather_a(groups[1][0]), gather_b(groups[1][1])
        fc2_a, fc2_b = gather_a(groups[2][0]), gather_b(groups[2][1])
        n_qkv = 3 * quarter

        wide_in = inputs.astype(F32)
        mean_one, inv_one = row_stats(wide_in)
        hat_one = (wide_in - mean_one) * inv_one
        normed_one = (hat_one * gain_one + shift_one).astype(BF16)

        mixed, probs, projected = [], [], []
        for colour, weight in enumerate((attn_a, attn_b)):
            cut = slice(colour * quarter, (colour + 1) * quarter)
            bias = jnp.concatenate(
                [qv_half[0, cut], jnp.zeros((quarter,), F32), qv_half[1, cut]]
            )
            here = (dot(normed_one, weight[:, :n_qkv]) + bias).astype(BF16)
            out, prob = attend(here, heads)
            projected.append(here)
            mixed.append(out)
            probs.append(prob)
        proj_ab = [attn_a[:, n_qkv:], attn_b[:, n_qkv:]]
        branch_one = dot(mixed[0], proj_ab[0], NT) + dot(mixed[1], proj_ab[1], NT)
        residual = wide_in + exchanged(branch_one) + proj_shift
        mean_two, inv_two = row_stats(residual)
        hat_two = (residual - mean_two) * inv_two
        normed_two = (hat_two * gain_two + shift_two).astype(BF16)

        hidden, slope = [], []
        for colour, weight in enumerate((fc1_a, fc1_b)):
            bias = fc1_half[colour * hidden_half : (colour + 1) * hidden_half]
            pre = dot(normed_two, weight) + bias
            cdf = 0.5 * (1.0 + lax.erf(pre * (1.0 / math.sqrt(2.0))))
            density = jnp.exp(-0.5 * pre * pre) * (1.0 / math.sqrt(2.0 * math.pi))
            hidden.append((pre * cdf).astype(BF16))
            slope.append((cdf + pre * density).astype(BF16))

        grad_fc2 = [dot(down, h, TN).astype(BF16) for h in hidden]
        scat_fc2 = [scatter_a(grad_fc2[0]), scatter_b(grad_fc2[1])]
        hidden_grad = [
            (dot(down, w) * s.astype(F32)).astype(BF16) for w, s in zip((fc2_a, fc2_b), slope)
        ]
        back_two = exchanged(dot(hidden_grad[0], fc1_a, NT) + dot(hidden_grad[1], fc1_b, NT))
        grad_fc1 = [dot(normed_two, g, TN).astype(BF16) for g in hidden_grad]
        scat_fc1 = [scatter_a(grad_fc1[0]), scatter_b(grad_fc1[1])]
        grad_fc1_shift = jnp.concatenate([jnp.sum(g.astype(F32), axis=0) for g in hidden_grad])

        branch_two = dot(hidden[0], fc2_a, NT) + dot(hidden[1], fc2_b, NT)
        output = (own(residual) + exchanged_own(branch_two) + out_shift).astype(BF16)[:SEQ]

        upstream = down.astype(F32)
        resid_grad = upstream + norm_back(back_two, hat_two, inv_two, gain_two)
        attn_grad = resid_grad.astype(BF16)

        parts, back_one, grad_qv = [], [], []
        for colour, weight in enumerate((attn_a, attn_b)):
            mixed_grad = dot(attn_grad, weight[:, n_qkv:]).astype(BF16)
            qkv_grad = attend_back(projected[colour], probs[colour], mixed_grad, heads)
            grad_qkv = dot(normed_one, qkv_grad, TN).astype(BF16)
            grad_proj = dot(attn_grad, mixed[colour], TN).astype(BF16)
            parts.append(jnp.concatenate([grad_qkv, grad_proj], axis=1))
            back_one.append(dot(qkv_grad, weight[:, :n_qkv], NT))
            grad_qv.append(jnp.sum(qkv_grad.astype(F32), axis=0))
        scat_attn = [scatter_a(parts[0]), scatter_b(parts[1])]
        back_one = exchanged_own(back_one[0] + back_one[1])
        hat_own = own(hat_one)
        grad_tokens = own(resid_grad) + norm_back(back_one, hat_own, own(inv_one), gain_one)

        six = [
            jnp.sum(back_one * hat_own, axis=0),
            jnp.sum(back_one, axis=0),
            jnp.sum(own(back_two) * own(hat_two), axis=0),
            jnp.sum(own(back_two), axis=0),
            jnp.sum(own(resid_grad), axis=0),
            jnp.sum(own(upstream), axis=0),
        ]
        halves = [g[:quarter] for g in grad_qv] + [g[2 * quarter :] for g in grad_qv]
        sums = jnp.concatenate(six + halves + [grad_fc1_shift])[None]
        for axis in ("z", "x", "y"):
            moved = [send(sums, shift(axis, k)) for k in range(1, sizes[axis])]
            sums = functools.reduce(jnp.add, moved, sums)
        moved = swap(sums)[0]
        sums = sums[0]
        spot = ((z * n_x + x) * 2 + c) * 2 + y
        small_own = (sums[: 6 * width] + moved[: 6 * width]).reshape(6, -1, share)
        small_own = pick(small_own, 1, spot)
        half = jnp.where(owner, sums[6 * width :], moved[6 * width :])
        deep = (z * n_x + x) * 2 + c
        grad_qv = half[: 4 * quarter].reshape(2, qv_bias.shape[1], -1, per_qv)
        grad_qv = pick(grad_qv, 2, deep)
        grad_fc1_bias = pick(half[4 * quarter :].reshape(fc1_bias.shape[0], -1, per_fc1), 1, deep)

        def joined(index):
            cut = slice(index * quarter, (index + 1) * quarter)
            return jnp.concatenate([s[:, cut] for s in scat_attn], axis=1)

        grad_qkv = jnp.stack([joined(0), joined(1), joined(2)], axis=1)
        return (
            output,
            grad_tokens[:SEQ],
            small_own[0],
            small_own[1],
            grad_qkv,
            grad_qv,
            joined(3).T,
            small_own[4],
            small_own[2],
            small_own[3],
            jnp.concatenate(scat_fc1, axis=1),
            grad_fc1_bias,
            jnp.concatenate(scat_fc2, axis=1).T,
            small_own[5],
        )

    return on_device


def solution(mesh):
    chips = mesh.shape["dp"] // 2
    n_x = 1
    while n_x * n_x * 4 <= chips and chips % (n_x * 2) == 0:
        n_x *= 2
    n_z = chips // n_x
    fine = Mesh(np.asarray(mesh.devices).reshape(n_z, n_x, 2, 2), ALL)
    dp = ("z", "x", "c")
    every = P(ALL)
    rows = P(ALL, None)
    in_specs = (
        rows,
        every,
        every,
        P(dp, None, "y"),
        P(None, "y", dp),
        P("y", dp),
        every,
        every,
        every,
        P(dp, "y"),
        P("y", dp),
        P("y", dp),
        every,
        rows,
    )
    out_specs = (
        rows,
        rows,
        every,
        every,
        P(dp, None, "y"),
        P(None, "y", dp),
        P("y", dp),
        every,
        every,
        every,
        P(dp, "y"),
        P("y", dp),
        P("y", dp),
        every,
    )
    return jax.shard_map(
        build(n_z, n_x), mesh=fine, in_specs=in_specs, out_specs=out_specs, check_vma=False
    )
```

time: 1000 us -> 624 us (0.62)
  blocking collectives: 309 us -> 0 us
  starting transfers between devices: 8.51 us -> 175 us
  waiting for transfers between devices: 269 us -> 141 us
  matrix products: 219 us -> 93.7 us
  local copies, waits for them, and re-layouts: 140 us -> 73.3 us
  Pallas kernels: 0 us -> 47.7 us
  other arithmetic: 34.6 us -> 80.1 us
  between operations: 16.6 us -> 3.38 us
    unnamed x6 -> x0, blocking collectives: 265 us -> none
    all_gather x8 -> x0, waiting for transfers between devices: 195 us -> none  [the longest x4 61.3 us: all_rows(): return lax.all_gather(member, 'mp', axis=0, tiled=True)]
    ppermute x0 -> x86, starting transfers between devices: none -> 175 us  [send(): return lax.ppermute(value, ALL, perm)]
    ppermute x0 -> x86, waiting for transfers between devices: none -> 141 us  [send(): return lax.ppermute(value, ALL, perm)]
    dot_general x26 -> x24, matrix products: 219 us -> 93.7 us  [dot(): return lax.dot_general(left, right, dims, preferred_element_type=F32)]
    reduce_scatter x4 -> x0, waiting for transfers between devices: 70.4 us -> none  [the longest x1 70.4 us: on_device(): lax.psum_scatter(grad_fc1, 'dp', scatter_dimension=0, tiled=True)]
    pallas_call x0 -> x16, Pallas kernels: none -> 47.7 us  [the longest x2 20 us: attend_back(): pl.pallas_call(functools.partial(attend_back_kernel, heads), grid=(2,), i...]
    all_gather x2 -> x0, blocking collectives: 43.3 us -> none  [the longest x1 22.5 us: on_device(): lax.all_gather(qv_bias, 'dp', axis=2, tiled=True)]
  transfers between devices with their start and end apart: 16 -> 86, of which waited for: 8 -> 25; matrix products, arithmetic and copies ran while one was open for 42% -> 30% of each run, Pallas kernels for 0% -> 8%
where the time goes in v1:
time: 624 us; the launch traced here: 614 us
  starting transfers between devices  175 us (28%)
  waiting for transfers between devices  141 us (23%)
  matrix products  93.7 us (15%)
  other arithmetic  80.1 us (13%)
  local copies, waits for them, and re-layouts  73.3 us (12%)
  Pallas kernels  47.7 us (8%)
    ppermute x86, starting transfers between devices, send(): return lax.ppermute(value, ALL, perm)  175 us
    ppermute x86, waiting for transfers between devices, send(): return lax.ppermute(value, ALL, perm)  141 us
    dot_general x24, matrix products, dot(): return lax.dot_general(left, right, dims, preferred_element_type=F32)  93.7 us
    unnamed x154, local copies, waits for them, and re-layouts  22.8 us
    pallas_call x2, Pallas kernels, attend_back(): pl.pallas_call(functools.partial(attend_back_kernel, heads), grid=(2,), i...  20 us
    dynamic_slice x8, local copies, waits for them, and re-layouts, pick(): return lax.dynamic_index_in_dim(array, index, axis, keepdims=False)  19.6 us
    convert_element_type x30, other arithmetic, add(): return (left.astype(F32) + right.astype(F32)).astype(BF16)  18.5 us
    pallas_call x2, Pallas kernels, attend(): pl.pallas_call(functools.partial(attend_kernel, heads), grid=(2,), in_spe...  15.1 us
  transfers between devices with their start and end apart: 86, of which 25 were waited for; matrix products, arithmetic and copies ran while one was open for 30% of the time, Pallas kernels for 8%

profile of v1, /device:TPU:1, one launch (start us, length us, event | category | flops | bytes accessed | tf_op | source)
XLA Modules:
  0.0 614.2 jit_solution(1321331714794798068)
XLA Ops:
  34.4 5.8 collective-permute-done.8
  48.4 9.2 %collective-permute-done.25 = bf16[128,1024]{1,0:T(8,128)(2,1)S(1)} collective-permute-done((bf16[128,1024]{1,0:T(8,128)(2,1)S(1)}, bf16[128,1024]{1,0:T(8,128)(2,1)S(1)}, u32[]{:S(2)}, u32[]{:S(2)}) %collective-permute-start.25) | collective-permute-done | bytes 262176 | tf_op jit(solution)/shard_map/ppermute | solution.py:199
  102.3 7.5 %shard_map.247 = (bf16[1184,256]{1,0:T(8,128)(2,1)S(1)}, bf16[2,4,592,592]{3,2,1,0:T(8,128)(2,1)}) custom-call(bf16[1184,768]{1,0:T(8,128)(2,1)S(1)} %fusion.14.qkv_ref), custom_call_target="tpu_custom_call" | custom-call | flops 4306501632 | bytes 8032256 | tf_op jit(solution)/shard_map/pallas_call | solution.py:57
  109.8 51.1 %collective-permute-start.41 = (bf16[592,1024]{1,0:T(8,128)(2,1)}, bf16[592,1024]{1,0:T(8,128)(2,1)}, u32[]{:S(2)}, u32[]{:S(2)}) collective-permute-start(bf16[592,1024]{1,0:T(8,128)(2,1)} %pad.8), channel_id=1, source_target_pairs={{0,2},{1,3},{2,0},{3,1},{4,6},{5,7},{6,4},{7,5},{8,10},{9,11},{10,... | collective-permute-start | bytes 3637256 | tf_op jit(solution)/shard_map/ppermute | solution.py:199
  170.2 7.6 %shard_map.250 = (bf16[1184,256]{1,0:T(8,128)(2,1)S(1)}, bf16[2,4,592,592]{3,2,1,0:T(8,128)(2,1)}) custom-call(bf16[1184,768]{1,0:T(8,128)(2,1)S(1)} %fusion.15.qkv_ref), custom_call_target="tpu_custom_call" | custom-call | flops 4306501632 | bytes 8032256 | tf_op jit(solution)/shard_map/pallas_call | solution.py:57
  188.4 7.1 %collective-permute-done.28.refs_3_ = bf16[128,1024]{1,0:T(8,128)(2,1)S(1)} collective-permute-done((bf16[128,1024]{1,0:T(8,128)(2,1)S(1)}, bf16[128,1024]{1,0:T(8,128)(2,1)S(1)}, u32[]{:S(2)}, u32[]{:S(2)}) %collective-permute-start.28) | collective-permute-done | bytes 262176 | tf_op jit(solution)/shard_map/ppermute | solution.py:199
  211.7 14.2 %collective-permute-done.29.refs_1_ = bf16[4,128,1024]{2,1,0:T(8,128)(2,1)} collective-permute-done((bf16[4,128,1024]{2,1,0:T(8,128)(2,1)S(1)}, bf16[4,128,1024]{2,1,0:T(8,128)(2,1)}, u32[]{:S(2)}, u32[]{:S(2)}) %collective-permute-start.29) | collective-permute-done | bytes 1048608 | tf_op jit(solution)/shard_map/ppermute | solution.py:199
  227.8 20.6 %collective-permute-done.24.refs_1_ = bf16[4,128,1024]{2,1,0:T(8,128)(2,1)} collective-permute-done((bf16[4,128,1024]{2,1,0:T(8,128)(2,1)}, bf16[4,128,1024]{2,1,0:T(8,128)(2,1)}, u32[]{:S(2)}, u32[]{:S(2)}) %collective-permute-start.24) | collective-permute-done | bytes 1048608 | tf_op jit(solution)/shard_map/ppermute | solution.py:199
  266.0 7.2 %convert_reduce_fusion.1 = (f32[1024]{0:T(1024)}, bf16[1184,1024]{1,0:T(8,128)(2,1)S(1)}) fusion(f32[1184,1024]{1,0:T(8,128)S(1)} %get-tuple-element.96, bf16[1024,1024]{1,0:T(8,128)(2,1)S(1)} %bitcast.265, bf16[592,1024]{1,0:T(8,128)(2,1)} %collective-permute-done.41, bf16[592,1024]{1,0:T(8,128)(2,1)} %pad.8), kind=kOutput, calls=%fused_computation.21 | convolution fusion | flops 2504850432 | bytes 11800576 | tf_op jit(solution)/shard_map/dot_general | solution.py:29
  286.1 6.7 %convert_reduce_fusion.2 = (f32[1024]{0:T(1024)S(1)}, bf16[1184,1024]{1,0:T(8,128)(2,1)S(1)}) fusion(f32[1184,1024]{1,0:T(8,128)S(1)} %get-tuple-element.98, bf16[1024,1024]{1,0:T(8,128)(2,1)S(1)} %bitcast.242, bf16[592,1024]{1,0:T(8,128)(2,1)} %collective-permute-done.41, bf16[592,1024]{1,0:T(8,128)(2,1)} %pad.8), kind=kOutput, calls=%fused_computation.22 | convolution fusion | flops 2504850432 | bytes 11800576 | tf_op jit(solution)/shard_map/dot_general | solution.py:29
  310.3 6.2 %fusion.93 = f32[1184,1024]{1,0:T(8,128)} fusion(bf16[1184,1024]{1,0:T(8,128)(2,1)} %copy-done.57, bf16[1024,1024]{1,0:T(8,128)(2,1)S(1)} %bitcast.266), kind=kOutput, calls=%fused_computation.305 | convolution fusion | flops 2483027968 | bytes 9371648 | tf_op jit(solution)/shard_map/dot_general | solution.py:29
  316.5 8.2 %collective-permute-done.74 = bf16[4,128,1024]{2,1,0:T(8,128)(2,1)S(1)} collective-permute-done((bf16[4,128,1024]{2,1,0:T(8,128)(2,1)S(1)}, bf16[4,128,1024]{2,1,0:T(8,128)(2,1)S(1)}, u32[]{:S(2)}, u32[]{:S(2)}) %collective-permute-start.74) | collective-permute-done | bytes 1048608 | tf_op jit(solution)/shard_map/ppermute | solution.py:199
  325.2 21.9 %collective-permute-done.62 = bf16[4,128,1024]{2,1,0:T(8,128)(2,1)S(1)} collective-permute-done((bf16[4,128,1024]{2,1,0:T(8,128)(2,1)S(1)}, bf16[4,128,1024]{2,1,0:T(8,128)(2,1)S(1)}, u32[]{:S(2)}, u32[]{:S(2)}) %collective-permute-start.62) | collective-permute-done | bytes 1048608 | tf_op jit(solution)/shard_map/ppermute | solution.py:199
  360.3 7.3 %fusion.92 = (bf16[1184,1024]{1,0:T(8,128)(2,1)}, f32[1184,1024]{1,0:T(8,128)S(1)}) fusion(f32[1184,1024]{1,0:T(8,128)} %fusion.94, bf16[1184,1024]{1,0:T(8,128)(2,1)} %copy-done.54, bf16[1024,1024]{1,0:T(8,128)(2,1)S(1)} %bitcast.241), kind=kOutput, calls=%fused_computation.304 | convolution fusion | flops 2485452800 | bytes 16646144 | tf_op jit(solution)/shard_map/dot_general | solution.py:29
  413.4 10.0 %shard_map.260 = bf16[1184,768]{1,0:T(8,128)(2,1)S(1)} custom-call(bf16[1184,768]{1,0:T(8,128)(2,1)S(1)} %copy-done.15, bf16[2,4,592,592]{3,2,1,0:T(8,128)(2,1)} %get-tuple-element.21.probs_ref, bf16[1184,256]{1,0:T(8,128)(2,1)S(1)} %convolution_convert_fusion.grad_ref), custom_call_target="tpu_custom_call" | custom-call | flops 7177502720 | bytes 9850880 | tf_op jit(solution)/shard_map/pallas_call | solution.py:113
  435.3 10.0 %shard_map.259 = bf16[1184,768]{1,0:T(8,128)(2,1)S(1)} custom-call(bf16[1184,768]{1,0:T(8,128)(2,1)S(1)} %copy-done.13, bf16[2,4,592,592]{3,2,1,0:T(8,128)(2,1)} %get-tuple-element.20.probs_ref, bf16[1184,256]{1,0:T(8,128)(2,1)S(1)} %convolution_convert_fusion.1.grad_ref), custom_call_target="tpu_custom_call" | custom-call | flops 7177502720 | bytes 9850880 | tf_op jit(solution)/shard_map/pallas_call | solution.py:113
  461.9 6.3 %constant_dynamic-slice_fusion.20 = (bf16[4,1,128,1024]{2,1,0,3:T(2,128)(2,1)}, bf16[4,1,128,1024]{2,1,0,3:T(2,128)(2,1)}) fusion(bf16[4,2,128,1024]{2,1,0,3:T(2,128)(2,1)S(1)} %copy-done.18, s32[]{:T(128)S(6)} %select_n.370, s32[]{:T(128)S(6)} %select_n.368), kind=kLoop, calls=%fused_computation.234 | loop fusion | bytes 4194312 | tf_op jit(solution)/shard_map/jit(dynamic_index_in_dim)/dynamic_slice | solution.py:297
  468.2 6.0 copy.97
  474.2 5.9 copy.87
  497.1 7.7 %collective-permute-done.50 = bf16[4,128,1024]{2,1,0:T(8,128)(2,1)S(1)} collective-permute-done((bf16[4,128,1024]{2,1,0:T(8,128)(2,1)}, bf16[4,128,1024]{2,1,0:T(8,128)(2,1)S(1)}, u32[]{:S(2)}, u32[]{:S(2)}) %collective-permute-start.50) | collective-permute-done | bytes 1048608 | tf_op jit(solution)/shard_map/ppermute | solution.py:199
  516.0 10.9 %collective-permute-done.45 = f32[1,9216]{1,0:T(1,128)S(1)} collective-permute-done((f32[1,9216]{1,0:T(1,128)S(1)}, f32[1,9216]{1,0:T(1,128)S(1)}, u32[]{:S(2)}, u32[]{:S(2)}) %collective-permute-start.45) | collective-permute-done | bytes 36896 | tf_op jit(solution)/shard_map/ppermute | solution.py:199
  533.8 7.3 %collective-permute-start.49 = (f32[1,9216]{1,0:T(1,128)S(1)}, f32[1,9216]{1,0:T(1,128)S(1)}, u32[]{:S(2)}, u32[]{:S(2)}) collective-permute-start(f32[1,9216]{1,0:T(1,128)S(1)} %add.528), channel_id=1, source_target_pairs={{0,2},{1,3},{2,0},{3,1},{4,6},{5,7},{6,4},{7,5},{8,10},{9,11},{10,... | collective-permute-start | bytes 110600 | tf_op jit(solution)/shard_map/ppermute | solution.py:199
  582.1 9.7 %collective-permute-start.55 = (bf16[64,1024]{1,0:T(8,128)(2,1)S(1)}, bf16[64,1024]{1,0:T(8,128)(2,1)S(1)}, u32[]{:S(2)}, u32[]{:S(2)}) collective-permute-start(bf16[64,1024]{1,0:T(8,128)(2,1)S(1)} %broadcast_select_fusion.11), channel_id=1, source_target_pairs={{0,2},{1,3},{2,0},{3,1},{4,6},{5,7},{6,4},{7,5},{8,10},{9,11},{10,... | collective-permute-start | bytes 393224 | tf_op jit(solution)/shard_map/ppermute | solution.py:199
  594.1 17.1 %collective-permute-start.61 = (bf16[64,1024]{1,0:T(8,128)(2,1)S(1)}, bf16[64,1024]{1,0:T(8,128)(2,1)S(1)}, u32[]{:S(2)}, u32[]{:S(2)}) collective-permute-start(bf16[64,1024]{1,0:T(8,128)(2,1)S(1)} %broadcast_select_fusion.10), channel_id=1, source_target_pairs={{0,2},{1,3},{2,0},{3,1},{4,6},{5,7},{6,4},{7,5},{8,10},{9,11},{10,... | collective-permute-start | bytes 393224 | tf_op jit(solution)/shard_map/ppermute | solution.py:199
  (517 shorter events, 339.5 us)
Async XLA Ops:
  15.3 27.0 %collective-permute-start.19 = (bf16[64,4096]{1,0:T(8,128)(2,1)}, bf16[64,4096]{1,0:T(8,128)(2,1)}, u32[]{:S(2)}, u32[]{:S(2)}) collective-permute-start(bf16[64,4096]{1,0:T(8,128)(2,1)} %get-tuple-element.66), channel_id=1, source_target_pairs={{0,2},{1,3},{2,0},{3,1},{4,6},{5,7},{6,4},{7,5},{8,10},{9,11},{10,... | collective-permute-start | bytes 1572872 | tf_op jit(solution)/shard_map/ppermute | solution.py:199
  16.5 58.7 %collective-permute-start = (bf16[592,1024]{1,0:T(8,128)(2,1)}, bf16[592,1024]{1,0:T(8,128)(2,1)}, u32[]{:S(2)}, u32[]{:S(2)}) collective-permute-start(bf16[592,1024]{1,0:T(8,128)(2,1)} %pad.7), channel_id=1, source_target_pairs={{0,2},{1,3},{2,0},{3,1},{4,6},{5,7},{6,4},{7,5},{8,10},{9,11},{10,... | collective-permute-start | bytes 3637256 | tf_op jit(solution)/shard_map/ppermute | solution.py:199
  69.8 40.0 %collective-permute-start.26 = (bf16[128,1024]{1,0:T(8,128)(2,1)S(1)}, bf16[128,1024]{1,0:T(8,128)(2,1)S(1)}, u32[]{:S(2)}, u32[]{:S(2)}) collective-permute-start(bf16[128,1024]{1,0:T(8,128)(2,1)S(1)} %get-tuple-element.61.refs_0_), channel_id=1, source_target_pairs={{0,24},{1,25},{2,26},{3,27},{4,28},{5,29},{6,30},{7,31},{8,0},{9,1... | collective-permute-start | bytes 786440 | tf_op jit(solution)/shard_map/ppermute | solution.py:199
  85.3 79.6 %collective-permute-start.17 = (bf16[4,2,128,1024]{3,2,1,0:T(8,128)(2,1)S(1)}, bf16[4,2,128,1024]{3,2,1,0:T(8,128)(2,1)}, u32[]{:S(2)}, u32[]{:S(2)}) collective-permute-start(bf16[4,2,128,1024]{3,2,1,0:T(8,128)(2,1)S(1)} %shard_map.249), channel_id=1, source_target_pairs={{0,1},{3,2},{4,5},{7,6},{8,9},{11,10},{12,13},{15,14},{16,17},{19,... | collective-permute-start | bytes 6291464 | tf_op jit(solution)/shard_map/ppermute | solution.py:199
  95.1 65.8 %collective-permute-start.21 = (bf16[128,1024]{1,0:T(8,128)(2,1)S(1)}, bf16[128,1024]{1,0:T(8,128)(2,1)S(1)}, u32[]{:S(2)}, u32[]{:S(2)}) collective-permute-start(bf16[128,1024]{1,0:T(8,128)(2,1)S(1)} %broadcast_select_fusion.4.refs_0_), channel_id=1, source_target_pairs={{0,24},{1,25},{2,26},{3,27},{4,28},{5,29},{6,30},{7,31},{8,0},{9,1... | collective-permute-start | bytes 786440 | tf_op jit(solution)/shard_map/ppermute | solution.py:199
  97.8 63.8 %collective-permute-start.33 = (bf16[2,128,1024]{2,1,0:T(8,128)(2,1)S(1)}, bf16[2,128,1024]{2,1,0:T(8,128)(2,1)S(1)}, u32[]{:S(2)}, u32[]{:S(2)}) collective-permute-start(bf16[2,128,1024]{2,1,0:T(8,128)(2,1)S(1)} %collective-permute-done.32.refs_2_), channel_id=1, source_target_pairs={{0,24},{3,27},{4,28},{7,31},{8,0},{11,3},{12,4},{15,7},{16,8},{19,... | collective-permute-start | bytes 1572872 | tf_op jit(solution)/shard_map/ppermute | solution.py:199
  98.5 62.3 %collective-permute-start.38 = (bf16[2,128,1024]{2,1,0:T(8,128)(2,1)S(1)}, bf16[2,128,1024]{2,1,0:T(8,128)(2,1)S(1)}, u32[]{:S(2)}, u32[]{:S(2)}) collective-permute-start(bf16[2,128,1024]{2,1,0:T(8,128)(2,1)S(1)} %collective-permute-done.37.refs_2_), channel_id=1, source_target_pairs={{0,24},{3,27},{4,28},{7,31},{8,0},{11,3},{12,4},{15,7},{16,8},{19,... | collective-permute-start | bytes 1572872 | tf_op jit(solution)/shard_map/ppermute | solution.py:199
  109.8 95.0 %collective-permute-start.41 = (bf16[592,1024]{1,0:T(8,128)(2,1)}, bf16[592,1024]{1,0:T(8,128)(2,1)}, u32[]{:S(2)}, u32[]{:S(2)}) collective-permute-start(bf16[592,1024]{1,0:T(8,128)(2,1)} %pad.8), channel_id=1, source_target_pairs={{0,2},{1,3},{2,0},{3,1},{4,6},{5,7},{6,4},{7,5},{8,10},{9,11},{10,... | collective-permute-start | bytes 3637256 | tf_op jit(solution)/shard_map/ppermute | solution.py:199
  160.9 26.4 %collective-permute-start.22 = (bf16[128,1024]{1,0:T(8,128)(2,1)S(1)}, bf16[128,1024]{1,0:T(8,128)(2,1)S(1)}, u32[]{:S(2)}, u32[]{:S(2)}) collective-permute-start(bf16[128,1024]{1,0:T(8,128)(2,1)S(1)} %collective-permute-done.21.refs_1_), channel_id=1, source_target_pairs={{0,24},{1,25},{2,26},{3,27},{4,28},{5,29},{6,30},{7,31},{8,0},{9,1... | collective-permute-start | bytes 786440 | tf_op jit(solution)/shard_map/ppermute | solution.py:199
  161.7 88.8 %collective-permute-start.39 = (bf16[4,2,128,1024]{3,2,1,0:T(8,128)(2,1)S(1)}, bf16[4,2,128,1024]{3,2,1,0:T(8,128)(2,1)}, u32[]{:S(2)}, u32[]{:S(2)}) collective-permute-start(bf16[4,2,128,1024]{3,2,1,0:T(8,128)(2,1)S(1)} %shard_map.258), channel_id=1, source_target_pairs={{0,1},{3,2},{4,5},{7,6},{8,9},{11,10},{12,13},{15,14},{16,17},{19,... | collective-permute-start | bytes 6291464 | tf_op jit(solution)/shard_map/ppermute | solution.py:199
  164.9 87.4 %collective-permute-start.34 = (bf16[4,2,128,1024]{3,2,1,0:T(8,128)(2,1)}, bf16[4,2,128,1024]{3,2,1,0:T(8,128)(2,1)}, u32[]{:S(2)}, u32[]{:S(2)}) collective-permute-start(bf16[4,2,128,1024]{3,2,1,0:T(8,128)(2,1)} %shard_map.256), channel_id=1, source_target_pairs={{0,1},{3,2},{4,5},{7,6},{8,9},{11,10},{12,13},{15,14},{16,17},{19,... | collective-permute-start | bytes 6291464 | tf_op jit(solution)/shard_map/ppermute | solution.py:199
  182.5 71.8 %collective-permute-start.18 = (bf16[1184,1024]{1,0:T(8,128)(2,1)}, bf16[1184,1024]{1,0:T(8,128)(2,1)}, u32[]{:S(2)}, u32[]{:S(2)}) collective-permute-start(bf16[1184,1024]{1,0:T(8,128)(2,1)} %get-tuple-element.93), channel_id=1, source_target_pairs={{0,2},{1,3},{2,0},{3,1},{4,6},{5,7},{6,4},{7,5},{8,10},{9,11},{10,... | collective-permute-start | bytes 7274504 | tf_op jit(solution)/shard_map/ppermute | solution.py:199
  204.8 43.6 %collective-permute-start.24 = (bf16[4,128,1024]{2,1,0:T(8,128)(2,1)}, bf16[4,128,1024]{2,1,0:T(8,128)(2,1)}, u32[]{:S(2)}, u32[]{:S(2)}) collective-permute-start(bf16[4,128,1024]{2,1,0:T(8,128)(2,1)} %shard_map.251.refs_0_), channel_id=1, source_target_pairs={{0,4},{1,5},{2,6},{3,7},{4,0},{5,1},{6,2},{7,3},{8,12},{9,13},{10,... | collective-permute-start | bytes 3145736 | tf_op jit(solution)/shard_map/ppermute | solution.py:199
  301.5 45.7 %collective-permute-start.62 = (bf16[4,128,1024]{2,1,0:T(8,128)(2,1)S(1)}, bf16[4,128,1024]{2,1,0:T(8,128)(2,1)S(1)}, u32[]{:S(2)}, u32[]{:S(2)}) collective-permute-start(bf16[4,128,1024]{2,1,0:T(8,128)(2,1)S(1)} %dynamic-slice_bitcast_fusion.1), channel_id=1, source_target_pairs={{0,4},{1,5},{2,6},{3,7},{4,0},{5,1},{6,2},{7,3},{8,12},{9,13},{10,... | collective-permute-start | bytes 3145736 | tf_op jit(solution)/shard_map/ppermute | solution.py:199
  307.4 80.2 %collective-permute-start.80 = (bf16[1024,1024]{1,0:T(8,128)(2,1)S(1)}, bf16[1024,1024]{1,0:T(8,128)(2,1)S(1)}, u32[]{:S(2)}, u32[]{:S(2)}) collective-permute-start(bf16[1024,1024]{1,0:T(8,128)(2,1)S(1)} %convolution_convert_fusion.2), channel_id=1, source_target_pairs={{1,0},{2,3},{5,4},{6,7},{9,8},{10,11},{13,12},{14,15},{17,16},{18,... | collective-permute-start | bytes 6291464 | tf_op jit(solution)/shard_map/ppermute | solution.py:199
  308.8 82.2 %collective-permute-start.68 = (bf16[1024,1024]{1,0:T(8,128)(2,1)S(1)}, bf16[1024,1024]{1,0:T(8,128)(2,1)S(1)}, u32[]{:S(2)}, u32[]{:S(2)}) collective-permute-start(bf16[1024,1024]{1,0:T(8,128)(2,1)S(1)} %convolution_convert_fusion.4), channel_id=1, source_target_pairs={{1,0},{2,3},{5,4},{6,7},{9,8},{10,11},{13,12},{14,15},{17,16},{18,... | collective-permute-start | bytes 6291464 | tf_op jit(solution)/shard_map/ppermute | solution.py:199
  325.2 30.1 %collective-permute-start.75 = (bf16[128,1024]{1,0:T(8,128)(2,1)S(1)}, bf16[128,1024]{1,0:T(8,128)(2,1)S(1)}, u32[]{:S(2)}, u32[]{:S(2)}) collective-permute-start(bf16[128,1024]{1,0:T(8,128)(2,1)S(1)} %dynamic-slice_bitcast_fusion.5), channel_id=1, source_target_pairs={{0,8},{1,9},{2,10},{3,11},{4,12},{5,13},{6,14},{7,15},{8,16},{9,17... | collective-permute-start | bytes 786440 | tf_op jit(solution)/shard_map/ppermute | solution.py:199
  369.4 30.1 %collective-permute-start.42 = (bf16[1184,1024]{1,0:T(8,128)(2,1)S(1)}, bf16[1184,1024]{1,0:T(8,128)(2,1)S(1)}, u32[]{:S(2)}, u32[]{:S(2)}) collective-permute-start(bf16[1184,1024]{1,0:T(8,128)(2,1)S(1)} %copy-done.53), channel_id=1, source_target_pairs={{0,2},{1,3},{2,0},{3,1},{4,6},{5,7},{6,4},{7,5},{8,10},{9,11},{10,... | collective-permute-start | bytes 7274504 | tf_op jit(solution)/shard_map/ppermute | solution.py:199
  389.6 98.4 %collective-permute-start.81 = (bf16[2,128,1024]{2,1,0:T(8,128)(2,1)}, bf16[2,128,1024]{2,1,0:T(8,128)(2,1)}, u32[]{:S(2)}, u32[]{:S(2)}) collective-permute-start(bf16[2,128,1024]{2,1,0:T(8,128)(2,1)} %dynamic-slice_bitcast_fusion.2), channel_id=1, source_target_pairs={{0,8},{3,11},{4,12},{7,15},{8,16},{11,19},{12,20},{15,23},{16,24},... | collective-permute-start | bytes 1572872 | tf_op jit(solution)/shard_map/ppermute | solution.py:199
  393.1 97.0 %collective-permute-start.69 = (bf16[2,128,1024]{2,1,0:T(8,128)(2,1)}, bf16[2,128,1024]{2,1,0:T(8,128)(2,1)}, u32[]{:S(2)}, u32[]{:S(2)}) collective-permute-start(bf16[2,128,1024]{2,1,0:T(8,128)(2,1)} %dynamic-slice_bitcast_fusion.3), channel_id=1, source_target_pairs={{0,8},{3,11},{4,12},{7,15},{8,16},{11,19},{12,20},{15,23},{16,24},... | collective-permute-start | bytes 1572872 | tf_op jit(solution)/shard_map/ppermute | solution.py:199
  460.1 45.2 %collective-permute-start.43 = (bf16[592,1024]{1,0:T(8,128)(2,1)}, bf16[592,1024]{1,0:T(8,128)(2,1)}, u32[]{:S(2)}, u32[]{:S(2)}) collective-permute-start(bf16[592,1024]{1,0:T(8,128)(2,1)} %slice.536), channel_id=1, source_target_pairs={{0,2},{1,3},{2,0},{3,1},{4,6},{5,7},{6,4},{7,5},{8,10},{9,11},{10,... | collective-permute-start | bytes 3637256 | tf_op jit(solution)/shard_map/ppermute | solution.py:199
  483.6 62.0 %collective-permute-start.56 = (bf16[1024,1024]{0,1:T(8,128)(2,1)}, bf16[1024,1024]{0,1:T(8,128)(2,1)}, u32[]{:S(2)}, u32[]{:S(2)}) collective-permute-start(bf16[1024,1024]{0,1:T(8,128)(2,1)} %pad_maximum_fusion.3), channel_id=1, source_target_pairs={{1,0},{2,3},{5,4},{6,7},{9,8},{10,11},{13,12},{14,15},{17,16},{18,... | collective-permute-start | bytes 6291464 | tf_op jit(solution)/shard_map/ppermute | solution.py:199
  496.3 31.4 %collective-permute-start.71 = (bf16[2,128,1024]{2,1,0:T(8,128)(2,1)S(1)}, bf16[2,128,1024]{2,1,0:T(8,128)(2,1)S(1)}, u32[]{:S(2)}, u32[]{:S(2)}) collective-permute-start(bf16[2,128,1024]{2,1,0:T(8,128)(2,1)S(1)} %fusion.33), channel_id=1, source_target_pairs={{0,8},{3,11},{4,12},{7,15},{8,16},{11,19},{12,20},{15,23},{16,24},... | collective-permute-start | bytes 1572872 | tf_op jit(solution)/shard_map/ppermute | solution.py:199
  531.4 27.6 %collective-permute-start.72 = (bf16[128,1024]{1,0:T(8,128)(2,1)}, bf16[128,1024]{1,0:T(8,128)(2,1)}, u32[]{:S(2)}, u32[]{:S(2)}) collective-permute-start(bf16[128,1024]{1,0:T(8,128)(2,1)} %dynamic-slice_bitcast_fusion.6), channel_id=1, source_target_pairs={{0,4},{3,7},{4,0},{7,3},{8,12},{11,15},{12,8},{15,11},{16,20},{19,... | collective-permute-start | bytes 786440 | tf_op jit(solution)/shard_map/ppermute | solution.py:199
  (125 other events, 1648.5 us)

commit v2 on v1

--- a/solution.py
+++ b/solution.py
@@ -8,6 +8,7 @@
 from jax import lax
 from jax.experimental import pallas as pl
 from jax.experimental.pallas import tpu as pltpu
+from jax.experimental.layout import Layout, with_layout_constraint
 from jax.sharding import Mesh
 from jax.sharding import PartitionSpec as P
 
@@ -23,6 +24,12 @@
 NT = (((1,), (1,)), ((), ()))
 TN = (((0,), (0,)), ((), ()))
 VMEM_LIMIT = 48 * 2**20
+LITTLE = pl.CostEstimate(flops=2**20, bytes_accessed=2**18, transcendentals=0)
+LONG = pl.CostEstimate(flops=2**36, bytes_accessed=2**18, transcendentals=0)
+
+
+def rows_first(array):
+    return with_layout_constraint(array, Layout(major_to_minor=(0, 1)))
 
 
 def dot(left, right, dims=NN):
@@ -67,11 +74,7 @@
             jax.ShapeDtypeStruct((2, heads, ROWS, ROWS), BF16),
         ],
         compiler_params=pltpu.CompilerParams(vmem_limit_bytes=VMEM_LIMIT),
-        cost_estimate=pl.CostEstimate(
-            flops=12 * heads * ROWS * ROWS * 256,
-            bytes_accessed=2 * 2 * heads * ROWS * (ROWS + 256),
-            transcendentals=2 * heads * ROWS * ROWS,
-        ),
+        cost_estimate=LONG,
     )(projected)
 
 
@@ -121,11 +124,7 @@
         out_specs=pl.BlockSpec((ROWS, 3 * width), lambda i: (i, 0)),
         out_shape=jax.ShapeDtypeStruct((2 * ROWS, 3 * width), BF16),
         compiler_params=pltpu.CompilerParams(vmem_limit_bytes=VMEM_LIMIT),
-        cost_estimate=pl.CostEstimate(
-            flops=20 * heads * ROWS * ROWS * 256,
-            bytes_accessed=2 * 2 * heads * ROWS * (ROWS + 448),
-            transcendentals=0,
-        ),
+        cost_estimate=LONG,
     )(projected, probs, mixed_grad)
 
 
@@ -142,7 +141,6 @@
         for copy in copies:
             copy.wait()
 
-    size = math.prod(shape) * 2
     return pl.pallas_call(
         kernel,
         grid_spec=pltpu.PrefetchScalarGridSpec(
@@ -154,8 +152,25 @@
         ),
         out_shape=jax.ShapeDtypeStruct(shape, parts[0].dtype),
         compiler_params=pltpu.CompilerParams(vmem_limit_bytes=2**20),
-        cost_estimate=pl.CostEstimate(flops=0, bytes_accessed=2 * size, transcendentals=0),
+        cost_estimate=LITTLE,
     )(spots, *parts)
+
+
+def pack(qkv, proj, quarter):
+    def kernel(qkv_ref, proj_ref, out_ref):
+        for colour in range(2):
+            cut = slice(colour * quarter, (colour + 1) * quarter)
+            for n in range(4):
+                at = (4 * colour + n) * quarter
+                part = qkv_ref[n, :, cut] if n < 3 else proj_ref[:, cut]
+                out_ref[:, at : at + quarter] = part
+
+    return pl.pallas_call(
+        kernel,
+        out_shape=jax.ShapeDtypeStruct((proj.shape[0], 8 * quarter), proj.dtype),
+        compiler_params=pltpu.CompilerParams(vmem_limit_bytes=VMEM_LIMIT),
+        cost_estimate=LITTLE,
+    )(qkv, proj)
 
 
 def row_stats(values):
@@ -198,11 +213,10 @@
     def send(value, perm):
         return lax.ppermute(value, ALL, perm)
 
-    def is_owner(spot):
-        return spot["c"] == spot["y"]
-
-    def not_owner(spot):
-        return spot["c"] != spot["y"]
+    def exchange(spot):
+        spot["c"], spot["y"] = spot["y"], spot["c"]
+
+    transpose = pairs(exchange)
 
     def on_device(
         tokens,
@@ -222,108 +236,106 @@
     ):
         z, x, c, y = [lax.axis_index(a) for a in ALL]
         owner = c == y
+        where_am_i = dict(z=z, x=x, c=c, y=y)
         width = tokens.shape[1]
         depth = fc1_weight.shape[0]
-        pair = 2 * depth
         heads = qv_bias.shape[1] // 2
 
         def swap(value):
             return send(value, shift("c", 1))
 
-        def chunks(arrays):
-            own = jnp.concatenate(arrays, axis=1)
-            other = swap(own)
-            both = jnp.where(c == 0, jnp.stack([own, other]), jnp.stack([other, own]))
-            both = both.reshape(pair, own.shape[1])
-            return both
+        def after(value, *earlier):
+            return lax.optimization_barrier((value,) + earlier)[0]
 
         quarter = proj_weight.shape[0] // 2
+        hidden_half = fc1_weight.shape[1] // 2
+        n_qkv = 3 * quarter
         proj_t = proj_weight.T
         fc2_t = fc2_weight.T
-        parts = []
-        for colour in range(2):
-            cut = slice(colour * quarter, (colour + 1) * quarter)
-            parts += [qkv_weight[:, n, cut] for n in range(3)] + [proj_t[:, cut]]
-        first = chunks(parts)
-        span = 4 * quarter
-        rest = chunks([fc1_weight, fc2_t])
-        hidden_half = fc1_weight.shape[1] // 2
-        groups = [
-            (first[:, :span], first[:, span:]),
-            (rest[:, :hidden_half], rest[:, hidden_half : 2 * hidden_half]),
-            (rest[:, 2 * hidden_half : 3 * hidden_half], rest[:, 3 * hidden_half :]),
-        ]
-
-        z_spots = (z + jnp.arange(n_z, dtype=jnp.int32)) % n_z
-        x_spots = (x + jnp.arange(n_x, dtype=jnp.int32)) % n_x
-
-        def gather_a(chunk):
-            wide = chunk.shape[1]
-            moved = send(chunk, shift("y", 1, is_owner))
-            chunk = jnp.where(owner, chunk, moved)
-            bufs = [chunk]
-            for _ in range(n_z - 1):
-                bufs.append(send(bufs[-1], shift("z", -1)))
-            column = place(bufs, z_spots, (n_z, pair, wide), lambda ref, n: ref.at[n])
-            bufs = [column]
-            for _ in range(n_x - 1):
-                bufs.append(send(bufs[-1], shift("x", -1)))
-            whole = place(bufs, x_spots, (n_z, n_x, pair, wide), lambda ref, n: ref.at[:, n])
-            return whole.reshape(width, wide)
-
-        def gather_b(chunk):
-            wide = chunk.shape[1]
-            bufs = [chunk]
-            for _ in range(n_x - 1):
-                bufs.append(send(bufs[-1], shift("x", -1, is_owner)))
-            line = place(bufs, x_spots, (n_x, pair, wide), lambda ref, n: ref.at[n])
-            bufs = [line]
-            for _ in range(n_z - 1):
-                bufs.append(send(bufs[-1], shift("z", -1, is_owner)))
-            plane = place(bufs, z_spots, (n_z, n_x, pair, wide), lambda ref, n: ref.at[n])
-            moved = send(plane, shift("y", 1, is_owner))
-            return jnp.where(owner, plane, moved).reshape(width, wide)
-
-        def add(left, right):
-            return (left.astype(F32) + right.astype(F32)).astype(BF16)
-
-        def finish(total):
-            first, second = total[:depth], total[depth:]
-            moved = swap(jnp.where(c == 0, second, first))
-            kept = jnp.where(c == 0, first, second)
-            return jnp.where(owner, kept, moved).astype(F32)
+        shards = [pack(qkv_weight.transpose(1, 0, 2), proj_t, quarter), fc1_weight, fc2_t]
+
+        def spots(axis):
+            count = sizes[axis]
+            return (where_am_i[axis] + jnp.arange(count, dtype=jnp.int32)) % count
+
+        def from_all(value, axis, shape, block, earlier=()):
+            moved = [send(value, shift(axis, -k)) for k in range(1, sizes[axis])]
+            if earlier:
+                moved = [after(part, *earlier) for part in moved]
+            return place([value] + moved, spots(axis), shape, block)
+
+        def crossed(shard):
+            return send(shard, transpose)
+
+        def halves(line):
+            wide = line.shape[2] // 2
+            return line[:, :, :wide], line[:, :, wide:]
+
+        def step_one(first, second, *earlier):
+            at = (n_z, n_x, depth, first.shape[2])
+            first = from_all(first, "x", at, lambda ref, n: ref.at[:, n], earlier)
+            at = (n_z, 2, depth, second.shape[2])
+            return first, from_all(second, "y", at, lambda ref, n: ref.at[:, n], earlier)
+
+        def step_two(first, second, *earlier):
+            wide = first.shape[3]
+            at = (n_z, n_x, 2, depth, wide)
+            first = from_all(first, "y", at, lambda ref, n: ref.at[:, :, n], earlier)
+            second = from_all(second, "x", at, lambda ref, n: ref.at[:, n], earlier)
+            return first.reshape(width, wide), second.reshape(width, wide)
 
         def pick(array, axis, index):
             return lax.dynamic_index_in_dim(array, index, axis, keepdims=False)
 
-        def scatter_a(grad):
-            grad = grad.reshape(n_z, n_x, pair, grad.shape[1])
-            total = pick(grad, 1, (x + n_x - 1) % n_x)
-            for k in range(n_x - 2, -1, -1):
-                total = add(send(total, shift("x", 1)), pick(grad, 1, (x + k) % n_x))
-            lines = total
-            total = pick(lines, 0, (z + n_z - 1) % n_z)
-            for k in range(n_z - 2, -1, -1):
-                total = add(send(total, shift("z", 1)), pick(lines, 0, (z + k) % n_z))
-            return finish(add(send(total, shift("y", 1, not_owner)), total))
-
-        def scatter_b(grad):
-            grad = add(send(grad, shift("y", 1, not_owner)), grad)
-            grad = grad.reshape(n_z, n_x, pair, grad.shape[1])
-            total = pick(grad, 0, (z + n_z - 1) % n_z)
-            for k in range(n_z - 2, -1, -1):
-                total = add(send(total, shift("z", 1, is_owner)), pick(grad, 0, (z + k) % n_z))
-            lines = total
-            total = pick(lines, 0, (x + n_x - 1) % n_x)
-            for k in range(n_x - 2, -1, -1):
-                total = add(send(total, shift("x", 1, is_owner)), pick(lines, 0, (x + k) % n_x))
-            return finish(total)
+        def give(array, axis, dim):
+            count, here = sizes[axis], where_am_i[axis]
+            moved = [
+                send(pick(array, dim, (here + k) % count), shift(axis, k))
+                for k in range(1, count)
+            ]
+            return moved, pick(array, dim, here)
+
+        def summed(given, *earlier):
+            moved, own_part = given
+            total = own_part.astype(F32)
+            for part in moved:
+                total = total + (after(part, *earlier) if earlier else part).astype(F32)
+            return total.astype(BF16)
+
+        def scatter_one(first, second):
+            at = (n_z, n_x, 2, depth, first.shape[1])
+            return give(first.reshape(at), "y", 2), give(second.reshape(at), "x", 1)
+
+        def scatter_two(first, second):
+            return give(first, "x", 1), give(second, "y", 1)
+
+        def scatter_three(first, second):
+            both = jnp.concatenate([first, second], axis=2)
+            own = lax.psum_scatter(both, "z", scatter_dimension=0, tiled=False)
+            return send(own, transpose)
+
+        shard_one = crossed(shards[0])
+        shard_two = crossed(after(shards[1], shard_one))
+        shard_three = crossed(after(shards[2], shard_one))
+        shard_one = after(shard_one, shard_two, shard_three)
+        wide = shards[0].shape[1] // 2
+        around = [shard_one] + [send(shard_one, shift("z", -k)) for k in range(1, n_z)]
+        line_one = [
+            place(
+                [part[:, cut] for part in around],
+                spots("z"),
+                (n_z, depth, wide),
+                lambda ref, n: ref.at[n],
+            )
+            for cut in (slice(0, wide), slice(wide, 2 * wide))
+        ]
+        line_two = lax.all_gather(after(shard_two, around[1]), "z", axis=0)
+        line_three = lax.all_gather(after(shard_three, line_two), "z", axis=0)
 
         small = jnp.concatenate(
-            [ln1_gain, ln1_bias, ln2_gain, ln2_bias, proj_bias, fc2_bias]
+            [after(ln1_gain, around[1]), ln1_bias, ln2_gain, ln2_bias, proj_bias, fc2_bias]
             + [qv_bias.reshape(-1), fc1_bias.reshape(-1)]
         )[None]
-        where_am_i = dict(z=z, x=x, c=c, y=y)
         for axis in ("c", "y", "x", "z"):
             count = sizes[axis]
             stacked = jnp.stack([small] + [send(small, shift(axis, -k)) for k in range(1, count)])
@@ -347,86 +359,128 @@
             value = jnp.pad(value, ((0, ROWS - SEQ), (0, 0)))
             return jnp.concatenate([value, swap(value)])
 
-        inputs = both_images(tokens)
-        down = both_images(cotangent)
+        inputs = both_images(after(tokens, around[1]))
 
         def own(value):
             return value[:ROWS]
 
-        def exchanged(partial):
-            moved = swap(partial.astype(BF16)).astype(F32)
+        def exchanged(partial, low, *earlier):
+            moved = swap(low)
+            moved = (after(moved, *earlier) if earlier else moved).astype(F32)
             return partial + jnp.concatenate([moved[ROWS:], moved[:ROWS]])
 
         def exchanged_own(partial):
             return partial[:ROWS] + swap(partial[ROWS:].astype(BF16)).astype(F32)
 
-        attn_a, attn_b = gather_a(groups[0][0]), gather_b(groups[0][1])
-        fc1_a, fc1_b = gather_a(groups[1][0]), gather_b(groups[1][1])
-        fc2_a, fc2_b = gather_a(groups[2][0]), gather_b(groups[2][1])
-        n_qkv = 3 * quarter
-
+        square_one = step_one(*line_one)
         wide_in = inputs.astype(F32)
         mean_one, inv_one = row_stats(wide_in)
         hat_one = (wide_in - mean_one) * inv_one
         normed_one = (hat_one * gain_one + shift_one).astype(BF16)
-
-        mixed, probs, projected = [], [], []
-        for colour, weight in enumerate((attn_a, attn_b)):
+        down = both_images(after(cotangent, normed_one))
+
+        attn_w = step_two(*square_one, normed_one)
+        half_two = [after(v, *square_one) for v in halves(line_two)]
+        projected, probs, mixed = [None] * 2, [None] * 2, [None] * 2
+
+        def attend_half(colour, rows):
             cut = slice(colour * quarter, (colour + 1) * quarter)
             bias = jnp.concatenate(
                 [qv_half[0, cut], jnp.zeros((quarter,), F32), qv_half[1, cut]]
             )
-            here = (dot(normed_one, weight[:, :n_qkv]) + bias).astype(BF16)
-            out, prob = attend(here, heads)
-            projected.append(here)
-            mixed.append(out)
-            probs.append(prob)
-        proj_ab = [attn_a[:, n_qkv:], attn_b[:, n_qkv:]]
+            here = (dot(rows, attn_w[colour][:, :n_qkv]) + bias).astype(BF16)
+            projected[colour] = here
+            mixed[colour], probs[colour] = attend(here, heads)
+
+        attend_half(0, after(normed_one, *half_two))
+        square_two = step_one(*half_two, mixed[0])
+        half_three = [after(v, *square_two) for v in halves(line_three)]
+        attend_half(1, after(normed_one, *half_three))
+        proj_ab = [w[:, n_qkv:] for w in attn_w]
         branch_one = dot(mixed[0], proj_ab[0], NT) + dot(mixed[1], proj_ab[1], NT)
-        residual = wide_in + exchanged(branch_one) + proj_shift
+        branch_low = branch_one.astype(BF16)
+        fc1_w = step_two(*square_two, branch_low)
+        residual = wide_in + exchanged(branch_one, branch_low) + proj_shift
         mean_two, inv_two = row_stats(residual)
         hat_two = (residual - mean_two) * inv_two
         normed_two = (hat_two * gain_two + shift_two).astype(BF16)
+        square_three = step_one(*half_three, normed_two)
 
         hidden, slope = [], []
-        for colour, weight in enumerate((fc1_a, fc1_b)):
+        rows_two = after(normed_two, *square_three)
+        for colour, weight in enumerate(fc1_w):
             bias = fc1_half[colour * hidden_half : (colour + 1) * hidden_half]
-            pre = dot(normed_two, weight) + bias
+            pre = dot(rows_two, weight) + bias
             cdf = 0.5 * (1.0 + lax.erf(pre * (1.0 / math.sqrt(2.0))))
             density = jnp.exp(-0.5 * pre * pre) * (1.0 / math.sqrt(2.0 * math.pi))
             hidden.append((pre * cdf).astype(BF16))
             slope.append((cdf + pre * density).astype(BF16))
 
-        grad_fc2 = [dot(down, h, TN).astype(BF16) for h in hidden]
-        scat_fc2 = [scatter_a(grad_fc2[0]), scatter_b(grad_fc2[1])]
+        grad_fc2 = [rows_first(dot(down, h, TN).astype(BF16)) for h in hidden]
+        fc2_one = scatter_one(*grad_fc2)
+        fc2_w = step_two(*square_three, *grad_fc2)
+        down_late = after(down, *grad_fc2)
         hidden_grad = [
-            (dot(down, w) * s.astype(F32)).astype(BF16) for w, s in zip((fc2_a, fc2_b), slope)
+            (dot(down_late, w) * s.astype(F32)).astype(BF16) for w, s in zip(fc2_w, slope)
         ]
-        back_two = exchanged(dot(hidden_grad[0], fc1_a, NT) + dot(hidden_grad[1], fc1_b, NT))
-        grad_fc1 = [dot(normed_two, g, TN).astype(BF16) for g in hidden_grad]
-        scat_fc1 = [scatter_a(grad_fc1[0]), scatter_b(grad_fc1[1])]
+        back_two = dot(hidden_grad[0], fc1_w[0], NT) + dot(hidden_grad[1], fc1_w[1], NT)
+        back_low = back_two.astype(BF16)
+        fc2_sums = [summed(given, back_low) for given in fc2_one]
+        fc2_two = scatter_two(*fc2_sums)
+        normed_late = after(normed_two, *fc2_sums)
+        grad_fc1 = [rows_first(dot(normed_late, g, TN).astype(BF16)) for g in hidden_grad]
         grad_fc1_shift = jnp.concatenate([jnp.sum(g.astype(F32), axis=0) for g in hidden_grad])
-
-        branch_two = dot(hidden[0], fc2_a, NT) + dot(hidden[1], fc2_b, NT)
-        output = (own(residual) + exchanged_own(branch_two) + out_shift).astype(BF16)[:SEQ]
+        fc1_one = scatter_one(*grad_fc1)
 
         upstream = down.astype(F32)
+        back_two = exchanged(back_two, back_low, *grad_fc1)
         resid_grad = upstream + norm_back(back_two, hat_two, inv_two, gain_two)
         attn_grad = resid_grad.astype(BF16)
 
-        parts, back_one, grad_qv = [], [], []
-        for colour, weight in enumerate((attn_a, attn_b)):
-            mixed_grad = dot(attn_grad, weight[:, n_qkv:]).astype(BF16)
-            qkv_grad = attend_back(projected[colour], probs[colour], mixed_grad, heads)
-            grad_qkv = dot(normed_one, qkv_grad, TN).astype(BF16)
-            grad_proj = dot(attn_grad, mixed[colour], TN).astype(BF16)
-            parts.append(jnp.concatenate([grad_qkv, grad_proj], axis=1))
-            back_one.append(dot(qkv_grad, weight[:, :n_qkv], NT))
-            grad_qv.append(jnp.sum(qkv_grad.astype(F32), axis=0))
-        scat_attn = [scatter_a(parts[0]), scatter_b(parts[1])]
-        back_one = exchanged_own(back_one[0] + back_one[1])
+        mixed_grad = [dot(attn_grad, w).astype(BF16) for w in proj_ab]
+        fc2_lines = [summed(given, *mixed_grad) for given in fc2_two]
+        scat_fc2 = scatter_three(*fc2_lines)
+
+        def attn_grads(colour, qkv_grad, *earlier):
+            rows, top = after(normed_one, *earlier), after(attn_grad, *earlier)
+            grad_qkv = dot(rows, qkv_grad, TN).astype(BF16)
+            grad_proj = dot(top, mixed[colour], TN).astype(BF16)
+            cut = 2 * quarter
+            return (
+                rows_first(grad_qkv[:, :cut]),
+                rows_first(jnp.concatenate([grad_qkv[:, cut:], grad_proj], axis=1)),
+            )
+
+        back_a = attend_back(after(projected[0], *fc2_lines), probs[0], mixed_grad[0], heads)
+        fc1_sums = [summed(given, back_a) for given in fc1_one]
+        fc1_two = scatter_two(*fc1_sums)
+        grads_a = attn_grads(0, back_a, *fc1_sums)
+        a_one = scatter_one(*grads_a)
+        back_b = attend_back(after(projected[1], *grads_a), probs[1], mixed_grad[1], heads)
+        fc1_lines = [summed(given, back_b) for given in fc1_two]
+        scat_fc1 = scatter_three(*fc1_lines)
+        a_sums = [summed(given, *fc1_lines) for given in a_one]
+        a_two = scatter_two(*a_sums)
+        grads_b = attn_grads(1, back_b, *a_sums)
+        b_one = scatter_one(*grads_b)
+        a_lines = [summed(given, *grads_b) for given in a_two]
+        scat_a = scatter_three(*a_lines)
+        qkv_grads = [after(g, *a_lines) for g in (back_a, back_b)]
+        back_one = [dot(g, w[:, :n_qkv], NT) for g, w in zip(qkv_grads, attn_w)]
+        back_one = back_one[0] + back_one[1]
+        b_sums = [summed(given, back_one) for given in b_one]
+        b_two = scatter_two(*b_sums)
+        back_one = exchanged_own(after(back_one, *b_sums))
+        grad_qv = [jnp.sum(g.astype(F32), axis=0) for g in qkv_grads]
         hat_own = own(hat_one)
         grad_tokens = own(resid_grad) + norm_back(back_one, hat_own, own(inv_one), gain_one)
+        b_lines = [summed(given, back_one) for given in b_two]
+        scat_b = scatter_three(*b_lines)
+        scat_attn = jnp.concatenate([scat_a, scat_b], axis=1).astype(F32)
+
+        hidden_late = [after(h, *b_lines) for h in hidden]
+        branch_two = dot(hidden_late[0], fc2_w[0], NT) + dot(hidden_late[1], fc2_w[1], NT)
+        output = (own(residual) + exchanged_own(branch_two) + out_shift).astype(BF16)[:SEQ]
 
         six = [
             jnp.sum(back_one * hat_own, axis=0),
@@ -453,8 +507,9 @@
         grad_fc1_bias = pick(half[4 * quarter :].reshape(fc1_bias.shape[0], -1, per_fc1), 1, deep)
 
         def joined(index):
-            cut = slice(index * quarter, (index + 1) * quarter)
-            return jnp.concatenate([s[:, cut] for s in scat_attn], axis=1)
+            at = index * quarter
+            cuts = [scat_attn[:, at + half : at + half + quarter] for half in (0, 4 * quarter)]
+            return jnp.concatenate(cuts, axis=1)
 
         grad_qkv = jnp.stack([joined(0), joined(1), joined(2)], axis=1)
         return (
@@ -468,9 +523,9 @@
             small_own[4],
             small_own[2],
             small_own[3],
-            jnp.concatenate(scat_fc1, axis=1),
+            scat_fc1.astype(F32),
             grad_fc1_bias,
-            jnp.concatenate(scat_fc2, axis=1).T,
+            scat_fc2.astype(F32).T,
             small_own[5],
         )
 

time: 624 us -> 452 us (0.72)
  starting transfers between devices: 175 us -> 73.1 us
  waiting for transfers between devices: 141 us -> 116 us
  other arithmetic: 80.1 us -> 56.5 us
  local copies, waits for them, and re-layouts: 73.3 us -> 51.9 us
  between operations: 3.38 us -> 16.6 us
  matrix products: 93.7 us -> 82.8 us
    ppermute x86 -> x56, starting transfers between devices: 175 us -> 72.4 us  [send(): return lax.ppermute(value, ALL, perm)]
    ppermute x86 -> x56, waiting for transfers between devices: 141 us -> 77.9 us  [send(): return lax.ppermute(value, ALL, perm)]
    reduce_scatter x0 -> x4, waiting for transfers between devices: none -> 33.5 us  [scatter_three(): own = lax.psum_scatter(both, 'z', scatter_dimension=0, tiled=False)]
    select_n x20 -> x2, other arithmetic: 15.2 us -> 0.02 us  [spots(): return (where_am_i[axis] + jnp.arange(count, dtype=jnp.int32)) % count]
    dynamic_slice x8 -> x20, local copies, waits for them, and re-layouts: 19.6 us -> 6.83 us  [pick(): return lax.dynamic_index_in_dim(array, index, axis, keepdims=False)]
    dot_general x24, matrix products: 93.7 us -> 82.8 us  [dot(): return lax.dot_general(left, right, dims, preferred_element_type=F32)]
    convert_element_type x32 -> x18, other arithmetic: 18.5 us -> 8.78 us  [the longest x16 7.91 us: summed(): return total.astype(BF16)]
    unnamed x154 -> x147, local copies, waits for them, and re-layouts: 22.8 us -> 14.3 us
  transfers between devices with their start and end apart: 86 -> 62, of which waited for: 25 -> 24; matrix products, arithmetic and copies ran while one was open for 30% -> 34% of each run, Pallas kernels for 8% -> 9%
where the time goes in v2:
time: 452 us; the launch traced here: 446 us
  waiting for transfers between devices  116 us (26%)
  matrix products  82.8 us (18%)
  starting transfers between devices  73.1 us (16%)
  other arithmetic  56.5 us (12%)
  local copies, waits for them, and re-layouts  51.9 us (11%)
  Pallas kernels  49.6 us (11%)
  between operations  16.6 us (4%)
    dot_general x24, matrix products, dot(): return lax.dot_general(left, right, dims, preferred_element_type=F32)  82.8 us
    ppermute x56, waiting for transfers between devices, send(): return lax.ppermute(value, ALL, perm)  77.9 us
    ppermute x56, starting transfers between devices, send(): return lax.ppermute(value, ALL, perm)  72.4 us
    reduce_scatter x4, waiting for transfers between devices, scatter_three(): own = lax.psum_scatter(both, 'z', scatter_dimension=0, tiled=False)  33.5 us
    pallas_call x2, Pallas kernels, attend_back(): pl.pallas_call(functools.partial(attend_back_kernel, heads), grid=(2,), i...  19.8 us
    pallas_call x2, Pallas kernels, attend(): pl.pallas_call(functools.partial(attend_kernel, heads), grid=(2,), in_spe...  15.4 us
    pallas_call x14, Pallas kernels, place(): pl.pallas_call(kernel, grid_spec=pltpu.PrefetchScalarGridSpec(num_scalar_...  14.4 us
    unnamed x147, local copies, waits for them, and re-layouts  14.3 us
  transfers between devices with their start and end apart: 62, of which 24 were waited for; matrix products, arithmetic and copies ran while one was open for 34% of the time, Pallas kernels for 9%

profile of v2, /device:TPU:1, one launch (start us, length us, event | category | flops | bytes accessed | tf_op | source)
XLA Modules:
  0.0 446.2 jit_solution(563088796193418690)
XLA Ops:
  9.0 4.5 %collective-permute-start = (bf16[64,2048]{1,0:T(8,128)(2,1)S(1)}, bf16[64,2048]{1,0:T(8,128)(2,1)S(1)}, u32[]{:S(2)}, u32[]{:S(2)}) collective-permute-start(bf16[64,2048]{1,0:T(8,128)(2,1)S(1)} %shard_map.245), channel_id=1, source_target_pairs={{0,0},{1,2},{2,1},{3,3},{4,4},{5,6},{6,5},{7,7},{8,8},{9,10},{10,9... | collective-permute-start | bytes 786440 | tf_op jit(solution)/shard_map/ppermute | solution.py:214
  73.2 5.1 %fusion = (f32[1184,1024]{1,0:T(8,128)}, bf16[1184,1024]{1,0:T(8,128)(2,1)}) fusion(f32[1184]{0:T(1024)S(1)} %add_rsqrt_fusion.1, f32[1184]{0:T(1024)S(1)} %broadcast_multiply_fusion.4, bf16[592,1024]{1,0:T(8,128)(2,1)} %collective-permute-done.4, bf16[592,1024]{1,0:T(8,128)(2,1)} %pad.7, f32[1024]{0:T(1024)S(1)} %add.450, f32[1024]{0:T(1024)S(1)} %mul.153), kind=kLoop, calls=%fused_computation.5 | loop fusion | flops 10911744 | bytes 9716992 | tf_op jit(solution)/shard_map/mul | solution.py:378
  81.8 8.0 %collective-permute-done.15.refs_1_ = bf16[4,2,64,1024]{3,2,1,0:T(8,128)(2,1)} collective-permute-done((bf16[4,2,64,1024]{3,2,1,0:T(8,128)(2,1)S(1)}, bf16[4,2,64,1024]{3,2,1,0:T(8,128)(2,1)}, u32[]{:S(2)}, u32[]{:S(2)}) %collective-permute-start.15) | collective-permute-done | bytes 1048608 | tf_op jit(solution)/shard_map/ppermute | solution.py:214
  95.1 7.6 %shard_map.251 = (bf16[1184,256]{1,0:T(8,128)(2,1)S(1)}, bf16[2,4,592,592]{3,2,1,0:T(8,128)(2,1)}) custom-call(bf16[1184,768]{1,0:T(8,128)(2,1)S(1)} %fusion.14.qkv_ref), custom_call_target="tpu_custom_call" | custom-call | flops 68719476736 | bytes 262144 | tf_op jit(solution)/shard_map/pallas_call | solution.py:64
  115.7 7.7 %shard_map.255 = (bf16[1184,256]{1,0:T(8,128)(2,1)S(1)}, bf16[2,4,592,592]{3,2,1,0:T(8,128)(2,1)}) custom-call(bf16[1184,768]{1,0:T(8,128)(2,1)S(1)} %fusion.15.qkv_ref), custom_call_target="tpu_custom_call" | custom-call | flops 68719476736 | bytes 262144 | tf_op jit(solution)/shard_map/pallas_call | solution.py:64
  125.6 5.0 %fusion.87 = (bf16[1184,1024]{1,0:T(8,128)(2,1)}, f32[1184,1024]{1,0:T(8,128)}) fusion(f32[1184,1024]{1,0:T(8,128)S(1)} %fusion.43, bf16[1184,256]{1,0:T(8,128)(2,1)S(1)} %copy-done.14, bf16[1024,1024]{1,0:T(8,128)(2,1)} %bitcast.233), kind=kOutput, calls=%fused_computation.287 | convolution fusion | flops 623181824 | bytes 13254656 | tf_op jit(solution)/shard_map/dot_general | solution.py:36
  138.9 4.7 %fusion.70 = (f32[1184,1024]{1,0:T(8,128)}, bf16[1184,1024]{1,0:T(8,128)(2,1)S(1)}) fusion(bf16[592,1024]{1,0:T(8,128)(2,1)} %collective-permute-done.23, bf16[592,1024]{1,0:T(8,128)(2,1)} %pad.8), kind=kLoop, calls=%fused_computation.272 | loop fusion | flops 6062080 | bytes 9699328 | tf_op jit(solution)/shard_map/convert_element_type | solution.py:435
  145.1 13.0 %collective-permute-done.22.refs_1_ = bf16[4,2,64,1024]{3,2,1,0:T(8,128)(2,1)} collective-permute-done((bf16[4,2,64,1024]{3,2,1,0:T(8,128)(2,1)S(1)}, bf16[4,2,64,1024]{3,2,1,0:T(8,128)(2,1)}, u32[]{:S(2)}, u32[]{:S(2)}) %collective-permute-start.22) | collective-permute-done | bytes 1048608 | tf_op jit(solution)/shard_map/ppermute | solution.py:214
  173.3 5.1 %multiply_convert_fusion.3 = (bf16[1184,1024]{1,0:T(8,128)(2,1)S(1)}, f32[1184,1024]{1,0:T(8,128)S(1)}) fusion(f32[1024]{0:T(1024)S(1)} %add.477, bf16[1184,1024]{1,0:T(8,128)(2,1)S(1)} %get-tuple-element.103, bf16[1024,1024]{1,0:T(8,128)(2,1)S(1)} %bitcast.246), kind=kOutput, calls=%fused_computation.29 | convolution fusion | flops 2490302464 | bytes 11800576 | tf_op jit(solution)/shard_map/dot_general | solution.py:36
  178.4 5.7 %convolution_convert_fusion.5 = bf16[1024,1024]{1,0:T(8,128)(2,1)S(1)} fusion(bf16[1184,1024]{1,0:T(8,128)(2,1)S(1)} %get-tuple-element.130, bf16[592,1024]{1,0:T(8,128)(2,1)} %collective-permute-done.23, bf16[592,1024]{1,0:T(8,128)(2,1)} %pad.8), kind=kOutput, calls=%fused_computation.81 | convolution fusion | flops 2488926208 | bytes 6946816 | tf_op jit(solution)/shard_map/dot_general | solution.py:36
  185.6 4.8 %multiply_convert_fusion.2 = (bf16[1184,1024]{1,0:T(8,128)(2,1)S(1)}, f32[1184,1024]{1,0:T(8,128)}) fusion(f32[1024]{0:T(1024)S(1)} %add.485, bf16[1184,1024]{1,0:T(8,128)(2,1)S(1)} %get-tuple-element.103, bf16[1024,1024]{1,0:T(8,128)(2,1)S(1)} %bitcast.244), kind=kOutput, calls=%fused_computation.27 | convolution fusion | flops 2490302464 | bytes 11800576 | tf_op jit(solution)/shard_map/dot_general | solution.py:36
  190.4 5.7 %convolution_convert_fusion.4 = bf16[1024,1024]{1,0:T(8,128)(2,1)S(1)} fusion(bf16[1184,1024]{1,0:T(8,128)(2,1)S(1)} %get-tuple-element.131, bf16[592,1024]{1,0:T(8,128)(2,1)} %collective-permute-done.23, bf16[592,1024]{1,0:T(8,128)(2,1)} %pad.8), kind=kOutput, calls=%fused_computation.80 | convolution fusion | flops 2488926208 | bytes 6946816 | tf_op jit(solution)/shard_map/dot_general | solution.py:36
  198.9 5.3 %convert_reduce_fusion.2 = (f32[1024]{0:T(1024)}, bf16[1184,1024]{1,0:T(8,128)(2,1)S(1)}) fusion(f32[1184,1024]{1,0:T(8,128)S(1)} %get-tuple-element.223, bf16[1184,1024]{1,0:T(8,128)(2,1)S(1)} %get-tuple-element.98, bf16[1024,1024]{1,0:T(8,128)(2,1)S(1)} %bitcast.240), kind=kOutput, calls=%fused_computation.22 | convolution fusion | flops 2500000768 | bytes 11800576 | tf_op jit(solution)/shard_map/dot_general | solution.py:36
  204.3 7.2 %convert_reduce_fusion.1 = (f32[1024]{0:T(1024)}, bf16[1184,1024]{1,0:T(8,128)(2,1)S(1)}) fusion(f32[1184,1024]{1,0:T(8,128)} %get-tuple-element.225, bf16[1184,1024]{1,0:T(8,128)(2,1)S(1)} %get-tuple-element.98, bf16[1024,1024]{1,0:T(8,128)(2,1)S(1)} %bitcast.242), kind=kOutput, calls=%fused_computation.21 | convolution fusion | flops 2500000768 | bytes 11800576 | tf_op jit(solution)/shard_map/dot_general | solution.py:36
  211.5 4.4 fusion.89
  215.9 5.3 %fusion.88 = (bf16[1184,1024]{1,0:T(8,128)(2,1)S(1)}, f32[1184,1024]{1,0:T(8,128)S(1)}) fusion(f32[1184,1024]{1,0:T(8,128)} %fusion.89, bf16[1184,1024]{1,0:T(8,128)(2,1)S(1)} %get-tuple-element.231, bf16[1024,1024]{1,0:T(8,128)(2,1)S(1)} %bitcast.245), kind=kOutput, calls=%fused_computation.288 | convolution fusion | flops 2485452800 | bytes 16646144 | tf_op jit(solution)/shard_map/dot_general | solution.py:36
  240.2 6.3 %fusion.71 = (bf16[1184,1024]{1,0:T(8,128)(2,1)S(1)}, f32[1184,1024]{1,0:T(8,128)}) fusion(f32[1184,1024]{1,0:T(8,128)S(1)} %get-tuple-element.152, f32[1184]{0:T(1024)S(1)} %broadcast_multiply_fusion.1, f32[1184]{0:T(1024)S(1)} %broadcast_multiply_fusion.2, f32[1184,1024]{1,0:T(8,128)S(1)} %get-tuple-element.150, f32[1024]{0:T(1024)S(1)} %mul.158, ...), kind=kLoop, calls=%fused_computation.273 | loop fusion | flops 13336576 | bytes 19416960 | tf_op jit(solution)/shard_map/convert_element_type | solution.py:438
  251.3 16.4 %collective-permute-done.32 = bf16[4,64,1024]{2,1,0:T(8,128)(2,1)S(1)} collective-permute-done((bf16[4,64,1024]{2,1,0:T(8,128)(2,1)S(1)}, bf16[4,64,1024]{2,1,0:T(8,128)(2,1)S(1)}, u32[]{:S(2)}, u32[]{:S(2)}) %collective-permute-start.32) | collective-permute-done | bytes 524320 | tf_op jit(solution)/shard_map/ppermute | solution.py:214
  268.7 9.8 %shard_map.262 = bf16[1184,768]{1,0:T(8,128)(2,1)S(1)} custom-call(bf16[1184,768]{1,0:T(8,128)(2,1)S(1)} %copy-done.21, bf16[2,4,592,592]{3,2,1,0:T(8,128)(2,1)} %get-tuple-element.108.probs_ref, bf16[1184,256]{1,0:T(8,128)(2,1)S(1)} %convolution_convert_fusion.1.grad_ref), custom_call_target="tpu_custom_call" | custom-call | flops 68719476736 | bytes 262144 | tf_op jit(solution)/shard_map/pallas_call | solution.py:116
  290.3 10.0 %shard_map.263 = bf16[1184,768]{1,0:T(8,128)(2,1)S(1)} custom-call(bf16[1184,768]{1,0:T(8,128)(2,1)S(1)} %copy-done.19, bf16[2,4,592,592]{3,2,1,0:T(8,128)(2,1)} %get-tuple-element.114.probs_ref, bf16[1184,256]{1,0:T(8,128)(2,1)S(1)} %convolution_convert_fusion.grad_ref), custom_call_target="tpu_custom_call" | custom-call | flops 68719476736 | bytes 262144 | tf_op jit(solution)/shard_map/pallas_call | solution.py:116
  301.2 8.3 %collective-permute-done.36 = bf16[4,64,1024]{2,1,0:T(8,128)(2,1)} collective-permute-done((bf16[4,64,1024]{2,1,0:T(8,128)(2,1)}, bf16[4,64,1024]{2,1,0:T(8,128)(2,1)}, u32[]{:S(2)}, u32[]{:S(2)}) %collective-permute-start.36) | collective-permute-done | bytes 524320 | tf_op jit(solution)/shard_map/ppermute | solution.py:214
  359.6 13.7 %reduce-scatter.11.cloned.1.call-done = bf16[1,64,2048]{2,1,0:T(8,128)(2,1)} async-done(((bf16[4,64,2048]{2,1,0:T(8,128)(2,1)}), bf16[1,64,2048]{2,1,0:T(8,128)(2,1)}) %reduce-scatter.11.cloned.1.call-update) | async-done | bytes 262160 | tf_op jit(solution)/shard_map/reduce_scatter | solution.py:314
  407.0 18.3 %reduce-scatter.7.cloned.1.call-done = bf16[1,64,1024]{2,1,0:T(8,128)(2,1)} async-done(((bf16[4,64,1024]{2,1,0:T(8,128)(2,1)}), bf16[1,64,1024]{2,1,0:T(8,128)(2,1)}) %reduce-scatter.7.cloned.1.call-update) | async-done | bytes 131088 | tf_op jit(solution)/shard_map/reduce_scatter | solution.py:314
  425.3 5.4 %collective-permute-start.53 = (bf16[64,1024]{1,0:T(8,128)(2,1)}, bf16[64,1024]{1,0:T(8,128)(2,1)S(1)}, u32[]{:S(2)}, u32[]{:S(2)}) collective-permute-start(bf16[64,1024]{1,0:T(8,128)(2,1)} %bitcast.300), channel_id=1, source_target_pairs={{0,0},{1,2},{2,1},{3,3},{4,4},{5,6},{6,5},{7,7},{8,8},{9,10},{10,9... | collective-permute-start | bytes 393224 | tf_op jit(solution)/shard_map/ppermute | solution.py:214
  (459 shorter events, 242.3 us)
Async XLA Ops:
  7.2 71.2 %all-gather.5.cloned.1.call-start = ((), (), s32[]{:S(2)}) async-start(), calls=%async_computation.8 | async-start | bytes 1310720 | tf_op jit(solution)/shard_map/all_gather | solution.py:332
  42.3 25.8 %collective-permute-start.4 = (bf16[592,1024]{1,0:T(8,128)(2,1)}, bf16[592,1024]{1,0:T(8,128)(2,1)}, u32[]{:S(2)}, u32[]{:S(2)}) collective-permute-start(bf16[592,1024]{1,0:T(8,128)(2,1)} %pad.7), channel_id=1, source_target_pairs={{0,2},{1,3},{2,0},{3,1},{4,6},{5,7},{6,4},{7,5},{8,10},{9,11},{10,... | collective-permute-start | bytes 3637256 | tf_op jit(solution)/shard_map/ppermute | solution.py:214
  42.9 67.4 %all-gather.7.cloned.1.call-start = ((), (), s32[]{:S(2)}) async-start(), calls=%async_computation.9 | async-start | bytes 1310720 | tf_op jit(solution)/shard_map/all_gather | solution.py:333
  67.2 35.5 %collective-permute-start.18 = (bf16[4,2,64,1024]{3,2,1,0:T(8,128)(2,1)S(1)}, bf16[4,2,64,1024]{3,2,1,0:T(8,128)(2,1)S(1)}, u32[]{:S(2)}, u32[]{:S(2)}) collective-permute-start(bf16[4,2,64,1024]{3,2,1,0:T(8,128)(2,1)S(1)} %shard_map.249.refs_0_), channel_id=1, source_target_pairs={{0,4},{1,5},{2,6},{3,7},{4,0},{5,1},{6,2},{7,3},{8,12},{9,13},{10,... | collective-permute-start | bytes 3145736 | tf_op jit(solution)/shard_map/ppermute | solution.py:214
  78.4 278.4 %reduce-scatter.5.cloned.1.call-start = ((), (), s32[]{:S(2)}) async-start(), calls=%async_computation.4 | async-start | bytes 655360 | tf_op jit(solution)/shard_map/reduce_scatter | solution.py:314
  130.6 32.3 %collective-permute-start.19 = (bf16[1184,1024]{1,0:T(8,128)(2,1)}, bf16[1184,1024]{1,0:T(8,128)(2,1)}, u32[]{:S(2)}, u32[]{:S(2)}) collective-permute-start(bf16[1184,1024]{1,0:T(8,128)(2,1)} %get-tuple-element.220), channel_id=1, source_target_pairs={{0,2},{1,3},{2,0},{3,1},{4,6},{5,7},{6,4},{7,5},{8,10},{9,11},{10,... | collective-permute-start | bytes 7274504 | tf_op jit(solution)/shard_map/ppermute | solution.py:214
  143.6 27.6 %collective-permute-start.20 = (bf16[4,64,1024]{2,1,0:T(8,128)(2,1)S(1)}, bf16[4,64,1024]{2,1,0:T(8,128)(2,1)S(1)}, u32[]{:S(2)}, u32[]{:S(2)}) collective-permute-start(bf16[4,64,1024]{2,1,0:T(8,128)(2,1)S(1)} %get-tuple-element.87.refs_0_), channel_id=1, source_target_pairs={{0,4},{1,5},{2,6},{3,7},{4,0},{5,1},{6,2},{7,3},{8,12},{9,13},{10,... | collective-permute-start | bytes 1572872 | tf_op jit(solution)/shard_map/ppermute | solution.py:214
  143.9 27.9 %collective-permute-start.21 = (bf16[4,64,1024]{2,1,0:T(8,128)(2,1)S(1)}, bf16[4,64,1024]{2,1,0:T(8,128)(2,1)S(1)}, u32[]{:S(2)}, u32[]{:S(2)}) collective-permute-start(bf16[4,64,1024]{2,1,0:T(8,128)(2,1)S(1)} %get-tuple-element.88.refs_0_), channel_id=1, source_target_pairs={{0,1},{1,0},{2,3},{3,2},{4,5},{5,4},{6,7},{7,6},{8,9},{9,8},{10,11... | collective-permute-start | bytes 1572872 | tf_op jit(solution)/shard_map/ppermute | solution.py:214
  184.4 41.0 %collective-permute-start.24 = (bf16[4,2,64,1024]{3,2,0,1:T(8,128)(2,1)S(1)}, bf16[4,2,64,1024]{3,2,0,1:T(8,128)(2,1)S(1)}, u32[]{:S(2)}, u32[]{:S(2)}) collective-permute-start(bf16[4,2,64,1024]{3,2,0,1:T(8,128)(2,1)S(1)} %bitcast.268), channel_id=1, source_target_pairs={{0,1},{1,0},{2,3},{3,2},{4,5},{5,4},{6,7},{7,6},{8,9},{9,8},{10,11... | collective-permute-start | bytes 3145736 | tf_op jit(solution)/shard_map/ppermute | solution.py:214
  196.4 29.0 %collective-permute-start.28 = (bf16[4,2,64,1024]{3,2,0,1:T(8,128)(2,1)S(1)}, bf16[4,2,64,1024]{3,2,0,1:T(8,128)(2,1)S(1)}, u32[]{:S(2)}, u32[]{:S(2)}) collective-permute-start(bf16[4,2,64,1024]{3,2,0,1:T(8,128)(2,1)S(1)} %bitcast.270), channel_id=1, source_target_pairs={{0,4},{1,5},{2,6},{3,7},{4,0},{5,1},{6,2},{7,3},{8,12},{9,13},{10,... | collective-permute-start | bytes 3145736 | tf_op jit(solution)/shard_map/ppermute | solution.py:214
  231.5 47.1 %collective-permute-start.29 = (bf16[4,2,64,1024]{3,2,0,1:T(8,128)(2,1)}, bf16[4,2,64,1024]{3,2,0,1:T(8,128)(2,1)S(1)}, u32[]{:S(2)}, u32[]{:S(2)}) collective-permute-start(bf16[4,2,64,1024]{3,2,0,1:T(8,128)(2,1)} %bitcast.222), channel_id=1, source_target_pairs={{0,1},{1,0},{2,3},{3,2},{4,5},{5,4},{6,7},{7,6},{8,9},{9,8},{10,11... | collective-permute-start | bytes 3145736 | tf_op jit(solution)/shard_map/ppermute | solution.py:214
  232.2 35.5 %collective-permute-start.32 = (bf16[4,64,1024]{2,1,0:T(8,128)(2,1)S(1)}, bf16[4,64,1024]{2,1,0:T(8,128)(2,1)S(1)}, u32[]{:S(2)}, u32[]{:S(2)}) collective-permute-start(bf16[4,64,1024]{2,1,0:T(8,128)(2,1)S(1)} %dynamic-slice_bitcast_fusion.2), channel_id=1, source_target_pairs={{0,1},{1,0},{2,3},{3,2},{4,5},{5,4},{6,7},{7,6},{8,9},{9,8},{10,11... | collective-permute-start | bytes 1572872 | tf_op jit(solution)/shard_map/ppermute | solution.py:214
  237.1 41.5 %collective-permute-start.33 = (bf16[4,2,64,1024]{3,2,0,1:T(8,128)(2,1)S(1)}, bf16[4,2,64,1024]{3,2,0,1:T(8,128)(2,1)S(1)}, u32[]{:S(2)}, u32[]{:S(2)}) collective-permute-start(bf16[4,2,64,1024]{3,2,0,1:T(8,128)(2,1)S(1)} %bitcast.267), channel_id=1, source_target_pairs={{0,4},{1,5},{2,6},{3,7},{4,0},{5,1},{6,2},{7,3},{8,12},{9,13},{10,... | collective-permute-start | bytes 3145736 | tf_op jit(solution)/shard_map/ppermute | solution.py:214
  285.3 27.5 %collective-permute-start.34 = (bf16[4,2,64,512]{3,2,0,1:T(8,128)(2,1)}, bf16[4,2,64,512]{3,2,0,1:T(8,128)(2,1)S(1)}, u32[]{:S(2)}, u32[]{:S(2)}) collective-permute-start(bf16[4,2,64,512]{3,2,0,1:T(8,128)(2,1)} %bitcast.228), channel_id=1, source_target_pairs={{0,1},{1,0},{2,3},{3,2},{4,5},{5,4},{6,7},{7,6},{8,9},{9,8},{10,11... | collective-permute-start | bytes 1572872 | tf_op jit(solution)/shard_map/ppermute | solution.py:214
  323.8 49.5 %reduce-scatter.11.cloned.1.call-start = ((), (), s32[]{:S(2)}) async-start(), calls=%async_computation.7 | async-start | bytes 1310720 | tf_op jit(solution)/shard_map/reduce_scatter | solution.py:314
  330.5 73.3 %reduce-scatter.9.cloned.1.call-start = ((), (), s32[]{:S(2)}) async-start(), calls=%async_computation.6 | async-start | bytes 1310720 | tf_op jit(solution)/shard_map/reduce_scatter | solution.py:314
  344.5 32.6 %collective-permute-start.43 = (bf16[592,1024]{1,0:T(8,128)(2,1)}, bf16[592,1024]{1,0:T(8,128)(2,1)}, u32[]{:S(2)}, u32[]{:S(2)}) collective-permute-start(bf16[592,1024]{1,0:T(8,128)(2,1)} %slice.447), channel_id=1, source_target_pairs={{0,2},{1,3},{2,0},{3,1},{4,6},{5,7},{6,4},{7,5},{8,10},{9,11},{10,... | collective-permute-start | bytes 3637256 | tf_op jit(solution)/shard_map/ppermute | solution.py:214
  352.4 72.9 %reduce-scatter.7.cloned.1.call-start = ((), (), s32[]{:S(2)}) async-start(), calls=%async_computation.5 | async-start | bytes 655360 | tf_op jit(solution)/shard_map/reduce_scatter | solution.py:314
  354.3 26.9 %collective-permute-start.41 = (bf16[4,64,512]{2,1,0:T(8,128)(2,1)S(1)}, bf16[4,64,512]{2,1,0:T(8,128)(2,1)S(1)}, u32[]{:S(2)}, u32[]{:S(2)}) collective-permute-start(bf16[4,64,512]{2,1,0:T(8,128)(2,1)S(1)} %dynamic-slice_bitcast_fusion.5), channel_id=1, source_target_pairs={{0,4},{1,5},{2,6},{3,7},{4,0},{5,1},{6,2},{7,3},{8,12},{9,13},{10,... | collective-permute-start | bytes 786440 | tf_op jit(solution)/shard_map/ppermute | solution.py:214
  355.6 25.6 %collective-permute-start.44 = (bf16[4,64,512]{2,1,0:T(8,128)(2,1)S(1)}, bf16[4,64,512]{2,1,0:T(8,128)(2,1)S(1)}, u32[]{:S(2)}, u32[]{:S(2)}) collective-permute-start(bf16[4,64,512]{2,1,0:T(8,128)(2,1)S(1)} %dynamic-slice_bitcast_fusion.4), channel_id=1, source_target_pairs={{0,1},{1,0},{2,3},{3,2},{4,5},{5,4},{6,7},{7,6},{8,9},{9,8},{10,11... | collective-permute-start | bytes 786440 | tf_op jit(solution)/shard_map/ppermute | solution.py:214
  356.8 76.7 %collective-permute-start.52 = (bf16[64,1024]{1,0:T(8,128)(2,1)}, bf16[64,1024]{1,0:T(8,128)(2,1)S(1)}, u32[]{:S(2)}, u32[]{:S(2)}) collective-permute-start(bf16[64,1024]{1,0:T(8,128)(2,1)} %bitcast.299), channel_id=1, source_target_pairs={{0,0},{1,2},{2,1},{3,3},{4,4},{5,6},{6,5},{7,7},{8,8},{9,10},{10,9... | collective-permute-start | bytes 393224 | tf_op jit(solution)/shard_map/ppermute | solution.py:214
  373.3 27.7 %collective-permute-start.55 = (bf16[64,2048]{1,0:T(8,128)(2,1)}, bf16[64,2048]{1,0:T(8,128)(2,1)S(1)}, u32[]{:S(2)}, u32[]{:S(2)}) collective-permute-start(bf16[64,2048]{1,0:T(8,128)(2,1)} %bitcast.297), channel_id=1, source_target_pairs={{0,0},{1,2},{2,1},{3,3},{4,4},{5,6},{6,5},{7,7},{8,8},{9,10},{10,9... | collective-permute-start | bytes 786440 | tf_op jit(solution)/shard_map/ppermute | solution.py:214
  391.0 44.2 %collective-permute-start.45 = (bf16[592,1024]{1,0:T(8,128)(2,1)}, bf16[592,1024]{1,0:T(8,128)(2,1)}, u32[]{:S(2)}, u32[]{:S(2)}) collective-permute-start(bf16[592,1024]{1,0:T(8,128)(2,1)} %slice.446), channel_id=1, source_target_pairs={{0,2},{1,3},{2,0},{3,1},{4,6},{5,7},{6,4},{7,5},{8,10},{9,11},{10,... | collective-permute-start | bytes 3637256 | tf_op jit(solution)/shard_map/ppermute | solution.py:214
  403.8 28.9 %collective-permute-start.54 = (bf16[64,2048]{1,0:T(8,128)(2,1)}, bf16[64,2048]{1,0:T(8,128)(2,1)S(1)}, u32[]{:S(2)}, u32[]{:S(2)}) collective-permute-start(bf16[64,2048]{1,0:T(8,128)(2,1)} %bitcast.298), channel_id=1, source_target_pairs={{0,0},{1,2},{2,1},{3,3},{4,4},{5,6},{6,5},{7,7},{8,8},{9,10},{10,9... | collective-permute-start | bytes 786440 | tf_op jit(solution)/shard_map/ppermute | solution.py:214
  (104 other events, 955.2 us)
Sparse Core Ops, SparseCore 0:
  43.0 30.2 all-gather.4
  78.5 31.6 all-gather.6
  323.9 20.1 reduce-scatter.4
  346.3 26.9 reduce-scatter.10
  376.1 27.6 reduce-scatter.8
  406.5 18.7 reduce-scatter.6

commit v3 on v2

v3 whole, which is shorter than its diff:
```python
import functools
import itertools
import math

import jax
import jax.numpy as jnp
import numpy as np
from jax import lax
from jax.experimental import pallas as pl
from jax.experimental.pallas import tpu as pltpu
from jax.experimental.layout import Layout, with_layout_constraint
from jax.sharding import Mesh
from jax.sharding import PartitionSpec as P

SEQ = 577
ROWS = 592
HEAD = 64
EPS = 1e-06
ALL = ("z", "x", "c", "y")
F32 = jnp.float32
BF16 = jnp.bfloat16

NN = (((1,), (0,)), ((), ()))
NT = (((1,), (1,)), ((), ()))
TN = (((0,), (0,)), ((), ()))
VMEM_LIMIT = 48 * 2**20
LITTLE = pl.CostEstimate(flops=2**20, bytes_accessed=2**18, transcendentals=0)


def rows_first(array):
    return with_layout_constraint(array, Layout(major_to_minor=(0, 1)))


def dot(left, right, dims=NN):
    return lax.dot_general(left, right, dims, preferred_element_type=F32)


def call(kernel, grid, ins, outs, *arrays):
    return pl.pallas_call(
        kernel,
        grid=grid,
        in_specs=[pl.BlockSpec(block, at) for block, at in ins],
        out_specs=[pl.BlockSpec(block, at) for block, at, _, _ in outs],
        out_shape=[jax.ShapeDtypeStruct(shape, dtype) for _, _, shape, dtype in outs],
        compiler_params=pltpu.CompilerParams(vmem_limit_bytes=VMEM_LIMIT),
        cost_estimate=LITTLE,
    )(*arrays)


def image(width):
    return (ROWS, width), lambda i: (i, 0)


def other_image(width):
    return (ROWS, width), lambda i: (1 - i, 0)


def fixed(*block):
    return block, lambda *i: (0,) * len(block)


def row_stats(values):
    mean = jnp.mean(values, axis=-1, keepdims=True)
    centered = values - mean
    inv = lax.rsqrt(jnp.mean(jnp.square(centered), axis=-1, keepdims=True) + EPS)
    return centered * inv, inv


def norm_back(upstream, normed, inv_scale, gain):
    scaled = upstream * gain
    first = jnp.mean(scaled, axis=-1, keepdims=True)
    second = jnp.mean(scaled * normed, axis=-1, keepdims=True)
    return inv_scale * (scaled - first - normed * second)


def norm_one(tokens, vectors):
    width = tokens.shape[1]

    def kernel(tokens_ref, vec_ref, out_ref):
        hat, _ = row_stats(tokens_ref[...].astype(F32))
        out_ref[...] = (hat * vec_ref[0:1] + vec_ref[1:2]).astype(BF16)

    out = image(width) + (tokens.shape, BF16)
    return call(kernel, (2,), [image(width), fixed(8, width)], [out], tokens, vectors)[0]


def attend(projected, heads):
    width = heads * HEAD

    def kernel(qkv_ref, mixed_ref, probs_ref):
        lane = lax.broadcasted_iota(jnp.int32, (ROWS, 128), 1)
        row = lax.broadcasted_iota(jnp.int32, (ROWS, ROWS), 0)
        for pair in range(heads // 2):
            at = pair * 128
            queries = qkv_ref[:, at : at + 128]
            keys = qkv_ref[:, width + at : width + at + 128]
            values = qkv_ref[:, 2 * width + at : 2 * width + at + 128]
            mixed = []
            for half in range(2):
                inside = (lane < HEAD) if half == 0 else (lane >= HEAD)
                own_keys = jnp.where(inside, keys, jnp.zeros_like(keys)) * BF16(0.125)
                scores = dot(own_keys, queries, NT)
                scores = jnp.where(row < SEQ, scores, -1e30)
                shifted = jnp.exp(scores - jnp.max(scores, axis=0, keepdims=True))
                total = jnp.sum(shifted, axis=0, keepdims=True)
                probs = (shifted * (1.0 / total)).astype(BF16)
                probs_ref[0, 2 * pair + half] = probs
                mixed.append(dot(probs, values, TN))
            mixed_ref[:, at : at + 128] = jnp.where(lane < HEAD, mixed[0], mixed[1]).astype(BF16)

    rows = 2 * ROWS
    return call(
        kernel,
        (2,),
        [image(3 * width)],
        [
            image(width) + ((rows, width), BF16),
            ((1, heads, ROWS, ROWS), lambda i: (i, 0, 0, 0), (2, heads, ROWS, ROWS), BF16),
        ],
        projected,
    )


def attend_back(projected, probs, mixed_grad, heads):
    width = heads * HEAD

    def kernel(qkv_ref, probs_ref, grad_ref, out_ref, sums_ref):
        lane = lax.broadcasted_iota(jnp.int32, (ROWS, 128), 1)
        for pair in range(heads // 2):
            at = pair * 128
            queries = qkv_ref[:, at : at + 128]
            keys = qkv_ref[:, width + at : width + at + 128]
            values = qkv_ref[:, 2 * width + at : 2 * width + at + 128]
            grad = grad_ref[:, at : at + 128]
            keys_t = (keys * BF16(0.125)).T
            queries_s = queries * BF16(0.125)
            d_query, d_key, d_value = [], [], []
            for half in range(2):
                inside = (lane < HEAD) if half == 0 else (lane >= HEAD)
                own_values = jnp.where(inside, values, jnp.zeros_like(values))
                low_probs = probs_ref[0, 2 * pair + half]
                prob_grad = dot(own_values, grad, NT)
                wide_probs = low_probs.astype(F32)
                product = prob_grad * wide_probs
                weighted = jnp.sum(product, axis=0, keepdims=True)
                score_grad = (product - wide_probs * weighted).astype(BF16)
                d_value.append(dot(low_probs, grad))
                d_key.append(dot(score_grad, queries_s))
                d_query.append(dot(keys_t[half * HEAD : (half + 1) * HEAD], score_grad))
            parts = [
                jnp.concatenate(d_query, 0).T,
                jnp.where(lane < HEAD, d_key[0], d_key[1]),
                jnp.where(lane < HEAD, d_value[0], d_value[1]),
            ]
            for n, part in enumerate(parts):
                out_ref[:, n * width + at : n * width + at + 128] = part.astype(BF16)
        total = jnp.sum(out_ref[...].astype(F32), axis=0, keepdims=True)
        total = jnp.broadcast_to(total, sums_ref.shape)

        @pl.when(pl.program_id(0) == 0)
        def _():
            sums_ref[...] = total

        @pl.when(pl.program_id(0) != 0)
        def _():
            sums_ref[...] += total

    return pl.pallas_call(
        kernel,
        grid=(2,),
        in_specs=[
            pl.BlockSpec(*image(3 * width)),
            pl.BlockSpec((1, heads, ROWS, ROWS), lambda i: (i, 0, 0, 0)),
            pl.BlockSpec(*image(width)),
        ],
        out_specs=[pl.BlockSpec(*image(3 * width)), pl.BlockSpec(*fixed(8, 3 * width))],
        out_shape=[
            jax.ShapeDtypeStruct((2 * ROWS, 3 * width), BF16),
            jax.ShapeDtypeStruct((8, 3 * width), F32),
        ],
        compiler_params=pltpu.CompilerParams(vmem_limit_bytes=VMEM_LIMIT),
        cost_estimate=LITTLE,
    )(projected, probs, mixed_grad)


def norm_two(tokens, low, moved, vectors):
    width = tokens.shape[1]

    def kernel(tokens_ref, low_ref, moved_ref, vec_ref, resid_ref, out_ref):
        branch = low_ref[...].astype(F32) + moved_ref[...].astype(F32)
        residual = tokens_ref[...].astype(F32) + branch + vec_ref[4:5]
        resid_ref[...] = residual
        hat, _ = row_stats(residual)
        out_ref[...] = (hat * vec_ref[2:3] + vec_ref[3:4]).astype(BF16)

    return call(
        kernel,
        (2,),
        [image(width), image(width), other_image(width), fixed(8, width)],
        [image(width) + (tokens.shape, F32), image(width) + (tokens.shape, BF16)],
        tokens,
        low,
        moved,
        vectors,
    )


def weight_grad(rows, grad):
    return rows_first(dot(rows, grad, TN).astype(BF16))


def attention_weight_grad(normed, qkv_grad, attn_grad, mixed):
    deep, width = normed.shape[1], mixed.shape[1]
    cut = 256
    half = 2 * width

    def kernel(normed_ref, qkv_ref, grad_ref, mixed_ref, first_ref, second_ref):
        grad = dot(normed_ref[...], qkv_ref[...], TN).astype(BF16)
        first_ref[...] = grad[:, :half]
        second_ref[:, :width] = grad[:, half:]
        second_ref[:, width:] = dot(grad_ref[...], mixed_ref[...], TN).astype(BF16)

    column = ((2 * ROWS, cut), lambda j: (0, j))
    out = ((cut, half), lambda j: (j, 0), (deep, half), BF16)
    return call(
        kernel,
        (deep // cut,),
        [column, fixed(2 * ROWS, 3 * width), column, fixed(2 * ROWS, width)],
        [out, out],
        normed,
        qkv_grad,
        attn_grad,
        mixed,
    )


def norm_two_back(low, moved, residual, down, vectors):
    width = low.shape[1]

    def kernel(low_ref, moved_ref, resid_ref, down_ref, vec_ref, own_ref, out_ref, sums_ref):
        back = low_ref[...].astype(F32) + moved_ref[...].astype(F32)
        upstream = down_ref[...].astype(F32)
        hat, inv = row_stats(resid_ref[...])
        grad = upstream + norm_back(back, hat, inv, vec_ref[2:3])
        out_ref[...] = grad.astype(BF16)

        @pl.when(pl.program_id(0) == 0)
        def _():
            own_ref[...] = grad
            for n, part in enumerate((back * hat, back, grad, upstream)):
                sums_ref[n : n + 1] = jnp.sum(part, axis=0, keepdims=True)

    return call(
        kernel,
        (2,),
        [image(width), other_image(width), image(width), image(width), fixed(8, width)],
        [
            fixed(ROWS, width) + ((ROWS, width), F32),
            image(width) + ((2 * ROWS, width), BF16),
            fixed(8, width) + ((8, width), F32),
        ],
        low,
        moved,
        residual,
        down,
        vectors,
    )


def norm_one_back(low, moved, tokens, grad, vectors):
    width = low.shape[1]

    def kernel(low_ref, moved_ref, tokens_ref, grad_ref, vec_ref, out_ref, sums_ref):
        back = low_ref[...].astype(F32) + moved_ref[...].astype(F32)
        hat, inv = row_stats(tokens_ref[...].astype(F32))
        total = grad_ref[...] + norm_back(back, hat, inv, vec_ref[0:1])
        out_ref[...] = total[:SEQ]
        for n, part in enumerate((back * hat, back)):
            sums_ref[n : n + 1] = jnp.sum(part, axis=0, keepdims=True)

    own_rows = fixed(ROWS, width)
    return call(
        kernel,
        (1,),
        [own_rows, own_rows, own_rows, own_rows, fixed(8, width)],
        [
            fixed(SEQ, width) + ((SEQ, width), F32),
            fixed(8, width) + ((8, width), F32),
        ],
        low,
        moved,
        tokens,
        grad,
        vectors,
    )


def layer_output(residual, low, moved, vectors):
    width = low.shape[1]

    def kernel(resid_ref, low_ref, moved_ref, vec_ref, out_ref):
        branch = low_ref[...].astype(F32) + moved_ref[...].astype(F32)
        out_ref[...] = (resid_ref[...] + branch + vec_ref[5:6]).astype(BF16)[:SEQ]

    own_rows = fixed(ROWS, width)
    out = fixed(SEQ, width) + ((SEQ, width), BF16)
    ins = [own_rows, own_rows, own_rows, fixed(8, width)]
    return call(kernel, (1,), ins, [out], residual, low, moved, vectors)[0]


def place(parts, spots, shape, block):
    def kernel(spot_ref, *refs):
        out_ref, sems = refs[-2], refs[-1]
        copies = []
        for n in range(len(parts)):
            copies.append(
                pltpu.make_async_copy(refs[n], block(out_ref, spot_ref[n]), sems.at[n])
            )
        for copy in copies:
            copy.start()
        for copy in copies:
            copy.wait()

    return pl.pallas_call(
        kernel,
        grid_spec=pltpu.PrefetchScalarGridSpec(
            num_scalar_prefetch=1,
            grid=(1,),
            in_specs=[pl.BlockSpec(memory_space=pl.ANY)] * len(parts),
            out_specs=pl.BlockSpec(memory_space=pl.ANY),
            scratch_shapes=[pltpu.SemaphoreType.DMA((len(parts),))],
        ),
        out_shape=jax.ShapeDtypeStruct(shape, parts[0].dtype),
        compiler_params=pltpu.CompilerParams(vmem_limit_bytes=2**20),
        cost_estimate=LITTLE,
    )(spots, *parts)


def pack(qkv, proj, quarter):
    def kernel(qkv_ref, proj_ref, out_ref):
        for colour in range(2):
            cut = slice(colour * quarter, (colour + 1) * quarter)
            for n in range(4):
                at = (4 * colour + n) * quarter
                part = qkv_ref[n, :, cut] if n < 3 else proj_ref[:, cut]
                out_ref[:, at : at + quarter] = part

    return pl.pallas_call(
        kernel,
        out_shape=jax.ShapeDtypeStruct((proj.shape[0], 8 * quarter), proj.dtype),
        compiler_params=pltpu.CompilerParams(vmem_limit_bytes=VMEM_LIMIT),
        cost_estimate=LITTLE,
    )(qkv, proj)


def build(n_z, n_x):
    sizes = dict(z=n_z, x=n_x, c=2, y=2)

    def pairs(move, only=None):
        found = []
        names = ALL
        spots = list(itertools.product(*[range(sizes[a]) for a in names]))
        index = {spot: n for n, spot in enumerate(spots)}
        for spot in spots:
            here = dict(zip(names, spot))
            if only is not None and not only(here):
                continue
            there = dict(here)
            move(there)
            found.append((index[spot], index[tuple(there[a] for a in names)]))
        return found

    def shift(axis, by, only=None):
        def move(spot):
            spot[axis] = (spot[axis] + by) % sizes[axis]

        return pairs(move, only)

    def flip(axis, by):
        def move(spot):
            spot[axis] ^= by

        return pairs(move)

    def send(value, perm):
        return lax.ppermute(value, ALL, perm)

    def exchange(spot):
        spot["c"], spot["y"] = spot["y"], spot["c"]

    transpose = pairs(exchange)

    def on_device(
        tokens,
        ln1_gain,
        ln1_bias,
        qkv_weight,
        qv_bias,
        proj_weight,
        proj_bias,
        ln2_gain,
        ln2_bias,
        fc1_weight,
        fc1_bias,
        fc2_weight,
        fc2_bias,
        cotangent,
    ):
        z, x, c, y = [lax.axis_index(a) for a in ALL]
        owner = c == y
        where_am_i = dict(z=z, x=x, c=c, y=y)
        width = tokens.shape[1]
        depth = fc1_weight.shape[0]
        heads = qv_bias.shape[1] // 2

        def swap(value):
            return send(value, shift("c", 1))

        def after(value, *earlier):
            return lax.optimization_barrier((value,) + earlier)[0]

        quarter = proj_weight.shape[0] // 2
        n_qkv = 3 * quarter
        hidden_half = fc1_weight.shape[1] // 2
        proj_t = proj_weight.T
        fc2_t = fc2_weight.T
        shards = [pack(qkv_weight.transpose(1, 0, 2), proj_t, quarter), fc1_weight, fc2_t]

        def spots(axis):
            count = sizes[axis]
            return (where_am_i[axis] + jnp.arange(count, dtype=jnp.int32)) % count

        def from_all(value, axis, shape, block, earlier=()):
            moved = [send(value, shift(axis, -k)) for k in range(1, sizes[axis])]
            if earlier:
                moved = [after(part, *earlier) for part in moved]
            return place([value] + moved, spots(axis), shape, block)

        def crossed(shard):
            return send(shard, transpose)

        def together(*values):
            return lax.optimization_barrier(values)

        def halves(line, *earlier):
            wide = line.shape[2] // 2
            return together(line[:, :, :wide], line[:, :, wide:], *earlier)[:2]

        def step_one(first, second, *earlier):
            at = (n_z, n_x, depth, first.shape[2])
            first = from_all(first, "x", at, lambda ref, n: ref.at[:, n], earlier)
            at = (n_z, 2, depth, second.shape[2])
            second = from_all(second, "y", at, lambda ref, n: ref.at[:, n], earlier)
            return together(first, second)

        def step_two(first, second, *earlier):
            wide = first.shape[3]
            at = (n_z, n_x, 2, depth, wide)
            first = from_all(first, "y", at, lambda ref, n: ref.at[:, :, n], earlier)
            second = from_all(second, "x", at, lambda ref, n: ref.at[:, n], earlier)
            return first.reshape(width, wide), second.reshape(width, wide)

        def pick(array, axis, index):
            return lax.dynamic_index_in_dim(array, index, axis, keepdims=False)

        def give(array, axis, dim):
            count, here = sizes[axis], where_am_i[axis]
            moved = [
                send(pick(array, dim, (here + k) % count), shift(axis, k))
                for k in range(1, count)
            ]
            return moved, pick(array, dim, here)

        def summed(given, *earlier):
            moved, own_part = given
            total = own_part.astype(F32)
            for part in moved:
                total = total + (after(part, *earlier) if earlier else part).astype(F32)
            return total.astype(BF16)

        def scatter_one(first, second):
            at = (n_z, n_x, 2, depth, first.shape[1])
            return give(first.reshape(at), "y", 2), give(second.reshape(at), "x", 1)

        def scatter_two(first, second):
            return give(first, "x", 1), give(second, "y", 1)

        def gathered(parts):
            return jnp.concatenate(parts, axis=2)

        def scatter_three(both):
            return lax.psum_scatter(both, "z", scatter_dimension=0, tiled=False)

        shard_one = crossed(shards[0])
        shard_two = crossed(after(shards[1], shard_one))
        shard_three = crossed(after(shards[2], shard_one))
        shard_one = after(shard_one, shard_two, shard_three)
        wide = shards[0].shape[1] // 2
        around = [shard_one] + [send(shard_one, shift("z", -k)) for k in range(1, n_z)]
        line_one = [
            place(
                [part[:, cut] for part in around],
                spots("z"),
                (n_z, depth, wide),
                lambda ref, n: ref.at[n],
            )
            for cut in (slice(0, wide), slice(wide, 2 * wide))
        ]
        line_one = together(*line_one)

        def both_images(value):
            value = jnp.pad(value, ((0, ROWS - SEQ), (0, 0)))
            return jnp.concatenate([value, swap(value)])

        inputs = both_images(after(tokens, around[1]))
        down = both_images(after(cotangent, around[1]))

        small = jnp.concatenate(
            [after(ln1_gain, around[1]), ln1_bias, ln2_gain, ln2_bias, proj_bias, fc2_bias]
            + [qv_bias.reshape(-1), fc1_bias.reshape(-1)]
        )[None]

        def spread(small, axis):
            for n in range(sizes[axis].bit_length() - 1):
                moved = send(small, flip(axis, 2**n))
                low_side = (where_am_i[axis] // 2**n) % 2 == 0
                small = jnp.where(
                    low_side, jnp.concatenate([small, moved]), jnp.concatenate([moved, small])
                )
            return small[None]

        for axis in ("c", "y", "x"):
            small = spread(small, axis)
        small = spread(after(small, *line_one), "z")
        square_one = step_one(*line_one, small)
        line_two = lax.all_gather(after(shard_two, small), "z", axis=0)
        line_three = lax.all_gather(after(shard_three, small), "z", axis=0)
        share = ln1_gain.shape[0]
        small = small.reshape(n_z, n_x, 2, 2, -1)
        small = small.transpose(0, 1, 3, 2, 4)
        vectors = small[..., : 6 * share].reshape(-1, 6, share).transpose(1, 0, 2).reshape(6, -1)
        vectors = jnp.pad(vectors.astype(F32), ((0, 2), (0, 0)))
        mine = pick(small[..., 6 * share :], 3, c).astype(F32)
        per_qv = qv_bias.shape[2]
        n_qv = qv_bias.size
        qv_half = mine[..., :n_qv].reshape((-1,) + qv_bias.shape)
        qv_half = qv_half.transpose(1, 2, 0, 3).reshape(2, -1)
        per_fc1 = fc1_bias.shape[1]
        fc1_half = mine[..., n_qv:].reshape((-1,) + fc1_bias.shape)
        fc1_half = fc1_half.transpose(1, 0, 2).reshape(-1)

        normed_one = norm_one(inputs, vectors)

        half_two = halves(line_two, normed_one)
        attn_w = step_two(*square_one, *half_two)
        projected, probs, mixed = [None] * 2, [None] * 2, [None] * 2

        def attend_half(colour, rows):
            cut = slice(colour * quarter, (colour + 1) * quarter)
            bias = jnp.concatenate(
                [qv_half[0, cut], jnp.zeros((quarter,), F32), qv_half[1, cut]]
            )
            projected[colour] = (dot(rows, attn_w[colour][:, :n_qkv]) + bias).astype(BF16)
            mixed[colour], probs[colour] = attend(projected[colour], heads)

        def back_product(lefts, weights):
            return (dot(lefts[0], weights[0], NT) + dot(lefts[1], weights[1], NT)).astype(BF16)

        attend_half(0, normed_one)
        square_two = step_one(*half_two, mixed[0])
        attend_half(1, after(normed_one, *square_two))
        half_three = halves(line_three, mixed[1])
        fc1_w = step_two(*square_two, *half_three)
        proj_ab = [w[:, n_qkv:] for w in attn_w]
        low = back_product([after(m, *fc1_w) for m in mixed], proj_ab)
        residual, normed_two = norm_two(inputs, low, swap(low), vectors)
        square_three = step_one(*half_three, normed_two)

        hidden, slope = [], []
        rows_two = after(normed_two, *square_three)
        for colour, weight in enumerate(fc1_w):
            bias = fc1_half[colour * hidden_half : (colour + 1) * hidden_half]
            pre = dot(rows_two, weight) + bias
            cdf = 0.5 * (1.0 + lax.erf(pre * (1.0 / math.sqrt(2.0))))
            density = jnp.exp(-0.5 * pre * pre) * (1.0 / math.sqrt(2.0 * math.pi))
            hidden.append((pre * cdf).astype(BF16))
            slope.append((cdf + pre * density).astype(BF16))

        grad_fc2 = [weight_grad(down, h) for h in hidden]
        fc2_one = scatter_one(*grad_fc2)
        fc2_w = step_two(*square_three, *grad_fc2)
        down_late = after(down, *fc2_w)
        hidden_grad = [
            (dot(down_late, w) * s.astype(F32)).astype(BF16) for w, s in zip(fc2_w, slope)
        ]
        unit_sums = [jnp.sum(g.astype(F32), axis=0) for g in hidden_grad]
        low = back_product(hidden_grad, fc1_w)
        moved = swap(low)
        fc2_sums = [summed(given, low) for given in fc2_one]
        fc2_two = scatter_two(*fc2_sums)
        normed_late = after(normed_two, *fc2_sums)
        grad_fc1 = [weight_grad(normed_late, g) for g in hidden_grad]
        fc1_one = scatter_one(*grad_fc1)
        resid_grad, attn_grad, sums_two = norm_two_back(
            low, after(moved, *grad_fc1), residual, down, vectors
        )

        fc2_lines = gathered([summed(given, attn_grad) for given in fc2_two])
        scat_fc2 = scatter_three(fc2_lines)
        attn_late = after(attn_grad, fc2_lines)
        mixed_grad = [dot(attn_late, w).astype(BF16) for w in proj_ab]
        back_a, sums_a = attend_back(projected[0], probs[0], mixed_grad[0], heads)
        grads_a = attention_weight_grad(normed_one, back_a, attn_grad, mixed[0])
        a_one = scatter_one(*grads_a)
        fc1_sums = [summed(given, *grads_a) for given in fc1_one]
        fc1_two = scatter_two(*fc1_sums)
        back_b, sums_b = attend_back(
            after(projected[1], *fc1_sums), probs[1], mixed_grad[1], heads
        )
        fc1_lines = gathered([summed(given, back_b) for given in fc1_two])
        scat_fc1 = scatter_three(fc1_lines)
        a_sums = [summed(given, fc1_lines) for given in a_one]
        a_two = scatter_two(*a_sums)
        grads_b = attention_weight_grad(
            after(normed_one, *a_sums, scat_fc2), back_b, attn_grad, mixed[1]
        )
        b_one = scatter_one(*grads_b)
        a_lines = gathered([summed(given, *grads_b) for given in a_two])
        scat_a = scatter_three(a_lines)
        qkv_ab = [w[:, :n_qkv] for w in attn_w]
        low = back_product((after(back_a, a_lines), back_b), qkv_ab)
        b_sums = [summed(given, low) for given in b_one]
        b_two = scatter_two(*b_sums)
        moved = after(swap(low[ROWS:]), *b_sums, scat_fc1)
        grad_tokens, sums_one = norm_one_back(low, moved, inputs, resid_grad, vectors)
        b_lines = gathered([summed(given, grad_tokens) for given in b_two])
        scat_b = scatter_three(b_lines)
        scat_attn = jnp.concatenate([scat_a, scat_b], axis=1)
        scat_fc1, scat_fc2, scat_attn = [
            send(part, transpose) for part in (scat_fc1, scat_fc2, scat_attn)
        ]
        scat_attn = scat_attn.astype(F32)

        hidden_late = [after(h, b_lines, scat_a) for h in hidden]
        branch_two = back_product(hidden_late, fc2_w)
        output = layer_output(residual, branch_two, swap(branch_two[ROWS:]), vectors)

        six = [sums_one[0], sums_one[1]] + [sums_two[n] for n in range(4)]
        grad_qv = [sums_a[0], sums_b[0]]
        grad_fc1_shift = jnp.concatenate(unit_sums)
        halves = [g[:quarter] for g in grad_qv] + [g[2 * quarter :] for g in grad_qv]
        sums = jnp.concatenate(six + halves + [grad_fc1_shift])[None]
        for axis in ("z", "x", "y"):
            moved = [send(sums, shift(axis, k)) for k in range(1, sizes[axis])]
            sums = functools.reduce(jnp.add, moved, sums)
        moved = swap(sums)[0]
        sums = sums[0]
        spot = ((z * n_x + x) * 2 + c) * 2 + y
        small_own = (sums[: 6 * width] + moved[: 6 * width]).reshape(6, -1, share)
        small_own = pick(small_own, 1, spot)
        half = jnp.where(owner, sums[6 * width :], moved[6 * width :])
        deep = (z * n_x + x) * 2 + c
        grad_qv = half[: 4 * quarter].reshape(2, qv_bias.shape[1], -1, per_qv)
        grad_qv = pick(grad_qv, 2, deep)
        grad_fc1_bias = pick(half[4 * quarter :].reshape(fc1_bias.shape[0], -1, per_fc1), 1, deep)

        def joined(index):
            at = index * quarter
            cuts = [scat_attn[:, at + half : at + half + quarter] for half in (0, 4 * quarter)]
            return jnp.concatenate(cuts, axis=1)

        grad_qkv = jnp.stack([joined(0), joined(1), joined(2)], axis=1)
        return (
            output,
            grad_tokens,
            small_own[0],
            small_own[1],
            grad_qkv,
            grad_qv,
            joined(3).T,
            small_own[4],
            small_own[2],
            small_own[3],
            scat_fc1.astype(F32),
            grad_fc1_bias,
            scat_fc2.astype(F32).T,
            small_own[5],
        )

    return on_device


def solution(mesh):
    chips = mesh.shape["dp"] // 2
    n_x = 1
    while n_x * n_x * 4 <= chips and chips % (n_x * 2) == 0:
        n_x *= 2
    n_z = chips // n_x
    fine = Mesh(np.asarray(mesh.devices).reshape(n_z, n_x, 2, 2), ALL)
    dp = ("z", "x", "c")
    every = P(ALL)
    rows = P(ALL, None)
    in_specs = (
        rows,
        every,
        every,
        P(dp, None, "y"),
        P(None, "y", dp),
        P("y", dp),
        every,
        every,
        every,
        P(dp, "y"),
        P("y", dp),
        P("y", dp),
        every,
        rows,
    )
    out_specs = (
        rows,
        rows,
        every,
        every,
        P(dp, None, "y"),
        P(None, "y", dp),
        P("y", dp),
        every,
        every,
        every,
        P(dp, "y"),
        P("y", dp),
        P("y", dp),
        every,
    )
    return jax.shard_map(
        build(n_z, n_x), mesh=fine, in_specs=in_specs, out_specs=out_specs, check_vma=False
    )
```

time: 452 us -> 432 us (0.956)
  waiting for transfers between devices: 116 us -> 72.7 us
  Pallas kernels: 49.6 us -> 92.5 us
  other arithmetic: 56.5 us -> 29.9 us
  local copies, waits for them, and re-layouts: 51.9 us -> 66.6 us
  matrix products: 82.8 us -> 69.7 us
  starting transfers between devices: 73.1 us -> 79.7 us
    pallas_call x4 -> x11, Pallas kernels: 35.2 us -> 71.7 us  [the longest x9 51.2 us: call(): pl.pallas_call(kernel, grid=grid, in_specs=[pl.BlockSpec(block, at) for b...]
    reduce_scatter x4, waiting for transfers between devices: 33.5 us -> 6.91 us  [scatter_three(): return lax.psum_scatter(both, 'z', scatter_dimension=0, tiled=False)]
    reduce_sum x11 -> x0, other arithmetic: 18 us -> none  [the longest x2 4.55 us: row_stats(): mean = jnp.mean(values, axis=-1, keepdims=True)]
    convert_element_type x5 -> x0, other arithmetic: 15.9 us -> none  [the longest x1 6.29 us: on_device(): attn_grad = resid_grad.astype(BF16)]
    dot_general x24 -> x20, matrix products: 82.8 us -> 69.7 us  [dot(): return lax.dot_general(left, right, dims, preferred_element_type=F32)]
    ppermute x56 -> x54, waiting for transfers between devices: 77.9 us -> 65.6 us  [send(): return lax.ppermute(value, ALL, perm)]
    slice x15 -> x10, local copies, waits for them, and re-layouts: 16 us -> 5.72 us  [the longest x2 3.36 us: halves(): return together(line[:, :, :wide], line[:, :, wide:], *earlier)[:2]]
    dynamic_slice x20, local copies, waits for them, and re-layouts: 6.83 us -> 15.7 us  [pick(): return lax.dynamic_index_in_dim(array, index, axis, keepdims=False)]
  transfers between devices with their start and end apart: 62 -> 60, of which waited for: 24 -> 25; matrix products, arithmetic and copies ran while one was open for 34% -> 31% of each run, Pallas kernels for 9% -> 21%
where the time goes in v3:
time: 432 us; the launch traced here: 427 us
  Pallas kernels  92.5 us (21%)
  starting transfers between devices  79.7 us (18%)
  waiting for transfers between devices  72.7 us (17%)
  matrix products  69.7 us (16%)
  local copies, waits for them, and re-layouts  66.6 us (15%)
  other arithmetic  29.9 us (7%)
  between operations  16.1 us (4%)
    ppermute x54, starting transfers between devices, send(): return lax.ppermute(value, ALL, perm)  79.2 us
    dot_general x20, matrix products, dot(): return lax.dot_general(left, right, dims, preferred_element_type=F32)  69.7 us
    ppermute x54, waiting for transfers between devices, send(): return lax.ppermute(value, ALL, perm)  65.6 us
    pallas_call x9, Pallas kernels, call(): pl.pallas_call(kernel, grid=grid, in_specs=[pl.BlockSpec(block, at) for b...  51.2 us
    unnamed x165, local copies, waits for them, and re-layouts  21.8 us
    pallas_call x14, Pallas kernels, place(): pl.pallas_call(kernel, grid_spec=pltpu.PrefetchScalarGridSpec(num_scalar_...  20.8 us
    pallas_call x2, Pallas kernels, attend_back(): pl.pallas_call(kernel, grid=(2,), in_specs=[pl.BlockSpec(*image(3 * width...  20.5 us
    convert_element_type x16, other arithmetic, summed(): return total.astype(BF16)  16.3 us
  transfers between devices with their start and end apart: 60, of which 25 were waited for; matrix products, arithmetic and copies ran while one was open for 31% of the time, Pallas kernels for 21%

profile of v3, /device:TPU:1, one launch (start us, length us, event | category | flops | bytes accessed | tf_op | source)
XLA Modules:
  0.0 427.4 jit_solution(4824595492328305761)
XLA Ops:
  9.0 4.7 %collective-permute-start = (bf16[64,2048]{1,0:T(8,128)(2,1)S(1)}, bf16[64,2048]{1,0:T(8,128)(2,1)S(1)}, u32[]{:S(2)}, u32[]{:S(2)}) collective-permute-start(bf16[64,2048]{1,0:T(8,128)(2,1)S(1)} %shard_map.245), channel_id=1, source_target_pairs={{0,0},{1,2},{2,1},{3,3},{4,4},{5,6},{6,5},{7,7},{8,8},{9,10},{10,9... | collective-permute-start | bytes 786440 | tf_op jit(solution)/shard_map/ppermute | solution.py:386
  41.9 4.7 %collective-permute-done.8 = bf16[64,2048]{1,0:T(8,128)(2,1)S(1)} collective-permute-done((bf16[64,2048]{1,0:T(8,128)(2,1)S(1)}, bf16[64,2048]{1,0:T(8,128)(2,1)S(1)}, u32[]{:S(2)}, u32[]{:S(2)}) %collective-permute-start.8) | collective-permute-done | bytes 262176 | tf_op jit(solution)/shard_map/ppermute | solution.py:386
  61.5 5.0 %collective-permute-start.4 = (bf16[592,1024]{1,0:T(8,128)(2,1)}, bf16[592,1024]{1,0:T(8,128)(2,1)}, u32[]{:S(2)}, u32[]{:S(2)}) collective-permute-start(bf16[592,1024]{1,0:T(8,128)(2,1)} %pad.13), channel_id=1, source_target_pairs={{0,2},{1,3},{2,0},{3,1},{4,6},{5,7},{6,4},{7,5},{8,10},{9,11},{10,... | collective-permute-start | bytes 3637256 | tf_op jit(solution)/shard_map/ppermute | solution.py:386
  69.6 11.0 %collective-permute-done.13.refs_1_ = bf16[4,64,1024]{2,1,0:T(8,128)(2,1)S(1)} collective-permute-done((bf16[4,64,1024]{2,1,0:T(8,128)(2,1)S(1)}, bf16[4,64,1024]{2,1,0:T(8,128)(2,1)S(1)}, u32[]{:S(2)}, u32[]{:S(2)}) %collective-permute-start.13) | collective-permute-done | bytes 524320 | tf_op jit(solution)/shard_map/ppermute | solution.py:386
  96.3 11.3 %collective-permute-done.14.refs_1_ = bf16[4,2,64,1024]{3,2,1,0:T(8,128)(2,1)} collective-permute-done((bf16[4,2,64,1024]{3,2,1,0:T(8,128)(2,1)S(1)}, bf16[4,2,64,1024]{3,2,1,0:T(8,128)(2,1)}, u32[]{:S(2)}, u32[]{:S(2)}) %collective-permute-start.14) | collective-permute-done | bytes 1048608 | tf_op jit(solution)/shard_map/ppermute | solution.py:386
  111.7 7.6 %shard_map.252 = (bf16[1184,256]{1,0:T(8,128)(2,1)S(1)}, bf16[2,4,592,592]{3,2,1,0:T(8,128)(2,1)}) custom-call(bf16[1184,768]{1,0:T(8,128)(2,1)S(1)} %fusion.10.qkv_ref), custom_call_target="tpu_custom_call" | custom-call | flops 1048576 | bytes 262144 | tf_op jit(solution)/shard_map/pallas_call | solution.py:39
  136.3 8.0 %shard_map.256 = (bf16[1184,256]{1,0:T(8,128)(2,1)S(1)}, bf16[2,4,592,592]{3,2,1,0:T(8,128)(2,1)}) custom-call(bf16[1184,768]{1,0:T(8,128)(2,1)S(1)} %fusion.11.qkv_ref), custom_call_target="tpu_custom_call" | custom-call | flops 1048576 | bytes 262144 | tf_op jit(solution)/shard_map/pallas_call | solution.py:39
  176.8 6.1 %shard_map.259 = (f32[1184,1024]{1,0:T(8,128)}, bf16[1184,1024]{1,0:T(8,128)(2,1)S(1)}) custom-call(bf16[1184,1024]{1,0:T(8,128)(2,1)S(1)} %pad_maximum_fusion.tokens_ref, bf16[1184,1024]{1,0:T(8,128)(2,1)} %add_convert_fusion.3.low_ref, bf16[1184,1024]{1,0:T(8,128)(2,1)} %collective-permute-done.20.moved_ref, f32[8,1024]{1,0:T(8,128)S(1)} %copy-done.32), custom_call_target="tpu_custom_call" | custom-call | flops 1048576 | bytes 262144 | tf_op jit(solution)/shard_map/pallas_call | solution.py:39
  187.3 5.1 %multiply_convert_fusion.2 = (bf16[1184,1024]{1,0:T(8,128)(2,1)S(1)}, f32[1184,1024]{1,0:T(8,128)S(1)}) fusion(f32[1024]{0:T(1024)S(1)} %copy-done.69, bf16[1184,1024]{1,0:T(8,128)(2,1)S(1)} %get-tuple-element.141, bf16[1024,1024]{1,0:T(8,128)(2,1)S(1)} %bitcast.230), kind=kOutput, calls=%fused_computation.19 | convolution fusion | flops 2490302464 | bytes 11800576 | tf_op jit(solution)/shard_map/dot_general | solution.py:35
  192.5 5.1 %multiply_convert_fusion.3 = (bf16[1184,1024]{1,0:T(8,128)(2,1)S(1)}, f32[1184,1024]{1,0:T(8,128)S(1)}) fusion(f32[1024]{0:T(1024)S(1)} %copy-done.70, bf16[1184,1024]{1,0:T(8,128)(2,1)S(1)} %get-tuple-element.141, bf16[1024,1024]{1,0:T(8,128)(2,1)S(1)} %bitcast.232), kind=kOutput, calls=%fused_computation.21 | convolution fusion | flops 2490302464 | bytes 11800576 | tf_op jit(solution)/shard_map/dot_general | solution.py:35
  197.7 5.7 %convolution_convert_fusion.4 = bf16[1024,1024]{1,0:T(8,128)(2,1)S(1)} fusion(bf16[1184,1024]{1,0:T(8,128)(2,1)S(1)} %get-tuple-element.173, bf16[592,1024]{1,0:T(8,128)(2,1)} %collective-permute-done.23, bf16[592,1024]{1,0:T(8,128)(2,1)} %pad.16), kind=kOutput, calls=%fused_computation.44 | convolution fusion | flops 2488926208 | bytes 6946816 | tf_op jit(solution)/shard_map/dot_general | solution.py:35
  204.9 4.8 %convolution_convert_fusion.5 = bf16[1024,1024]{1,0:T(8,128)(2,1)S(1)} fusion(bf16[1184,1024]{1,0:T(8,128)(2,1)S(1)} %get-tuple-element.172, bf16[592,1024]{1,0:T(8,128)(2,1)} %collective-permute-done.23, bf16[592,1024]{1,0:T(8,128)(2,1)} %pad.16), kind=kOutput, calls=%fused_computation.45 | convolution fusion | flops 2488926208 | bytes 6946816 | tf_op jit(solution)/shard_map/dot_general | solution.py:35
  250.5 7.4 %shard_map.264 = (f32[592,1024]{1,0:T(8,128)S(1)}, bf16[1184,1024]{1,0:T(8,128)(2,1)S(1)}, f32[8,1024]{1,0:T(8,128)S(1)}) custom-call(bf16[1184,1024]{1,0:T(8,128)(2,1)} %copy-done.55, bf16[1184,1024]{1,0:T(8,128)(2,1)} %copy-done.56, f32[1184,1024]{1,0:T(8,128)} %get-tuple-element.127.resid_ref, bf16[1184,1024]{1,0:T(8,128)(2,1)} %copy-done.48, ...), custom_call_target="tpu_custom_call" | custom-call | flops 1048576 | bytes 262144 | tf_op jit(solution)/shard_map/pallas_call | solution.py:39
  267.0 10.0 %shard_map.265 = (bf16[1184,768]{1,0:T(8,128)(2,1)S(1)}, f32[8,768]{1,0:T(8,128)S(1)}) custom-call(bf16[1184,768]{1,0:T(8,128)(2,1)S(1)} %copy-done.7, bf16[2,4,592,592]{3,2,1,0:T(8,128)(2,1)} %get-tuple-element.134.probs_ref, bf16[1184,256]{1,0:T(8,128)(2,1)S(1)} %convolution_convert_fusion.1.grad_ref), custom_call_target="tpu_custom_call" | custom-call | flops 1048576 | bytes 262144 | tf_op jit(solution)/shard_map/pallas_call | solution.py:168
  277.0 6.0 %shard_map.266 = (bf16[1024,512]{1,0:T(8,128)(2,1)S(1)}, bf16[1024,512]{1,0:T(8,128)(2,1)S(1)}) custom-call(bf16[1184,1024]{1,0:T(8,128)(2,1)} %copy-done, bf16[1184,768]{1,0:T(8,128)(2,1)S(1)} %get-tuple-element.164.qkv_ref, bf16[1184,1024]{1,0:T(8,128)(2,1)} %copy-done.2, bf16[1184,256]{1,0:T(8,128)(2,1)S(1)} %get-tuple-element.125.mixed_ref), custom_call_target="tpu_custom_call" | custom-call | flops 1048576 | bytes 262144 | tf_op jit(solution)/shard_map/pallas_call | solution.py:39
  299.6 10.6 %shard_map.267 = (bf16[1184,768]{1,0:T(8,128)(2,1)S(1)}, f32[8,768]{1,0:T(8,128)S(1)}) custom-call(bf16[1184,768]{1,0:T(8,128)(2,1)S(1)} %copy-done.5, bf16[2,4,592,592]{3,2,1,0:T(8,128)(2,1)} %get-tuple-element.153.probs_ref, bf16[1184,256]{1,0:T(8,128)(2,1)S(1)} %convolution_convert_fusion.grad_ref), custom_call_target="tpu_custom_call" | custom-call | flops 1048576 | bytes 262144 | tf_op jit(solution)/shard_map/pallas_call | solution.py:168
  319.5 7.9 %collective-permute-start.53 = (bf16[64,2048]{1,0:T(8,128)(2,1)}, bf16[64,2048]{1,0:T(8,128)(2,1)}, u32[]{:S(2)}, u32[]{:S(2)}) collective-permute-start(bf16[64,2048]{1,0:T(8,128)(2,1)} %bitcast.279), channel_id=1, source_target_pairs={{0,0},{1,2},{2,1},{3,3},{4,4},{5,6},{6,5},{7,7},{8,8},{9,10},{10,9... | collective-permute-start | bytes 786440 | tf_op jit(solution)/shard_map/ppermute | solution.py:386
  329.0 5.4 %shard_map.268 = (bf16[1024,512]{1,0:T(8,128)(2,1)S(1)}, bf16[1024,512]{1,0:T(8,128)(2,1)S(1)}) custom-call(bf16[1184,1024]{1,0:T(8,128)(2,1)} %copy-done, bf16[1184,768]{1,0:T(8,128)(2,1)S(1)} %copy-done.29, bf16[1184,1024]{1,0:T(8,128)(2,1)} %copy-done.2, bf16[1184,256]{1,0:T(8,128)(2,1)S(1)} %copy-done.15), custom_call_target="tpu_custom_call" | custom-call | flops 1048576 | bytes 262144 | tf_op jit(solution)/shard_map/pallas_call | solution.py:39
  360.8 5.8 %collective-permute-start.52 = (bf16[64,2048]{1,0:T(8,128)(2,1)}, bf16[64,2048]{1,0:T(8,128)(2,1)S(1)}, u32[]{:S(2)}, u32[]{:S(2)}) collective-permute-start(bf16[64,2048]{1,0:T(8,128)(2,1)} %bitcast.280), channel_id=1, source_target_pairs={{0,0},{1,2},{2,1},{3,3},{4,4},{5,6},{6,5},{7,7},{8,8},{9,10},{10,9... | collective-permute-start | bytes 786440 | tf_op jit(solution)/shard_map/ppermute | solution.py:386
  372.2 5.5 %shard_map.269 = (f32[577,1024]{1,0:T(8,128)}, f32[8,1024]{1,0:T(8,128)S(1)}) custom-call(bf16[1184,1024]{1,0:T(8,128)(2,1)S(1)} %copy-done.9, bf16[592,1024]{1,0:T(8,128)(2,1)} %collective-permute-done.41.moved_ref, bf16[1184,1024]{1,0:T(8,128)(2,1)S(1)} %pad_maximum_fusion.tokens_ref, f32[592,1024]{1,0:T(8,128)} %copy-done.16, f32[8,1024]{1,0:T(8,128)S(1)} %copy-done.33), custom_call_target="tpu_custom_call" | custom-call | flops 1048576 | bytes 262144 | tf_op jit(solution)/shard_map/pallas_call | solution.py:39
  386.0 4.6 %fusion.68 = f32[1184,1024]{1,0:T(8,128)S(1)} fusion(bf16[1184,1024]{1,0:T(8,128)(2,1)} %copy-done.71, bf16[1024,1024]{1,0:T(8,128)(2,1)S(1)} %bitcast.229), kind=kOutput, calls=%fused_computation.205 | convolution fusion | flops 2483027968 | bytes 9371648 | tf_op jit(solution)/shard_map/dot_general | solution.py:35
  390.7 4.7 %collective-permute-start.50 = (f32[1,9216]{1,0:T(1,128)S(1)}, f32[1,9216]{1,0:T(1,128)S(1)}, u32[]{:S(2)}, u32[]{:S(2)}) collective-permute-start(f32[1,9216]{1,0:T(1,128)S(1)} %add.415), channel_id=1, source_target_pairs={{0,2},{1,3},{2,0},{3,1},{4,6},{5,7},{6,4},{7,5},{8,10},{9,11},{10,... | collective-permute-start | bytes 110600 | tf_op jit(solution)/shard_map/ppermute | solution.py:386
  400.1 6.9 %reduce-scatter.11.cloned.1.call-done = bf16[1,64,1024]{2,1,0:T(8,128)(2,1)} async-done(((bf16[4,64,1024]{2,1,0:T(8,128)(2,1)}), bf16[1,64,1024]{2,1,0:T(8,128)(2,1)}) %reduce-scatter.11.cloned.1.call-update) | async-done | bytes 131088 | tf_op jit(solution)/shard_map/reduce_scatter | solution.py:492
  407.9 5.4 %collective-permute-start.51 = (bf16[64,2048]{1,0:T(8,128)(2,1)S(1)}, bf16[64,2048]{1,0:T(8,128)(2,1)S(1)}, u32[]{:S(2)}, u32[]{:S(2)}) collective-permute-start(bf16[64,2048]{1,0:T(8,128)(2,1)S(1)} %pad_maximum_fusion.7), channel_id=1, source_target_pairs={{0,0},{1,2},{2,1},{3,3},{4,4},{5,6},{6,5},{7,7},{8,8},{9,10},{10,9... | collective-permute-start | bytes 786440 | tf_op jit(solution)/shard_map/ppermute | solution.py:386
  (433 shorter events, 252.0 us)
Async XLA Ops:
  7.2 85.4 %all-gather.5.cloned.1.call-start = ((), (), s32[]{:S(2)}) async-start(), calls=%async_computation.8 | async-start | bytes 1310720 | tf_op jit(solution)/shard_map/all_gather | solution.py:536
  60.3 69.7 %all-gather.7.cloned.1.call-start = ((), (), s32[]{:S(2)}) async-start(), calls=%async_computation.9 | async-start | bytes 1310720 | tf_op jit(solution)/shard_map/all_gather | solution.py:537
  61.5 25.8 %collective-permute-start.4 = (bf16[592,1024]{1,0:T(8,128)(2,1)}, bf16[592,1024]{1,0:T(8,128)(2,1)}, u32[]{:S(2)}, u32[]{:S(2)}) collective-permute-start(bf16[592,1024]{1,0:T(8,128)(2,1)} %pad.13), channel_id=1, source_target_pairs={{0,2},{1,3},{2,0},{3,1},{4,6},{5,7},{6,4},{7,5},{8,10},{9,11},{10,... | collective-permute-start | bytes 3637256 | tf_op jit(solution)/shard_map/ppermute | solution.py:386
  83.8 23.8 %collective-permute-start.14 = (bf16[4,2,64,1024]{3,2,1,0:T(8,128)(2,1)S(1)}, bf16[4,2,64,1024]{3,2,1,0:T(8,128)(2,1)}, u32[]{:S(2)}, u32[]{:S(2)}) collective-permute-start(bf16[4,2,64,1024]{3,2,1,0:T(8,128)(2,1)S(1)} %shard_map.249.refs_0_), channel_id=1, source_target_pairs={{0,1},{1,0},{2,3},{3,2},{4,5},{5,4},{6,7},{7,6},{8,9},{9,8},{10,11... | collective-permute-start | bytes 3145736 | tf_op jit(solution)/shard_map/ppermute | solution.py:386
  85.1 234.4 %reduce-scatter.5.cloned.1.call-start = ((), (), s32[]{:S(2)}) async-start(), calls=%async_computation.4 | async-start | bytes 1310720 | tf_op jit(solution)/shard_map/reduce_scatter | solution.py:492
  86.1 40.5 %collective-permute-start.18 = (bf16[4,2,64,1024]{3,2,1,0:T(8,128)(2,1)}, bf16[4,2,64,1024]{3,2,1,0:T(8,128)(2,1)}, u32[]{:S(2)}, u32[]{:S(2)}) collective-permute-start(bf16[4,2,64,1024]{3,2,1,0:T(8,128)(2,1)} %shard_map.250.refs_0_), channel_id=1, source_target_pairs={{0,4},{1,5},{2,6},{3,7},{4,0},{5,1},{6,2},{7,3},{8,12},{9,13},{10,... | collective-permute-start | bytes 3145736 | tf_op jit(solution)/shard_map/ppermute | solution.py:386
  93.9 25.4 %collective-permute-start.16 = (bf16[4,64,1024]{2,1,0:T(8,128)(2,1)S(1)}, bf16[4,64,1024]{2,1,0:T(8,128)(2,1)S(1)}, u32[]{:S(2)}, u32[]{:S(2)}) collective-permute-start(bf16[4,64,1024]{2,1,0:T(8,128)(2,1)S(1)} %get-tuple-element.109.refs_0_), channel_id=1, source_target_pairs={{0,1},{1,0},{2,3},{3,2},{4,5},{5,4},{6,7},{7,6},{8,9},{9,8},{10,11... | collective-permute-start | bytes 1572872 | tf_op jit(solution)/shard_map/ppermute | solution.py:386
  95.1 26.3 %collective-permute-start.15 = (bf16[4,64,1024]{2,1,0:T(8,128)(2,1)S(1)}, bf16[4,64,1024]{2,1,0:T(8,128)(2,1)S(1)}, u32[]{:S(2)}, u32[]{:S(2)}) collective-permute-start(bf16[4,64,1024]{2,1,0:T(8,128)(2,1)S(1)} %get-tuple-element.108.refs_0_), channel_id=1, source_target_pairs={{0,4},{1,5},{2,6},{3,7},{4,0},{5,1},{6,2},{7,3},{8,12},{9,13},{10,... | collective-permute-start | bytes 1572872 | tf_op jit(solution)/shard_map/ppermute | solution.py:386
  124.5 23.3 %collective-permute-start.19 = (bf16[4,2,64,1024]{3,2,1,0:T(8,128)(2,1)}, bf16[4,2,64,1024]{3,2,1,0:T(8,128)(2,1)}, u32[]{:S(2)}, u32[]{:S(2)}) collective-permute-start(bf16[4,2,64,1024]{3,2,1,0:T(8,128)(2,1)} %shard_map.254.refs_0_), channel_id=1, source_target_pairs={{0,4},{1,5},{2,6},{3,7},{4,0},{5,1},{6,2},{7,3},{8,12},{9,13},{10,... | collective-permute-start | bytes 3145736 | tf_op jit(solution)/shard_map/ppermute | solution.py:386
  125.7 24.2 %collective-permute-start.17 = (bf16[4,2,64,1024]{3,2,1,0:T(8,128)(2,1)}, bf16[4,2,64,1024]{3,2,1,0:T(8,128)(2,1)}, u32[]{:S(2)}, u32[]{:S(2)}) collective-permute-start(bf16[4,2,64,1024]{3,2,1,0:T(8,128)(2,1)} %shard_map.253.refs_0_), channel_id=1, source_target_pairs={{0,1},{1,0},{2,3},{3,2},{4,5},{5,4},{6,7},{7,6},{8,9},{9,8},{10,11... | collective-permute-start | bytes 3145736 | tf_op jit(solution)/shard_map/ppermute | solution.py:386
  186.3 24.6 %collective-permute-start.25 = (bf16[4,2,64,1024]{3,2,1,0:T(8,128)(2,1)S(1)}, bf16[4,2,64,1024]{3,2,1,0:T(8,128)(2,1)S(1)}, u32[]{:S(2)}, u32[]{:S(2)}) collective-permute-start(bf16[4,2,64,1024]{3,2,1,0:T(8,128)(2,1)S(1)} %shard_map.261.refs_0_), channel_id=1, source_target_pairs={{0,4},{1,5},{2,6},{3,7},{4,0},{5,1},{6,2},{7,3},{8,12},{9,13},{10,... | collective-permute-start | bytes 3145736 | tf_op jit(solution)/shard_map/ppermute | solution.py:386
  186.7 24.9 %collective-permute-start.24 = (bf16[4,2,64,1024]{3,2,1,0:T(8,128)(2,1)S(1)}, bf16[4,2,64,1024]{3,2,1,0:T(8,128)(2,1)S(1)}, u32[]{:S(2)}, u32[]{:S(2)}) collective-permute-start(bf16[4,2,64,1024]{3,2,1,0:T(8,128)(2,1)S(1)} %shard_map.260.refs_0_), channel_id=1, source_target_pairs={{0,1},{1,0},{2,3},{3,2},{4,5},{5,4},{6,7},{7,6},{8,9},{9,8},{10,11... | collective-permute-start | bytes 3145736 | tf_op jit(solution)/shard_map/ppermute | solution.py:386
  203.7 28.8 %collective-permute-start.28 = (bf16[4,2,64,1024]{3,2,0,1:T(8,128)(2,1)S(1)}, bf16[4,2,64,1024]{3,2,0,1:T(8,128)(2,1)S(1)}, u32[]{:S(2)}, u32[]{:S(2)}) collective-permute-start(bf16[4,2,64,1024]{3,2,0,1:T(8,128)(2,1)S(1)} %bitcast.246), channel_id=1, source_target_pairs={{0,4},{1,5},{2,6},{3,7},{4,0},{5,1},{6,2},{7,3},{8,12},{9,13},{10,... | collective-permute-start | bytes 3145736 | tf_op jit(solution)/shard_map/ppermute | solution.py:386
  210.0 22.8 %collective-permute-start.27 = (bf16[4,2,64,1024]{3,2,0,1:T(8,128)(2,1)S(1)}, bf16[4,2,64,1024]{3,2,0,1:T(8,128)(2,1)S(1)}, u32[]{:S(2)}, u32[]{:S(2)}) collective-permute-start(bf16[4,2,64,1024]{3,2,0,1:T(8,128)(2,1)S(1)} %bitcast.247), channel_id=1, source_target_pairs={{0,1},{1,0},{2,3},{3,2},{4,5},{5,4},{6,7},{7,6},{8,9},{9,8},{10,11... | collective-permute-start | bytes 3145736 | tf_op jit(solution)/shard_map/ppermute | solution.py:386
  227.1 21.9 %collective-permute-start.26 = (bf16[1184,1024]{1,0:T(8,128)(2,1)S(1)}, bf16[1184,1024]{1,0:T(8,128)(2,1)S(1)}, u32[]{:S(2)}, u32[]{:S(2)}) collective-permute-start(bf16[1184,1024]{1,0:T(8,128)(2,1)S(1)} %add_convert_fusion.2.low_ref), channel_id=1, source_target_pairs={{0,2},{1,3},{2,0},{3,1},{4,6},{5,7},{6,4},{7,5},{8,10},{9,11},{10,... | collective-permute-start | bytes 7274504 | tf_op jit(solution)/shard_map/ppermute | solution.py:386
  234.5 26.2 %collective-permute-start.29 = (bf16[4,64,1024]{2,1,0:T(8,128)(2,1)}, bf16[4,64,1024]{2,1,0:T(8,128)(2,1)}, u32[]{:S(2)}, u32[]{:S(2)}) collective-permute-start(bf16[4,64,1024]{2,1,0:T(8,128)(2,1)} %dynamic-slice_bitcast_fusion.3), channel_id=1, source_target_pairs={{0,4},{1,5},{2,6},{3,7},{4,0},{5,1},{6,2},{7,3},{8,12},{9,13},{10,... | collective-permute-start | bytes 1572872 | tf_op jit(solution)/shard_map/ppermute | solution.py:386
  235.6 25.1 %collective-permute-start.30 = (bf16[4,64,1024]{2,1,0:T(8,128)(2,1)}, bf16[4,64,1024]{2,1,0:T(8,128)(2,1)}, u32[]{:S(2)}, u32[]{:S(2)}) collective-permute-start(bf16[4,64,1024]{2,1,0:T(8,128)(2,1)} %dynamic-slice_bitcast_fusion.2), channel_id=1, source_target_pairs={{0,1},{1,0},{2,3},{3,2},{4,5},{5,4},{6,7},{7,6},{8,9},{9,8},{10,11... | collective-permute-start | bytes 1572872 | tf_op jit(solution)/shard_map/ppermute | solution.py:386
  241.9 41.2 %collective-permute-start.32 = (bf16[4,2,64,1024]{3,2,0,1:T(8,128)(2,1)}, bf16[4,2,64,1024]{3,2,0,1:T(8,128)(2,1)}, u32[]{:S(2)}, u32[]{:S(2)}) collective-permute-start(bf16[4,2,64,1024]{3,2,0,1:T(8,128)(2,1)} %bitcast.211), channel_id=1, source_target_pairs={{0,1},{1,0},{2,3},{3,2},{4,5},{5,4},{6,7},{7,6},{8,9},{9,8},{10,11... | collective-permute-start | bytes 3145736 | tf_op jit(solution)/shard_map/ppermute | solution.py:386
  247.9 35.1 %collective-permute-start.34 = (bf16[4,2,64,1024]{3,2,0,1:T(8,128)(2,1)}, bf16[4,2,64,1024]{3,2,0,1:T(8,128)(2,1)}, u32[]{:S(2)}, u32[]{:S(2)}) collective-permute-start(bf16[4,2,64,1024]{3,2,0,1:T(8,128)(2,1)} %bitcast.210), channel_id=1, source_target_pairs={{0,4},{1,5},{2,6},{3,7},{4,0},{5,1},{6,2},{7,3},{8,12},{9,13},{10,... | collective-permute-start | bytes 3145736 | tf_op jit(solution)/shard_map/ppermute | solution.py:386
  290.0 70.8 %reduce-scatter.7.cloned.1.call-start = ((), (), s32[]{:S(2)}) async-start(), calls=%async_computation.5 | async-start | bytes 1310720 | tf_op jit(solution)/shard_map/reduce_scatter | solution.py:492
  319.5 64.8 %reduce-scatter.9.cloned.1.call-start = ((), (), s32[]{:S(2)}) async-start(), calls=%async_computation.6 | async-start | bytes 655360 | tf_op jit(solution)/shard_map/reduce_scatter | solution.py:492
  319.5 34.1 %collective-permute-start.53 = (bf16[64,2048]{1,0:T(8,128)(2,1)}, bf16[64,2048]{1,0:T(8,128)(2,1)}, u32[]{:S(2)}, u32[]{:S(2)}) collective-permute-start(bf16[64,2048]{1,0:T(8,128)(2,1)} %bitcast.279), channel_id=1, source_target_pairs={{0,0},{1,2},{2,1},{3,3},{4,4},{5,6},{6,5},{7,7},{8,8},{9,10},{10,9... | collective-permute-start | bytes 786440 | tf_op jit(solution)/shard_map/ppermute | solution.py:386
  353.5 53.4 %reduce-scatter.11.cloned.1.call-start = ((), (), s32[]{:S(2)}) async-start(), calls=%async_computation.7 | async-start | bytes 655360 | tf_op jit(solution)/shard_map/reduce_scatter | solution.py:492
  359.5 21.7 %collective-permute-start.40 = (bf16[4,64,512]{2,1,0:T(8,128)(2,1)}, bf16[4,64,512]{2,1,0:T(8,128)(2,1)}, u32[]{:S(2)}, u32[]{:S(2)}) collective-permute-start(bf16[4,64,512]{2,1,0:T(8,128)(2,1)} %dynamic-slice_bitcast_fusion.5), channel_id=1, source_target_pairs={{0,4},{1,5},{2,6},{3,7},{4,0},{5,1},{6,2},{7,3},{8,12},{9,13},{10,... | collective-permute-start | bytes 786440 | tf_op jit(solution)/shard_map/ppermute | solution.py:386
  (112 other events, 1043.4 us)
Sparse Core Ops, SparseCore 0:
  60.5 32.0 all-gather.4
  94.7 27.4 all-gather.6
  290.1 28.3 reduce-scatter.4
  320.7 29.4 reduce-scatter.6
  353.7 18.4 reduce-scatter.8
  384.3 22.5 reduce-scatter.10

commit v4 on v3

--- a/solution.py
+++ b/solution.py
@@ -23,7 +23,7 @@
 NN = (((1,), (0,)), ((), ()))
 NT = (((1,), (1,)), ((), ()))
 TN = (((0,), (0,)), ((), ()))
-VMEM_LIMIT = 48 * 2**20
+VMEM_LIMIT = 20 * 2**20
 LITTLE = pl.CostEstimate(flops=2**20, bytes_accessed=2**18, transcendentals=0)
 
 
@@ -121,17 +121,19 @@
     )
 
 
-def attend_back(projected, probs, mixed_grad, heads):
+def attend_back(projected, probs, attn_grad, weight, heads):
     width = heads * HEAD
-
-    def kernel(qkv_ref, probs_ref, grad_ref, out_ref, sums_ref):
+    deep = attn_grad.shape[1]
+
+    def kernel(qkv_ref, probs_ref, grad_ref, weight_ref, out_ref, sums_ref, mixed_ref):
+        mixed_ref[...] = dot(grad_ref[...], weight_ref[...]).astype(BF16)
         lane = lax.broadcasted_iota(jnp.int32, (ROWS, 128), 1)
         for pair in range(heads // 2):
             at = pair * 128
             queries = qkv_ref[:, at : at + 128]
             keys = qkv_ref[:, width + at : width + at + 128]
             values = qkv_ref[:, 2 * width + at : 2 * width + at + 128]
-            grad = grad_ref[:, at : at + 128]
+            grad = mixed_ref[:, at : at + 128]
             keys_t = (keys * BF16(0.125)).T
             queries_s = queries * BF16(0.125)
             d_query, d_key, d_value = [], [], []
@@ -171,38 +173,167 @@
         in_specs=[
             pl.BlockSpec(*image(3 * width)),
             pl.BlockSpec((1, heads, ROWS, ROWS), lambda i: (i, 0, 0, 0)),
-            pl.BlockSpec(*image(width)),
+            pl.BlockSpec(*image(deep)),
+            pl.BlockSpec((deep, width), lambda i: (0, 3)),
         ],
         out_specs=[pl.BlockSpec(*image(3 * width)), pl.BlockSpec(*fixed(8, 3 * width))],
         out_shape=[
             jax.ShapeDtypeStruct((2 * ROWS, 3 * width), BF16),
             jax.ShapeDtypeStruct((8, 3 * width), F32),
         ],
+        scratch_shapes=[pltpu.VMEM((ROWS, width), BF16)],
         compiler_params=pltpu.CompilerParams(vmem_limit_bytes=VMEM_LIMIT),
         cost_estimate=LITTLE,
-    )(projected, probs, mixed_grad)
+    )(projected, probs, attn_grad, weight)
+
+
+def pieces(width):
+    unit = width // 128
+    part = -(-unit // 3) * 128
+    return [part, part, width - 2 * part]
+
+
+def joined_columns(refs):
+    return jnp.concatenate([ref[...] for ref in refs], axis=1).astype(F32)
+
+
+def rows_product(lefts, weights, block, split):
+    width = lefts[0].shape[1]
+    deep = weights[0].shape[0]
+    count = len(lefts)
+    cuts = pieces(deep)
+
+    def kernel(*refs):
+        outs = refs[2 * count :]
+        total = dot(refs[0][...], refs[count][...], NT)
+        for n in range(1, count):
+            total = total + dot(refs[n][...], refs[count + n][...], NT)
+        total = total.astype(BF16)
+
+        def put(refs_out):
+            at = 0
+            for ref, cut in zip(refs_out, cuts):
+                ref[...] = total[:, at : at + cut]
+                at += cut
+
+        if not split:
+            put(outs)
+            return
+
+        @pl.when(pl.program_id(0) == 0)
+        def _():
+            outs[0][...] = total
+
+        @pl.when(pl.program_id(0) != 0)
+        def _():
+            put(outs[1:])
+
+    if split:
+        outs = [fixed(ROWS, deep) + ((ROWS, deep), BF16)]
+        outs += [fixed(ROWS, cut) + ((ROWS, cut), BF16) for cut in cuts]
+    else:
+        outs = [image(cut) + ((2 * ROWS, cut), BF16) for cut in cuts]
+    ins = [image(width)] * count + [block] * count
+    found = call(kernel, (2,), ins, outs, *lefts, *weights)
+    return (found[0], found[1:]) if split else found
 
 
 def norm_two(tokens, low, moved, vectors):
     width = tokens.shape[1]
-
-    def kernel(tokens_ref, low_ref, moved_ref, vec_ref, resid_ref, out_ref):
-        branch = low_ref[...].astype(F32) + moved_ref[...].astype(F32)
+    count = len(low)
+
+    def kernel(tokens_ref, vec_ref, *refs):
+        resid_ref, out_ref = refs[2 * count :]
+        branch = joined_columns(refs[:count]) + joined_columns(refs[count : 2 * count])
         residual = tokens_ref[...].astype(F32) + branch + vec_ref[4:5]
         resid_ref[...] = residual
         hat, _ = row_stats(residual)
         out_ref[...] = (hat * vec_ref[2:3] + vec_ref[3:4]).astype(BF16)
 
+    ins = [image(width), fixed(8, width)]
+    ins += [image(part.shape[1]) for part in low] + [other_image(part.shape[1]) for part in moved]
+    outs = [image(width) + (tokens.shape, F32), image(width) + (tokens.shape, BF16)]
+    return call(kernel, (2,), ins, outs, tokens, vectors, *low, *moved)
+
+
+def hidden_units(normed, weight, bias):
+    deep, width = weight.shape
+    cut = 512
+
+    def kernel(rows_ref, weight_ref, bias_ref, hidden_ref, slope_ref):
+        pre = dot(rows_ref[...], weight_ref[...]) + bias_ref[0:1]
+        cdf = 0.5 * (1.0 + lax.erf(pre * (1.0 / math.sqrt(2.0))))
+        density = jnp.exp(-0.5 * pre * pre) * (1.0 / math.sqrt(2.0 * math.pi))
+        hidden_ref[...] = (pre * cdf).astype(BF16)
+        slope_ref[...] = (cdf + pre * density).astype(BF16)
+
+    out = ((ROWS, cut), lambda j, i: (i, j), (2 * ROWS, width), BF16)
     return call(
         kernel,
-        (2,),
-        [image(width), image(width), other_image(width), fixed(8, width)],
-        [image(width) + (tokens.shape, F32), image(width) + (tokens.shape, BF16)],
-        tokens,
-        low,
-        moved,
-        vectors,
+        (width // cut, 2),
+        [
+            ((ROWS, deep), lambda j, i: (i, 0)),
+            ((deep, cut), lambda j, i: (0, j)),
+            ((8, cut), lambda j, i: (0, j)),
+        ],
+        [out, out],
+        normed,
+        weight,
+        bias,
     )
+
+
+def hidden_back(down, weight, slope):
+    deep, width = weight.shape
+    cut = 1024
+
+    def kernel(rows_ref, weight_ref, slope_ref, out_ref, sums_ref):
+        grad = (dot(rows_ref[...], weight_ref[...]) * slope_ref[...].astype(F32)).astype(BF16)
+        out_ref[...] = grad
+        total = jnp.sum(grad.astype(F32), axis=0, keepdims=True)
+        total = jnp.broadcast_to(total, sums_ref.shape)
+
+        @pl.when(pl.program_id(1) == 0)
+        def _():
+            sums_ref[...] = total
+
+        @pl.when(pl.program_id(1) != 0)
+        def _():
+            sums_ref[...] += total
+
+    return call(
+        kernel,
+        (width // cut, 2),
+        [
+            ((ROWS, deep), lambda j, i: (i, 0)),
+            ((deep, cut), lambda j, i: (0, j)),
+            ((ROWS, cut), lambda j, i: (i, j)),
+        ],
+        [
+            ((ROWS, cut), lambda j, i: (i, j), (2 * ROWS, width), BF16),
+            ((8, cut), lambda j, i: (0, j), (8, width), F32),
+        ],
+        down,
+        weight,
+        slope,
+    )
+
+
+def weight_grad_kernel(rows, grad):
+    deep, width = rows.shape[1], grad.shape[1]
+    cut = 256
+
+    def kernel(rows_ref, grad_ref, out_ref):
+        out_ref[...] = dot(rows_ref[...], grad_ref[...], TN).astype(BF16)
+
+    return call(
+        kernel,
+        (deep // cut,),
+        [((2 * ROWS, cut), lambda j: (0, j)), fixed(2 * ROWS, width)],
+        [((cut, width), lambda j: (j, 0), (deep, width), BF16)],
+        rows,
+        grad,
+    )[0]
 
 
 def weight_grad(rows, grad):
@@ -235,10 +366,12 @@
 
 
 def norm_two_back(low, moved, residual, down, vectors):
-    width = low.shape[1]
-
-    def kernel(low_ref, moved_ref, resid_ref, down_ref, vec_ref, own_ref, out_ref, sums_ref):
-        back = low_ref[...].astype(F32) + moved_ref[...].astype(F32)
+    width = residual.shape[1]
+    count = len(low)
+
+    def kernel(resid_ref, down_ref, vec_ref, *refs):
+        own_ref, out_ref, sums_ref = refs[2 * count :]
+        back = joined_columns(refs[:count]) + joined_columns(refs[count : 2 * count])
         upstream = down_ref[...].astype(F32)
         hat, inv = row_stats(resid_ref[...])
         grad = upstream + norm_back(back, hat, inv, vec_ref[2:3])
@@ -250,28 +383,23 @@
             for n, part in enumerate((back * hat, back, grad, upstream)):
                 sums_ref[n : n + 1] = jnp.sum(part, axis=0, keepdims=True)
 
-    return call(
-        kernel,
-        (2,),
-        [image(width), other_image(width), image(width), image(width), fixed(8, width)],
-        [
-            fixed(ROWS, width) + ((ROWS, width), F32),
-            image(width) + ((2 * ROWS, width), BF16),
-            fixed(8, width) + ((8, width), F32),
-        ],
-        low,
-        moved,
-        residual,
-        down,
-        vectors,
-    )
+    ins = [image(width), image(width), fixed(8, width)]
+    ins += [image(part.shape[1]) for part in low] + [other_image(part.shape[1]) for part in moved]
+    outs = [
+        fixed(ROWS, width) + ((ROWS, width), F32),
+        image(width) + ((2 * ROWS, width), BF16),
+        fixed(8, width) + ((8, width), F32),
+    ]
+    return call(kernel, (2,), ins, outs, residual, down, vectors, *low, *moved)
 
 
 def norm_one_back(low, moved, tokens, grad, vectors):
     width = low.shape[1]
-
-    def kernel(low_ref, moved_ref, tokens_ref, grad_ref, vec_ref, out_ref, sums_ref):
-        back = low_ref[...].astype(F32) + moved_ref[...].astype(F32)
+    count = len(moved)
+
+    def kernel(low_ref, tokens_ref, grad_ref, vec_ref, *refs):
+        out_ref, sums_ref = refs[count:]
+        back = low_ref[...].astype(F32) + joined_columns(refs[:count])
         hat, inv = row_stats(tokens_ref[...].astype(F32))
         total = grad_ref[...] + norm_back(back, hat, inv, vec_ref[0:1])
         out_ref[...] = total[:SEQ]
@@ -279,61 +407,142 @@
             sums_ref[n : n + 1] = jnp.sum(part, axis=0, keepdims=True)
 
     own_rows = fixed(ROWS, width)
-    return call(
-        kernel,
-        (1,),
-        [own_rows, own_rows, own_rows, own_rows, fixed(8, width)],
-        [
-            fixed(SEQ, width) + ((SEQ, width), F32),
-            fixed(8, width) + ((8, width), F32),
-        ],
-        low,
-        moved,
-        tokens,
-        grad,
-        vectors,
-    )
+    ins = [own_rows, own_rows, own_rows, fixed(8, width)]
+    ins += [fixed(ROWS, part.shape[1]) for part in moved]
+    outs = [fixed(SEQ, width) + ((SEQ, width), F32), fixed(8, width) + ((8, width), F32)]
+    return call(kernel, (1,), ins, outs, low, tokens, grad, vectors, *moved)
 
 
 def layer_output(residual, low, moved, vectors):
     width = low.shape[1]
 
-    def kernel(resid_ref, low_ref, moved_ref, vec_ref, out_ref):
-        branch = low_ref[...].astype(F32) + moved_ref[...].astype(F32)
-        out_ref[...] = (resid_ref[...] + branch + vec_ref[5:6]).astype(BF16)[:SEQ]
+    def kernel(resid_ref, low_ref, vec_ref, *refs):
+        branch = low_ref[...].astype(F32) + joined_columns(refs[:-1])
+        refs[-1][...] = (resid_ref[...] + branch + vec_ref[5:6]).astype(BF16)[:SEQ]
 
     own_rows = fixed(ROWS, width)
     out = fixed(SEQ, width) + ((SEQ, width), BF16)
-    ins = [own_rows, own_rows, own_rows, fixed(8, width)]
-    return call(kernel, (1,), ins, [out], residual, low, moved, vectors)[0]
-
-
-def place(parts, spots, shape, block):
+    ins = [own_rows, own_rows, fixed(8, width)] + [fixed(ROWS, p.shape[1]) for p in moved]
+    return call(kernel, (1,), ins, [out], residual, low, vectors, *moved)[0]
+
+
+def place(parts, spots, shape, dim):
+    part = parts[0].shape
+    block = shape[:dim] + (1,) + shape[dim + 1 :]
+    before, later = (0,) * dim, (0,) * (len(shape) - dim - 1)
+
     def kernel(spot_ref, *refs):
-        out_ref, sems = refs[-2], refs[-1]
-        copies = []
+        out_ref = refs[-1]
         for n in range(len(parts)):
-            copies.append(
-                pltpu.make_async_copy(refs[n], block(out_ref, spot_ref[n]), sems.at[n])
-            )
-        for copy in copies:
-            copy.start()
-        for copy in copies:
-            copy.wait()
+
+            @pl.when(pl.program_id(0) == n)
+            def _():
+                out_ref[...] = refs[n][...].reshape(block)
 
     return pl.pallas_call(
         kernel,
         grid_spec=pltpu.PrefetchScalarGridSpec(
             num_scalar_prefetch=1,
-            grid=(1,),
-            in_specs=[pl.BlockSpec(memory_space=pl.ANY)] * len(parts),
-            out_specs=pl.BlockSpec(memory_space=pl.ANY),
-            scratch_shapes=[pltpu.SemaphoreType.DMA((len(parts),))],
+            grid=(len(parts),),
+            in_specs=[pl.BlockSpec(part, lambda i, spot: (0,) * len(part))] * len(parts),
+            out_specs=pl.BlockSpec(block, lambda i, spot: before + (spot[i],) + later),
         ),
         out_shape=jax.ShapeDtypeStruct(shape, parts[0].dtype),
-        compiler_params=pltpu.CompilerParams(vmem_limit_bytes=2**20),
+        compiler_params=pltpu.CompilerParams(vmem_limit_bytes=VMEM_LIMIT),
         cost_estimate=LITTLE,
     )(spots, *parts)
+
+
+def at_index(parts, index):
+    found = parts[0]
+    for n in range(1, len(parts)):
+        found = jnp.where(index == n, parts[n], found)
+    return found
+
+
+def prefetched(kernel, spots, steps, ins, outs, arrays):
+    return pl.pallas_call(
+        kernel,
+        grid_spec=pltpu.PrefetchScalarGridSpec(
+            num_scalar_prefetch=1,
+            grid=(steps,),
+            in_specs=[pl.BlockSpec(block, at) for block, at in ins],
+            out_specs=[pl.BlockSpec(block, at) for block, at, _ in outs],
+        ),
+        out_shape=[jax.ShapeDtypeStruct(shape, BF16) for _, _, shape in outs],
+        compiler_params=pltpu.CompilerParams(vmem_limit_bytes=VMEM_LIMIT),
+        cost_estimate=LITTLE,
+    )(spots, *arrays)
+
+
+def parts_to_give(first, second, spots, wide, columns):
+    n_z, n_x, _, depth, _ = first.shape
+    at_a, at_b = columns
+
+    def kernel(spot_ref, *refs):
+        half = len(refs) // 2
+        for n in range(half):
+            refs[half + n][...] = refs[n][...].reshape(refs[half + n].shape)
+
+    ins = [((1, n_x, 1, depth, wide), lambda i, s: (i, 0, s[1], 0, at_a))]
+    outs = [((1, n_x, depth, wide), lambda i, s: (i, 0, 0, 0), (n_z, n_x, depth, wide))]
+    for k in range(1, n_x):
+        ins.append(((1, 1, 2, depth, wide), lambda i, s, k=k: (i, s[2 + k], 0, 0, at_b)))
+        outs.append(((1, 2, depth, wide), lambda i, s: (i, 0, 0, 0), (n_z, 2, depth, wide)))
+    arrays = [first] + [second] * (n_x - 1)
+    found = prefetched(kernel, spots, n_z, ins, outs, arrays)
+    return found[0], found[1:]
+
+
+def sums_to_give(first, first_moved, second, second_moved, spots, wide, columns):
+    n_z, n_x, _, depth, _ = first.shape
+    at_a, at_b = columns
+
+    def kernel(spot_ref, first_ref, moved_ref, second_ref, *refs):
+        moved_refs, outs = refs[: n_x - 1], refs[n_x - 1 :]
+        sums = []
+        for x in range(n_x):
+            total = first_ref[0, x, 0].astype(F32) + moved_ref[0, x].astype(F32)
+            sums.append(total)
+        for k in range(n_x):
+            outs[k][0] = at_index(sums, spot_ref[2 + k]).astype(BF16)
+        sums = []
+        for y in range(2):
+            total = second_ref[0, 0, y].astype(F32)
+            for ref in moved_refs:
+                total = total + ref[0, y].astype(F32)
+            sums.append(total)
+        for k in range(2):
+            outs[n_x + k][0] = at_index(sums, spot_ref[k]).astype(BF16)
+
+    ins = [
+        ((1, n_x, 1, depth, wide), lambda i, s: (i, 0, s[0], 0, at_a)),
+        ((1, n_x, depth, wide), lambda i, s: (i, 0, 0, 0)),
+        ((1, 1, 2, depth, wide), lambda i, s: (i, s[2], 0, 0, at_b)),
+    ] + [((1, 2, depth, wide), lambda i, s: (i, 0, 0, 0))] * (n_x - 1)
+    out = ((1, depth, wide), lambda i, s: (i, 0, 0), (n_z, depth, wide))
+    arrays = [first, first_moved, second, *second_moved]
+    found = prefetched(kernel, spots, n_z, ins, [out] * (n_x + 2), arrays)
+    return found[0], found[1:n_x], found[n_x], found[n_x + 1]
+
+
+def line_sums(first, first_moved, second, second_moved):
+    n_z, depth, wide = first.shape
+
+    def kernel(first_ref, *refs):
+        count = len(first_moved)
+        second_ref, moved_ref, out_ref = refs[count:]
+        total = first_ref[0].astype(F32)
+        for ref in refs[:count]:
+            total = total + ref[0].astype(F32)
+        out_ref[0, :, :wide] = total.astype(BF16)
+        total = second_ref[0].astype(F32) + moved_ref[0].astype(F32)
+        out_ref[0, :, wide:] = total.astype(BF16)
+
+    block = ((1, depth, wide), lambda i: (i, 0, 0))
+    out = ((1, depth, 2 * wide), lambda i: (i, 0, 0), (n_z, depth, 2 * wide), BF16)
+    arrays = [first, *first_moved, second, second_moved]
+    return call(kernel, (n_z,), [block] * len(arrays), [out], *arrays)[0]
 
 
 def pack(qkv, proj, quarter):
@@ -430,11 +639,11 @@
             count = sizes[axis]
             return (where_am_i[axis] + jnp.arange(count, dtype=jnp.int32)) % count
 
-        def from_all(value, axis, shape, block, earlier=()):
+        def from_all(value, axis, shape, dim, earlier=()):
             moved = [send(value, shift(axis, -k)) for k in range(1, sizes[axis])]
             if earlier:
                 moved = [after(part, *earlier) for part in moved]
-            return place([value] + moved, spots(axis), shape, block)
+            return place([value] + moved, spots(axis), shape, dim)
 
         def crossed(shard):
             return send(shard, transpose)
@@ -448,75 +657,56 @@
 
         def step_one(first, second, *earlier):
             at = (n_z, n_x, depth, first.shape[2])
-            first = from_all(first, "x", at, lambda ref, n: ref.at[:, n], earlier)
+            first = from_all(first, "x", at, 1, earlier)
             at = (n_z, 2, depth, second.shape[2])
-            second = from_all(second, "y", at, lambda ref, n: ref.at[:, n], earlier)
+            second = from_all(second, "y", at, 1, earlier)
             return together(first, second)
 
         def step_two(first, second, *earlier):
             wide = first.shape[3]
             at = (n_z, n_x, 2, depth, wide)
-            first = from_all(first, "y", at, lambda ref, n: ref.at[:, :, n], earlier)
-            second = from_all(second, "x", at, lambda ref, n: ref.at[:, n], earlier)
+            first = from_all(first, "y", at, 2, earlier)
+            second = from_all(second, "x", at, 1, earlier)
             return first.reshape(width, wide), second.reshape(width, wide)
 
         def pick(array, axis, index):
             return lax.dynamic_index_in_dim(array, index, axis, keepdims=False)
 
-        def give(array, axis, dim):
-            count, here = sizes[axis], where_am_i[axis]
-            moved = [
-                send(pick(array, dim, (here + k) % count), shift(axis, k))
-                for k in range(1, count)
-            ]
-            return moved, pick(array, dim, here)
-
-        def summed(given, *earlier):
-            moved, own_part = given
-            total = own_part.astype(F32)
-            for part in moved:
-                total = total + (after(part, *earlier) if earlier else part).astype(F32)
-            return total.astype(BF16)
-
-        def scatter_one(first, second):
+        grad_spots = jnp.concatenate([spots("y"), spots("x")])
+
+        def scatter_one(first, second, columns=(0, 0)):
             at = (n_z, n_x, 2, depth, first.shape[1])
-            return give(first.reshape(at), "y", 2), give(second.reshape(at), "x", 1)
-
-        def scatter_two(first, second):
-            return give(first, "x", 1), give(second, "y", 1)
-
-        def gathered(parts):
-            return jnp.concatenate(parts, axis=2)
+            first, second = first.reshape(at), second.reshape(at)
+            parts = first.shape[4] // (max(columns) + 1)
+            to_y, to_x = parts_to_give(first, second, grad_spots, parts, columns)
+            from_y = send(to_y, shift("y", 1))
+            from_x = [send(part, shift("x", k + 1)) for k, part in enumerate(to_x)]
+            return (first, from_y, second, from_x, parts, columns), (to_y, *to_x)
+
+        def scatter_two(given, *earlier):
+            first, from_y, second, from_x, parts, columns = given
+            if earlier:
+                from_y, from_x = after(from_y, *earlier), [after(v, *earlier) for v in from_x]
+            own_a, to_x, own_b, to_y = sums_to_give(
+                first, from_y, second, from_x, grad_spots, parts, columns
+            )
+            from_x = [send(part, shift("x", k + 1)) for k, part in enumerate(to_x)]
+            return own_a, from_x, own_b, send(to_y, shift("y", 1))
+
+        def lines(given, *earlier):
+            own_a, from_x, own_b, from_y = given
+            from_y, from_x = after(from_y, *earlier), [after(v, *earlier) for v in from_x]
+            return line_sums(own_a, from_x, own_b, from_y)
 
         def scatter_three(both):
             return lax.psum_scatter(both, "z", scatter_dimension=0, tiled=False)
 
         shard_one = crossed(shards[0])
-        shard_two = crossed(after(shards[1], shard_one))
-        shard_three = crossed(after(shards[2], shard_one))
-        shard_one = after(shard_one, shard_two, shard_three)
         wide = shards[0].shape[1] // 2
         around = [shard_one] + [send(shard_one, shift("z", -k)) for k in range(1, n_z)]
-        line_one = [
-            place(
-                [part[:, cut] for part in around],
-                spots("z"),
-                (n_z, depth, wide),
-                lambda ref, n: ref.at[n],
-            )
-            for cut in (slice(0, wide), slice(wide, 2 * wide))
-        ]
-        line_one = together(*line_one)
-
-        def both_images(value):
-            value = jnp.pad(value, ((0, ROWS - SEQ), (0, 0)))
-            return jnp.concatenate([value, swap(value)])
-
-        inputs = both_images(after(tokens, around[1]))
-        down = both_images(after(cotangent, around[1]))
 
         small = jnp.concatenate(
-            [after(ln1_gain, around[1]), ln1_bias, ln2_gain, ln2_bias, proj_bias, fc2_bias]
+            [after(ln1_gain, shard_one), ln1_bias, ln2_gain, ln2_bias, proj_bias, fc2_bias]
             + [qv_bias.reshape(-1), fc1_bias.reshape(-1)]
         )[None]
 
@@ -531,10 +721,31 @@
 
         for axis in ("c", "y", "x"):
             small = spread(small, axis)
+        line_one = together(
+            *[
+                place(
+                    [after(part, small)[:, cut] for part in around],
+                    spots("z"),
+                    (n_z, depth, wide),
+                    0,
+                )
+                for cut in (slice(0, wide), slice(wide, 2 * wide))
+            ]
+        )
+        shard_two = crossed(after(shards[1], around[1]))
+        shard_three = crossed(after(shards[2], around[1]))
+
         small = spread(after(small, *line_one), "z")
         square_one = step_one(*line_one, small)
-        line_two = lax.all_gather(after(shard_two, small), "z", axis=0)
-        line_three = lax.all_gather(after(shard_three, small), "z", axis=0)
+
+        def both_images(value):
+            value = jnp.pad(value, ((0, ROWS - SEQ), (0, 0)))
+            return jnp.concatenate([value, swap(value)])
+
+        inputs = both_images(after(tokens, *square_one))
+        down = both_images(after(cotangent, *square_one))
+        line_two = lax.all_gather(shard_two, "z", axis=0)
+        line_three = lax.all_gather(after(shard_three, *line_one), "z", axis=0)
         share = ln1_gain.shape[0]
         small = small.reshape(n_z, n_x, 2, 2, -1)
         small = small.transpose(0, 1, 3, 2, 4)
@@ -551,7 +762,7 @@
 
         normed_one = norm_one(inputs, vectors)
 
-        half_two = halves(line_two, normed_one)
+        half_two = halves(line_two, normed_one, down)
         attn_w = step_two(*square_one, *half_two)
         projected, probs, mixed = [None] * 2, [None] * 2, [None] * 2
 
@@ -566,84 +777,84 @@
         def back_product(lefts, weights):
             return (dot(lefts[0], weights[0], NT) + dot(lefts[1], weights[1], NT)).astype(BF16)
 
+        def eight(row):
+            return jnp.broadcast_to(row.reshape(1, -1), (8, row.size))
+
         attend_half(0, normed_one)
-        square_two = step_one(*half_two, mixed[0])
+        fc1_half = after(fc1_half, mixed[0])
+        half_three = halves(line_three, mixed[0], fc1_half)
+        square_two = step_one(*half_two, *half_three)
         attend_half(1, after(normed_one, *square_two))
-        half_three = halves(line_three, mixed[1])
-        fc1_w = step_two(*square_two, *half_three)
-        proj_ab = [w[:, n_qkv:] for w in attn_w]
-        low = back_product([after(m, *fc1_w) for m in mixed], proj_ab)
-        residual, normed_two = norm_two(inputs, low, swap(low), vectors)
-        square_three = step_one(*half_three, normed_two)
-
+        square_three = step_one(*half_three, mixed[1])
+        block = ((width, quarter), lambda i: (0, 3))
+        low = rows_product(mixed, attn_w, block, False)
+        moved = [swap(part) for part in low]
+        residual, normed_two = norm_two(inputs, low, moved, vectors)
+        fc1_w = step_two(*square_two, normed_two)
         hidden, slope = [], []
-        rows_two = after(normed_two, *square_three)
         for colour, weight in enumerate(fc1_w):
             bias = fc1_half[colour * hidden_half : (colour + 1) * hidden_half]
-            pre = dot(rows_two, weight) + bias
+            pre = dot(after(normed_two, *fc1_w), weight) + bias
             cdf = 0.5 * (1.0 + lax.erf(pre * (1.0 / math.sqrt(2.0))))
             density = jnp.exp(-0.5 * pre * pre) * (1.0 / math.sqrt(2.0 * math.pi))
             hidden.append((pre * cdf).astype(BF16))
             slope.append((cdf + pre * density).astype(BF16))
 
-        grad_fc2 = [weight_grad(down, h) for h in hidden]
-        fc2_one = scatter_one(*grad_fc2)
-        fc2_w = step_two(*square_three, *grad_fc2)
+        grad_fc2 = [weight_grad_kernel(down, h) for h in hidden]
+        fc2_one, fc2_given = scatter_one(*grad_fc2)
+        fc2_w = step_two(*square_three, *fc2_given)
         down_late = after(down, *fc2_w)
-        hidden_grad = [
-            (dot(down_late, w) * s.astype(F32)).astype(BF16) for w, s in zip(fc2_w, slope)
-        ]
-        unit_sums = [jnp.sum(g.astype(F32), axis=0) for g in hidden_grad]
-        low = back_product(hidden_grad, fc1_w)
-        moved = swap(low)
-        fc2_sums = [summed(given, low) for given in fc2_one]
-        fc2_two = scatter_two(*fc2_sums)
-        normed_late = after(normed_two, *fc2_sums)
+        hidden_grad, unit_sums = [], []
+        for weight, unit_slope in zip(fc2_w, slope):
+            grad, total = hidden_back(down_late, weight, unit_slope)
+            hidden_grad.append(grad)
+            unit_sums.append(total[0])
+        low = rows_product(hidden_grad, fc1_w, fixed(width, hidden_half), False)
+        moved = [swap(part) for part in low]
+        fc2_two = scatter_two(fc2_one, low[0])
+        normed_late = after(normed_two, fc2_two[0])
         grad_fc1 = [weight_grad(normed_late, g) for g in hidden_grad]
-        fc1_one = scatter_one(*grad_fc1)
-        resid_grad, attn_grad, sums_two = norm_two_back(
-            low, after(moved, *grad_fc1), residual, down, vectors
+        fc1_one, fc1_given = scatter_one(*grad_fc1)
+        moved = [after(part, *fc1_given) for part in moved]
+        resid_grad, attn_grad, sums_two = norm_two_back(low, moved, residual, down, vectors)
+
+        fc2_lines = lines(fc2_two, attn_grad)
+        scat_fc2 = scatter_three(fc2_lines)
+        back_a, sums_a = attend_back(
+            after(projected[0], fc2_lines), probs[0], attn_grad, attn_w[0], heads
         )
-
-        fc2_lines = gathered([summed(given, attn_grad) for given in fc2_two])
-        scat_fc2 = scatter_three(fc2_lines)
-        attn_late = after(attn_grad, fc2_lines)
-        mixed_grad = [dot(attn_late, w).astype(BF16) for w in proj_ab]
-        back_a, sums_a = attend_back(projected[0], probs[0], mixed_grad[0], heads)
         grads_a = attention_weight_grad(normed_one, back_a, attn_grad, mixed[0])
-        a_one = scatter_one(*grads_a)
-        fc1_sums = [summed(given, *grads_a) for given in fc1_one]
-        fc1_two = scatter_two(*fc1_sums)
+        a_one, a_given = scatter_one(*grads_a)
+        fc1_two = scatter_two(fc1_one, *a_given)
+        a_two = scatter_two(a_one, fc1_two[0])
         back_b, sums_b = attend_back(
-            after(projected[1], *fc1_sums), probs[1], mixed_grad[1], heads
+            after(projected[1], fc1_two[0], a_two[0]), probs[1], attn_grad, attn_w[1], heads
         )
-        fc1_lines = gathered([summed(given, back_b) for given in fc1_two])
+        fc1_lines = lines(fc1_two, back_b)
         scat_fc1 = scatter_three(fc1_lines)
-        a_sums = [summed(given, fc1_lines) for given in a_one]
-        a_two = scatter_two(*a_sums)
+        a_lines = lines(a_two, fc1_lines)
         grads_b = attention_weight_grad(
-            after(normed_one, *a_sums, scat_fc2), back_b, attn_grad, mixed[1]
+            after(normed_one, a_lines, scat_fc2), back_b, attn_grad, mixed[1]
         )
-        b_one = scatter_one(*grads_b)
-        a_lines = gathered([summed(given, *grads_b) for given in a_two])
-        scat_a = scatter_three(a_lines)
-        qkv_ab = [w[:, :n_qkv] for w in attn_w]
-        low = back_product((after(back_a, a_lines), back_b), qkv_ab)
-        b_sums = [summed(given, low) for given in b_one]
-        b_two = scatter_two(*b_sums)
-        moved = after(swap(low[ROWS:]), *b_sums, scat_fc1)
-        grad_tokens, sums_one = norm_one_back(low, moved, inputs, resid_grad, vectors)
-        b_lines = gathered([summed(given, grad_tokens) for given in b_two])
-        scat_b = scatter_three(b_lines)
-        scat_attn = jnp.concatenate([scat_a, scat_b], axis=1)
+        b_one, b_given = scatter_one(*grads_b)
+        block = ((width, n_qkv), lambda i: (0, 0))
+        low_own, low_other = rows_product((after(back_a, *b_given), back_b), attn_w, block, True)
+        b_two = scatter_two(b_one, low_own)
+        b_lines = lines(b_two, scat_fc1)
+        attn_lines = jnp.concatenate([a_lines, b_lines], axis=2)
+        scat_attn = scatter_three(attn_lines)
+        moved = [after(swap(part), attn_lines) for part in low_other]
+        grad_tokens, sums_one = norm_one_back(low_own, moved, inputs, resid_grad, vectors)
         scat_fc1, scat_fc2, scat_attn = [
             send(part, transpose) for part in (scat_fc1, scat_fc2, scat_attn)
         ]
         scat_attn = scat_attn.astype(F32)
 
-        hidden_late = [after(h, b_lines, scat_a) for h in hidden]
-        branch_two = back_product(hidden_late, fc2_w)
-        output = layer_output(residual, branch_two, swap(branch_two[ROWS:]), vectors)
+        hidden_late = [after(h, grad_tokens) for h in hidden]
+        block = fixed(width, hidden_half)
+        low_own, low_other = rows_product(hidden_late, fc2_w, block, True)
+        moved = [swap(part) for part in low_other]
+        output = layer_output(residual, low_own, moved, vectors)
 
         six = [sums_one[0], sums_one[1]] + [sums_two[n] for n in range(4)]
         grad_qv = [sums_a[0], sums_b[0]]

time: 432 us -> 404 us (0.935)
  matrix products: 69.7 us -> 19.6 us
  Pallas kernels: 92.5 us -> 121 us
  other arithmetic: 29.9 us -> 10.5 us
  local copies, waits for them, and re-layouts: 66.6 us -> 81.4 us
  waiting for transfers between devices: 72.7 us -> 60.5 us
  starting transfers between devices: 79.7 us -> 90.7 us
    dot_general x20 -> x6, matrix products: 69.7 us -> 19.6 us  [dot(): return lax.dot_general(left, right, dims, preferred_element_type=F32)]
    unnamed x165 -> x175, local copies, waits for them, and re-layouts: 21.8 us -> 53.6 us
    pallas_call x9 -> x21, Pallas kernels: 51.2 us -> 74.1 us  [call(): pl.pallas_call(kernel, grid=grid, in_specs=[pl.BlockSpec(block, at) for b...]
    convert_element_type x16 -> x0, other arithmetic: 16.3 us -> none  [summed(): return total.astype(BF16)]
    dynamic_slice x20 -> x4, local copies, waits for them, and re-layouts: 15.7 us -> 1.37 us  [pick(): return lax.dynamic_index_in_dim(array, index, axis, keepdims=False)]
    ppermute x54 -> x62, starting transfers between devices: 79.2 us -> 90.5 us  [send(): return lax.ppermute(value, ALL, perm)]
    pallas_call x0 -> x8, Pallas kernels: none -> 9.04 us  [prefetched(): pl.pallas_call(kernel, grid_spec=pltpu.PrefetchScalarGridSpec(num_scalar_...]
    reduce_scatter x4 -> x3, waiting for transfers between devices: 6.91 us -> 0.04 us  [scatter_three(): return lax.psum_scatter(both, 'z', scatter_dimension=0, tiled=False)]
  transfers between devices with their start and end apart: 60 -> 67, of which waited for: 25 -> 21; matrix products, arithmetic and copies ran while one was open for 31% -> 13% of each run, Pallas kernels for 21% -> 29%
where the time goes in v4:
time: 404 us; the launch traced here: 399 us
  Pallas kernels  121 us (30%)
  starting transfers between devices  90.7 us (22%)
  local copies, waits for them, and re-layouts  81.4 us (20%)
  waiting for transfers between devices  60.5 us (15%)
  matrix products  19.6 us (5%)
  between operations  15.6 us (4%)
  other arithmetic  10.5 us (3%)
    ppermute x62, starting transfers between devices, send(): return lax.ppermute(value, ALL, perm)  90.5 us
    pallas_call x21, Pallas kernels, call(): pl.pallas_call(kernel, grid=grid, in_specs=[pl.BlockSpec(block, at) for b...  74.1 us
    ppermute x62, waiting for transfers between devices, send(): return lax.ppermute(value, ALL, perm)  60.4 us
    unnamed x175, local copies, waits for them, and re-layouts  53.6 us
    dot_general x6, matrix products, dot(): return lax.dot_general(left, right, dims, preferred_element_type=F32)  19.6 us
    pallas_call x2, Pallas kernels, attend_back(): pl.pallas_call(kernel, grid=(2,), in_specs=[pl.BlockSpec(*image(3 * width...  19.4 us
    pallas_call x14, Pallas kernels, place(): pl.pallas_call(kernel, grid_spec=pltpu.PrefetchScalarGridSpec(num_scalar_...  18.1 us
    pallas_call x8, Pallas kernels, prefetched(): pl.pallas_call(kernel, grid_spec=pltpu.PrefetchScalarGridSpec(num_scalar_...  9.04 us
  transfers between devices with their start and end apart: 67, of which 21 were waited for; matrix products, arithmetic and copies ran while one was open for 13% of the time, Pallas kernels for 29%

profile of v4, /device:TPU:1, one launch (start us, length us, event | category | flops | bytes accessed | tf_op | source)
XLA Modules:
  0.0 398.9 jit_solution(9240000732656601821)
XLA Ops:
  9.0 4.5 %collective-permute-start = (bf16[64,2048]{1,0:T(8,128)(2,1)S(1)}, bf16[64,2048]{1,0:T(8,128)(2,1)S(1)}, u32[]{:S(2)}, u32[]{:S(2)}) collective-permute-start(bf16[64,2048]{1,0:T(8,128)(2,1)S(1)} %shard_map.245), channel_id=1, source_target_pairs={{0,0},{1,2},{2,1},{3,3},{4,4},{5,6},{6,5},{7,7},{8,8},{9,10},{10,9... | collective-permute-start | bytes 786440 | tf_op jit(solution)/shard_map/ppermute | solution.py:595
  17.6 4.1 %concatenate.196 = bf16[384]{0:T(512)(128)(2,1)S(1)} concatenate(bf16[32]{0:T(256)(128)(2,1)} %param.15, bf16[32]{0:T(256)(128)(2,1)} %param.16, bf16[32]{0:T(256)(128)(2,1)} %param.21, bf16[32]{0:T(256)(128)(2,1)} %param.22, bf16[32]{0:T(256)(128)(2,1)} %param.20, bf16[32]{0:T(256)(128)(2,1)} %param.26, bf16[64]{0:T(256)(128)(2,1)S(1)} %reshape.528, bf16[128]{0:T(256)(128)(2,1)S(1)} %reshape.529), dimensions={0} | concatenate | bytes 1536 | tf_op jit(solution)/shard_map/concatenate | solution.py:708
  31.3 5.7 %collective-permute-done.6 = bf16[64,2048]{1,0:T(8,128)(2,1)S(1)} collective-permute-done((bf16[64,2048]{1,0:T(8,128)(2,1)S(1)}, bf16[64,2048]{1,0:T(8,128)(2,1)S(1)}, u32[]{:S(2)}, u32[]{:S(2)}) %collective-permute-start.6) | collective-permute-done | bytes 262176 | tf_op jit(solution)/shard_map/ppermute | solution.py:595
  37.0 10.2 %collective-permute-done.5 = bf16[64,2048]{1,0:T(8,128)(2,1)S(1)} collective-permute-done((bf16[64,2048]{1,0:T(8,128)(2,1)S(1)}, bf16[64,2048]{1,0:T(8,128)(2,1)S(1)}, u32[]{:S(2)}, u32[]{:S(2)}) %collective-permute-start.5) | collective-permute-done | bytes 262176 | tf_op jit(solution)/shard_map/ppermute | solution.py:595
  47.2 4.8 %collective-permute-start.13 = (bf16[64,2048]{1,0:T(8,128)(2,1)}, bf16[64,2048]{1,0:T(8,128)(2,1)S(1)}, u32[]{:S(2)}, u32[]{:S(2)}) collective-permute-start(bf16[64,2048]{1,0:T(8,128)(2,1)} %param.23), channel_id=1, source_target_pairs={{0,0},{1,2},{2,1},{3,3},{4,4},{5,6},{6,5},{7,7},{8,8},{9,10},{10,9... | collective-permute-start | bytes 786440 | tf_op jit(solution)/shard_map/ppermute | solution.py:595
  102.3 8.0 %collective-permute-done.12.refs_1_ = bf16[4,2,64,1024]{3,2,1,0:T(8,128)(2,1)} collective-permute-done((bf16[4,2,64,1024]{3,2,1,0:T(8,128)(2,1)}, bf16[4,2,64,1024]{3,2,1,0:T(8,128)(2,1)}, u32[]{:S(2)}, u32[]{:S(2)}) %collective-permute-start.12) | collective-permute-done | bytes 1048608 | tf_op jit(solution)/shard_map/ppermute | solution.py:595
  116.2 6.3 %shard_map.252 = (bf16[1184,256]{1,0:T(8,128)(2,1)S(1)}, bf16[2,4,592,592]{3,2,1,0:T(8,128)(2,1)S(1)}) custom-call(bf16[1184,768]{1,0:T(8,128)(2,1)S(1)} %fusion.10.qkv_ref), custom_call_target="tpu_custom_call" | custom-call | flops 1048576 | bytes 262144 | tf_op jit(solution)/shard_map/pallas_call | solution.py:39
  140.6 6.4 %shard_map.256 = (bf16[1184,256]{1,0:T(8,128)(2,1)S(1)}, bf16[2,4,592,592]{3,2,1,0:T(8,128)(2,1)S(1)}) custom-call(bf16[1184,768]{1,0:T(8,128)(2,1)S(1)} %fusion.11.qkv_ref), custom_call_target="tpu_custom_call" | custom-call | flops 1048576 | bytes 262144 | tf_op jit(solution)/shard_map/pallas_call | solution.py:39
  165.8 4.6 %fusion.4 = (bf16[1184,1024]{1,0:T(8,128)(2,1)S(1)}, bf16[1184,1024]{1,0:T(8,128)(2,1)S(1)}) fusion(f32[1024]{0:T(1024)S(1)} %get-tuple-element.315, bf16[1184,1024]{1,0:T(8,128)(2,1)S(1)} %get-tuple-element.200, bf16[1024,1024]{1,0:T(8,128)(2,1)S(1)} %bitcast.113), kind=kOutput, calls=%fused_computation.6 | convolution fusion | flops 2497576960 | bytes 9375744 | tf_op jit(solution)/shard_map/dot_general | solution.py:35
  170.4 4.6 %fusion.9 = (bf16[1184,1024]{1,0:T(8,128)(2,1)S(1)}, bf16[1184,1024]{1,0:T(8,128)(2,1)S(1)}) fusion(f32[1024]{0:T(1024)S(1)} %get-tuple-element.314, bf16[1184,1024]{1,0:T(8,128)(2,1)S(1)} %get-tuple-element.200, bf16[1024,1024]{1,0:T(8,128)(2,1)S(1)} %bitcast.115), kind=kOutput, calls=%fused_computation.11 | convolution fusion | flops 2497576960 | bytes 9375744 | tf_op jit(solution)/shard_map/dot_general | solution.py:35
  194.4 5.6 %shard_map.270 = (bf16[1184,384]{1,0:T(8,128)(2,1)S(1)}, bf16[1184,384]{1,0:T(8,128)(2,1)S(1)}, bf16[1184,256]{1,0:T(8,128)(2,1)S(1)}) custom-call(bf16[1184,1024]{1,0:T(8,128)(2,1)S(1)} %get-tuple-element.191.refs_0_, bf16[1184,1024]{1,0:T(8,128)(2,1)S(1)} %get-tuple-element.192.refs_1_, bf16[1024,1024]{1,0:T(8,128)(2,1)S(1)} %bitcast.114, ...), custom_call_target="tpu_custom_call" | custom-call | flops 1048576 | bytes 262144 | tf_op jit(solution)/shard_map/pallas_call | solution.py:39
  200.0 5.1 %collective-permute-start.31 = (bf16[1184,384]{1,0:T(8,128)(2,1)S(1)}, bf16[1184,384]{1,0:T(8,128)(2,1)S(1)}, u32[]{:S(2)}, u32[]{:S(2)}) collective-permute-start(bf16[1184,384]{1,0:T(8,128)(2,1)S(1)} %get-tuple-element.193.refs_0_), channel_id=1, source_target_pairs={{0,2},{1,3},{2,0},{3,1},{4,6},{5,7},{6,4},{7,5},{8,10},{9,11},{10,... | collective-permute-start | bytes 2727944 | tf_op jit(solution)/shard_map/ppermute | solution.py:595
  218.8 4.4 %shard_map.273 = (f32[592,1024]{1,0:T(8,128)S(1)}, bf16[1184,1024]{1,0:T(8,128)(2,1)S(1)}, f32[8,1024]{1,0:T(8,128)S(1)}) custom-call(f32[1184,1024]{1,0:T(8,128)S(1)} %get-tuple-element.177.resid_ref, bf16[1184,1024]{1,0:T(8,128)(2,1)S(1)} %pad_maximum_fusion.1.rows_ref.down_ref, f32[8,1024]{1,0:T(8,128)S(1)} %pad_convert_fusion.vec_ref, ...), custom_call_target="tpu_custom_call" | custom-call | flops 1048576 | bytes 262144 | tf_op jit(solution)/shard_map/pallas_call | solution.py:39
  236.1 9.7 %shard_map.275 = (bf16[1184,768]{1,0:T(8,128)(2,1)S(1)}, f32[8,768]{1,0:T(8,128)S(1)}) custom-call(bf16[1184,768]{1,0:T(8,128)(2,1)S(1)} %copy-done.34, bf16[2,4,592,592]{3,2,1,0:T(8,128)(2,1)S(1)} %copy-done.42, bf16[1184,1024]{1,0:T(8,128)(2,1)S(1)} %copy-done.4, bf16[1024,1024]{1,0:T(8,128)(2,1)S(1)} %bitcast.95), custom_call_target="tpu_custom_call" | custom-call | flops 1048576 | bytes 262144 | tf_op jit(solution)/shard_map/pallas_call | solution.py:170
  246.5 4.2 %shard_map.276 = (bf16[1024,512]{1,0:T(8,128)(2,1)S(1)}, bf16[1024,512]{1,0:T(8,128)(2,1)S(1)}) custom-call(bf16[1184,1024]{1,0:T(8,128)(2,1)S(1)} %copy-done.15, bf16[1184,768]{1,0:T(8,128)(2,1)S(1)} %get-tuple-element.242.qkv_ref.refs_0_, bf16[1184,1024]{1,0:T(8,128)(2,1)S(1)} %copy-done.4, bf16[1184,256]{1,0:T(8,128)(2,1)S(1)} %copy-done.47), custom_call_target="tpu_custom_call" | custom-call | flops 1048576 | bytes 262144 | tf_op jit(solution)/shard_map/pallas_call | solution.py:39
  255.9 4.2 %collective-permute-done.35.moved_ref = bf16[4,2,64,512]{3,2,1,0:T(8,128)(2,1)S(1)} collective-permute-done((bf16[4,2,64,512]{3,2,1,0:T(8,128)(2,1)S(1)}, bf16[4,2,64,512]{3,2,1,0:T(8,128)(2,1)S(1)}, u32[]{:S(2)}, u32[]{:S(2)}) %collective-permute-start.35) | collective-permute-done | bytes 524320 | tf_op jit(solution)/shard_map/ppermute | solution.py:595
  266.3 9.7 %shard_map.280 = (bf16[1184,768]{1,0:T(8,128)(2,1)S(1)}, f32[8,768]{1,0:T(8,128)S(1)}) custom-call(bf16[1184,768]{1,0:T(8,128)(2,1)S(1)} %copy-done.32, bf16[2,4,592,592]{3,2,1,0:T(8,128)(2,1)S(1)} %copy-done.40, bf16[1184,1024]{1,0:T(8,128)(2,1)S(1)} %copy-done.4, bf16[1024,1024]{1,0:T(8,128)(2,1)S(1)} %bitcast.99), custom_call_target="tpu_custom_call" | custom-call | flops 1048576 | bytes 262144 | tf_op jit(solution)/shard_map/pallas_call | solution.py:170
  291.2 4.2 %shard_map.283 = (bf16[1024,512]{1,0:T(8,128)(2,1)S(1)}, bf16[1024,512]{1,0:T(8,128)(2,1)S(1)}) custom-call(bf16[1184,1024]{1,0:T(8,128)(2,1)S(1)} %copy-done.16, bf16[1184,768]{1,0:T(8,128)(2,1)S(1)} %copy-done.38, bf16[1184,1024]{1,0:T(8,128)(2,1)S(1)} %copy-done.4, bf16[1184,256]{1,0:T(8,128)(2,1)S(1)} %get-tuple-element.173.refs_1_.mixed_ref), custom_call_target="tpu_custom_call" | custom-call | flops 1048576 | bytes 262144 | tf_op jit(solution)/shard_map/pallas_call | solution.py:39
  299.4 5.7 %shard_map.285 = (bf16[592,1024]{1,0:T(8,128)(2,1)S(1)}, bf16[592,384]{1,0:T(8,128)(2,1)}, bf16[592,384]{1,0:T(8,128)(2,1)}, bf16[592,256]{1,0:T(8,128)(2,1)}) custom-call(bf16[1184,768]{1,0:T(8,128)(2,1)S(1)} %copy-done.36, bf16[1184,768]{1,0:T(8,128)(2,1)S(1)} %copy-done.38, bf16[1024,1024]{1,0:T(8,128)(2,1)S(1)} %bitcast.96, bf16[1024,1024]{1,0:T(8,128)(2,1)S(1)} %bitcast.100), custom_call_target="tpu_custom_call" | custom-call | flops 1048576 | bytes 262144 | tf_op jit(solution)/shard_map/pallas_call | solution.py:39
  311.0 16.6 %collective-permute-start.43 = (bf16[592,384]{1,0:T(8,128)(2,1)}, bf16[592,384]{1,0:T(8,128)(2,1)}, u32[]{:S(2)}, u32[]{:S(2)}) collective-permute-start(bf16[592,384]{1,0:T(8,128)(2,1)} %get-tuple-element.245), channel_id=1, source_target_pairs={{0,2},{1,3},{2,0},{3,1},{4,6},{5,7},{6,4},{7,5},{8,10},{9,11},{10,... | collective-permute-start | bytes 1363976 | tf_op jit(solution)/shard_map/ppermute | solution.py:595
  338.2 4.7 %shard_map.288 = (f32[577,1024]{1,0:T(8,128)}, f32[8,1024]{1,0:T(8,128)S(1)}) custom-call(bf16[592,1024]{1,0:T(8,128)(2,1)S(1)} %copy-done.49, bf16[1184,1024]{1,0:T(8,128)(2,1)S(1)} %copy-done.2, f32[592,1024]{1,0:T(8,128)S(1)} %copy-done.44, f32[8,1024]{1,0:T(8,128)S(1)} %copy-done.51, bf16[592,384]{1,0:T(8,128)(2,1)} %collective-permute-done.43.refs_0_, ...), custom_call_target="tpu_custom_call" | custom-call | flops 1048576 | bytes 262144 | tf_op jit(solution)/shard_map/pallas_call | solution.py:39
  345.8 6.0 %collective-permute-start.61 = (bf16[64,2048]{1,0:T(8,128)(2,1)S(1)}, bf16[64,2048]{1,0:T(8,128)(2,1)S(1)}, u32[]{:S(2)}, u32[]{:S(2)}) collective-permute-start(bf16[64,2048]{1,0:T(8,128)(2,1)S(1)} %bitcast.159), channel_id=1, source_target_pairs={{0,0},{1,2},{2,1},{3,3},{4,4},{5,6},{6,5},{7,7},{8,8},{9,10},{10,9... | collective-permute-start | bytes 786440 | tf_op jit(solution)/shard_map/ppermute | solution.py:595
  358.1 4.5 %collective-permute-start.58 = (f32[1,9216]{1,0:T(1,128)S(1)}, f32[1,9216]{1,0:T(1,128)S(1)}, u32[]{:S(2)}, u32[]{:S(2)}) collective-permute-start(f32[1,9216]{1,0:T(1,128)S(1)} %add.241), channel_id=1, source_target_pairs={{0,2},{1,3},{2,0},{3,1},{4,6},{5,7},{6,4},{7,5},{8,10},{9,11},{10,... | collective-permute-start | bytes 110600 | tf_op jit(solution)/shard_map/ppermute | solution.py:595
  371.1 6.7 %shard_map.289 = (bf16[592,1024]{1,0:T(8,128)(2,1)S(1)}, bf16[592,384]{1,0:T(8,128)(2,1)}, bf16[592,384]{1,0:T(8,128)(2,1)}, bf16[592,256]{1,0:T(8,128)(2,1)}) custom-call(bf16[1184,1024]{1,0:T(8,128)(2,1)S(1)} %copy-done.24, bf16[1184,1024]{1,0:T(8,128)(2,1)S(1)} %copy-done.26, bf16[1024,1024]{1,0:T(8,128)(2,1)S(1)} %bitcast.102, ...), custom_call_target="tpu_custom_call" | custom-call | flops 1048576 | bytes 262144 | tf_op jit(solution)/shard_map/pallas_call | solution.py:39
  (415 shorter events, 232.9 us)
Async XLA Ops:
  7.2 92.4 %all-gather.5.cloned.1.call-start = ((), (), s32[]{:S(2)}) async-start(), calls=%async_computation.6 | async-start | bytes 1310720 | tf_op jit(solution)/shard_map/all_gather | solution.py:747
  25.2 22.0 %collective-permute-start.5 = (bf16[64,2048]{1,0:T(8,128)(2,1)S(1)}, bf16[64,2048]{1,0:T(8,128)(2,1)S(1)}, u32[]{:S(2)}, u32[]{:S(2)}) collective-permute-start(bf16[64,2048]{1,0:T(8,128)(2,1)S(1)} %collective-permute-done), channel_id=1, source_target_pairs={{0,16},{1,17},{2,18},{3,19},{4,20},{5,21},{6,22},{7,23},{8,24},{9,... | collective-permute-start | bytes 786440 | tf_op jit(solution)/shard_map/ppermute | solution.py:595
  57.3 69.9 %all-gather.7.cloned.1.call-start = ((), (), s32[]{:S(2)}) async-start(), calls=%async_computation.7 | async-start | bytes 1310720 | tf_op jit(solution)/shard_map/all_gather | solution.py:748
  85.4 24.9 %collective-permute-start.12 = (bf16[4,2,64,1024]{3,2,1,0:T(8,128)(2,1)}, bf16[4,2,64,1024]{3,2,1,0:T(8,128)(2,1)}, u32[]{:S(2)}, u32[]{:S(2)}) collective-permute-start(bf16[4,2,64,1024]{3,2,1,0:T(8,128)(2,1)} %shard_map.248.refs_0_), channel_id=1, source_target_pairs={{0,1},{1,0},{2,3},{3,2},{4,5},{5,4},{6,7},{7,6},{8,9},{9,8},{10,11... | collective-permute-start | bytes 3145736 | tf_op jit(solution)/shard_map/ppermute | solution.py:595
  90.9 197.1 %reduce-scatter.4.cloned.1.call-start = ((), (), s32[]{:S(2)}) async-start(), calls=%async_computation.3 | async-start | bytes 1310720 | tf_op jit(solution)/shard_map/reduce_scatter | solution.py:702
  91.7 36.8 %collective-permute-start.18 = (bf16[4,2,64,1024]{3,2,1,0:T(8,128)(2,1)S(1)}, bf16[4,2,64,1024]{3,2,1,0:T(8,128)(2,1)}, u32[]{:S(2)}, u32[]{:S(2)}) collective-permute-start(bf16[4,2,64,1024]{3,2,1,0:T(8,128)(2,1)S(1)} %shard_map.249.refs_0_), channel_id=1, source_target_pairs={{0,4},{1,5},{2,6},{3,7},{4,0},{5,1},{6,2},{7,3},{8,12},{9,13},{10,... | collective-permute-start | bytes 3145736 | tf_op jit(solution)/shard_map/ppermute | solution.py:595
  101.8 31.1 %collective-permute-start.15 = (bf16[4,64,1024]{2,1,0:T(8,128)(2,1)}, bf16[4,64,1024]{2,1,0:T(8,128)(2,1)}, u32[]{:S(2)}, u32[]{:S(2)}) collective-permute-start(bf16[4,64,1024]{2,1,0:T(8,128)(2,1)} %get-tuple-element.158.refs_0_), channel_id=1, source_target_pairs={{0,4},{1,5},{2,6},{3,7},{4,0},{5,1},{6,2},{7,3},{8,12},{9,13},{10,... | collective-permute-start | bytes 1572872 | tf_op jit(solution)/shard_map/ppermute | solution.py:595
  102.3 33.5 %collective-permute-start.17 = (bf16[4,64,1024]{2,1,0:T(8,128)(2,1)}, bf16[4,64,1024]{2,1,0:T(8,128)(2,1)}, u32[]{:S(2)}, u32[]{:S(2)}) collective-permute-start(bf16[4,64,1024]{2,1,0:T(8,128)(2,1)} %get-tuple-element.159.refs_0_), channel_id=1, source_target_pairs={{0,1},{1,0},{2,3},{3,2},{4,5},{5,4},{6,7},{7,6},{8,9},{9,8},{10,11... | collective-permute-start | bytes 1572872 | tf_op jit(solution)/shard_map/ppermute | solution.py:595
  128.5 26.2 %collective-permute-start.25 = (bf16[4,64,1024]{2,1,0:T(8,128)(2,1)S(1)}, bf16[4,64,1024]{2,1,0:T(8,128)(2,1)S(1)}, u32[]{:S(2)}, u32[]{:S(2)}) collective-permute-start(bf16[4,64,1024]{2,1,0:T(8,128)(2,1)S(1)} %get-tuple-element.165.refs_0_), channel_id=1, source_target_pairs={{0,4},{1,5},{2,6},{3,7},{4,0},{5,1},{6,2},{7,3},{8,12},{9,13},{10,... | collective-permute-start | bytes 1572872 | tf_op jit(solution)/shard_map/ppermute | solution.py:595
  129.9 24.9 %collective-permute-start.26 = (bf16[4,64,1024]{2,1,0:T(8,128)(2,1)S(1)}, bf16[4,64,1024]{2,1,0:T(8,128)(2,1)S(1)}, u32[]{:S(2)}, u32[]{:S(2)}) collective-permute-start(bf16[4,64,1024]{2,1,0:T(8,128)(2,1)S(1)} %get-tuple-element.166.refs_0_), channel_id=1, source_target_pairs={{0,1},{1,0},{2,3},{3,2},{4,5},{5,4},{6,7},{7,6},{8,9},{9,8},{10,11... | collective-permute-start | bytes 1572872 | tf_op jit(solution)/shard_map/ppermute | solution.py:595
  137.8 26.3 %collective-permute-start.22 = (bf16[4,2,64,1024]{3,2,1,0:T(8,128)(2,1)S(1)}, bf16[4,2,64,1024]{3,2,1,0:T(8,128)(2,1)S(1)}, u32[]{:S(2)}, u32[]{:S(2)}) collective-permute-start(bf16[4,2,64,1024]{3,2,1,0:T(8,128)(2,1)S(1)} %shard_map.253.refs_0_), channel_id=1, source_target_pairs={{0,1},{1,0},{2,3},{3,2},{4,5},{5,4},{6,7},{7,6},{8,9},{9,8},{10,11... | collective-permute-start | bytes 3145736 | tf_op jit(solution)/shard_map/ppermute | solution.py:595
  138.4 26.5 %collective-permute-start.23 = (bf16[4,2,64,1024]{3,2,1,0:T(8,128)(2,1)S(1)}, bf16[4,2,64,1024]{3,2,1,0:T(8,128)(2,1)S(1)}, u32[]{:S(2)}, u32[]{:S(2)}) collective-permute-start(bf16[4,2,64,1024]{3,2,1,0:T(8,128)(2,1)S(1)} %shard_map.254.refs_0_), channel_id=1, source_target_pairs={{0,4},{1,5},{2,6},{3,7},{4,0},{5,1},{6,2},{7,3},{8,12},{9,13},{10,... | collective-permute-start | bytes 3145736 | tf_op jit(solution)/shard_map/ppermute | solution.py:595
  159.0 27.5 %collective-permute-start.27 = (bf16[4,2,64,1024]{3,2,1,0:T(8,128)(2,1)S(1)}, bf16[4,2,64,1024]{3,2,1,0:T(8,128)(2,1)S(1)}, u32[]{:S(2)}, u32[]{:S(2)}) collective-permute-start(bf16[4,2,64,1024]{3,2,1,0:T(8,128)(2,1)S(1)} %shard_map.264.refs_0_), channel_id=1, source_target_pairs={{0,1},{1,0},{2,3},{3,2},{4,5},{5,4},{6,7},{7,6},{8,9},{9,8},{10,11... | collective-permute-start | bytes 3145736 | tf_op jit(solution)/shard_map/ppermute | solution.py:595
  160.5 25.9 %collective-permute-start.28 = (bf16[4,2,64,1024]{3,2,1,0:T(8,128)(2,1)S(1)}, bf16[4,2,64,1024]{3,2,1,0:T(8,128)(2,1)S(1)}, u32[]{:S(2)}, u32[]{:S(2)}) collective-permute-start(bf16[4,2,64,1024]{3,2,1,0:T(8,128)(2,1)S(1)} %shard_map.265.refs_0_), channel_id=1, source_target_pairs={{0,4},{1,5},{2,6},{3,7},{4,0},{5,1},{6,2},{7,3},{8,12},{9,13},{10,... | collective-permute-start | bytes 3145736 | tf_op jit(solution)/shard_map/ppermute | solution.py:595
  183.7 24.2 %collective-permute-start.24 = (bf16[4,2,64,1024]{3,2,1,0:T(8,128)(2,1)S(1)}, bf16[4,2,64,1024]{3,2,1,0:T(8,128)(2,1)S(1)}, u32[]{:S(2)}, u32[]{:S(2)}) collective-permute-start(bf16[4,2,64,1024]{3,2,1,0:T(8,128)(2,1)S(1)} %get-tuple-element.182), channel_id=1, source_target_pairs={{0,1},{1,0},{2,3},{3,2},{4,5},{5,4},{6,7},{7,6},{8,9},{9,8},{10,11... | collective-permute-start | bytes 3145736 | tf_op jit(solution)/shard_map/ppermute | solution.py:595
  184.3 23.6 %collective-permute-start.29 = (bf16[4,2,64,1024]{3,2,1,0:T(8,128)(2,1)S(1)}, bf16[4,2,64,1024]{3,2,1,0:T(8,128)(2,1)S(1)}, u32[]{:S(2)}, u32[]{:S(2)}) collective-permute-start(bf16[4,2,64,1024]{3,2,1,0:T(8,128)(2,1)S(1)} %get-tuple-element.186), channel_id=1, source_target_pairs={{0,4},{1,5},{2,6},{3,7},{4,0},{5,1},{6,2},{7,3},{8,12},{9,13},{10,... | collective-permute-start | bytes 3145736 | tf_op jit(solution)/shard_map/ppermute | solution.py:595
  228.4 101.1 %reduce-scatter.6.cloned.1.call-start = ((), (), s32[]{:S(2)}) async-start(), calls=%async_computation.4 | async-start | bytes 1310720 | tf_op jit(solution)/shard_map/reduce_scatter | solution.py:702
  228.4 24.2 %collective-permute-start.36 = (bf16[4,2,64,1024]{3,2,1,0:T(8,128)(2,1)}, bf16[4,2,64,1024]{3,2,1,0:T(8,128)(2,1)S(1)}, u32[]{:S(2)}, u32[]{:S(2)}) collective-permute-start(bf16[4,2,64,1024]{3,2,1,0:T(8,128)(2,1)} %copy-done.76), channel_id=1, source_target_pairs={{0,1},{1,0},{2,3},{3,2},{4,5},{5,4},{6,7},{7,6},{8,9},{9,8},{10,11... | collective-permute-start | bytes 3145736 | tf_op jit(solution)/shard_map/ppermute | solution.py:595
  228.9 23.8 %collective-permute-start.37 = (bf16[4,2,64,1024]{3,2,1,0:T(8,128)(2,1)}, bf16[4,2,64,1024]{3,2,1,0:T(8,128)(2,1)S(1)}, u32[]{:S(2)}, u32[]{:S(2)}) collective-permute-start(bf16[4,2,64,1024]{3,2,1,0:T(8,128)(2,1)} %copy-done.75), channel_id=1, source_target_pairs={{0,4},{1,5},{2,6},{3,7},{4,0},{5,1},{6,2},{7,3},{8,12},{9,13},{10,... | collective-permute-start | bytes 3145736 | tf_op jit(solution)/shard_map/ppermute | solution.py:595
  254.1 23.8 %collective-permute-start.40 = (bf16[4,64,1024]{2,1,0:T(8,128)(2,1)S(1)}, bf16[4,64,1024]{2,1,0:T(8,128)(2,1)S(1)}, u32[]{:S(2)}, u32[]{:S(2)}) collective-permute-start(bf16[4,64,1024]{2,1,0:T(8,128)(2,1)S(1)} %get-tuple-element.225), channel_id=1, source_target_pairs={{0,4},{1,5},{2,6},{3,7},{4,0},{5,1},{6,2},{7,3},{8,12},{9,13},{10,... | collective-permute-start | bytes 1572872 | tf_op jit(solution)/shard_map/ppermute | solution.py:595
  255.1 22.8 %collective-permute-start.41 = (bf16[4,64,1024]{2,1,0:T(8,128)(2,1)S(1)}, bf16[4,64,1024]{2,1,0:T(8,128)(2,1)S(1)}, u32[]{:S(2)}, u32[]{:S(2)}) collective-permute-start(bf16[4,64,1024]{2,1,0:T(8,128)(2,1)S(1)} %get-tuple-element.231), channel_id=1, source_target_pairs={{0,1},{1,0},{2,3},{3,2},{4,5},{5,4},{6,7},{7,6},{8,9},{9,8},{10,11... | collective-permute-start | bytes 1572872 | tf_op jit(solution)/shard_map/ppermute | solution.py:595
  279.5 100.0 %reduce-scatter.8.cloned.1.call-start = ((), (), s32[]{:S(2)}) async-start(), calls=%async_computation.5 | async-start | bytes 1310720 | tf_op jit(solution)/shard_map/reduce_scatter | solution.py:702
  311.0 24.2 %collective-permute-start.43 = (bf16[592,384]{1,0:T(8,128)(2,1)}, bf16[592,384]{1,0:T(8,128)(2,1)}, u32[]{:S(2)}, u32[]{:S(2)}) collective-permute-start(bf16[592,384]{1,0:T(8,128)(2,1)} %get-tuple-element.245), channel_id=1, source_target_pairs={{0,2},{1,3},{2,0},{3,1},{4,6},{5,7},{6,4},{7,5},{8,10},{9,11},{10,... | collective-permute-start | bytes 1363976 | tf_op jit(solution)/shard_map/ppermute | solution.py:595
  363.5 21.5 %collective-permute-start.60 = (bf16[64,2048]{1,0:T(8,128)(2,1)}, bf16[64,2048]{1,0:T(8,128)(2,1)}, u32[]{:S(2)}, u32[]{:S(2)}) collective-permute-start(bf16[64,2048]{1,0:T(8,128)(2,1)} %bitcast.37), channel_id=1, source_target_pairs={{0,0},{1,2},{2,1},{3,3},{4,4},{5,6},{6,5},{7,7},{8,8},{9,10},{10,9... | collective-permute-start | bytes 786440 | tf_op jit(solution)/shard_map/ppermute | solution.py:595
  (124 other events, 1115.9 us)
Sparse Core Ops, SparseCore 0:
  57.4 27.9 all-gather.4
  91.0 26.8 all-gather.6
  228.5 30.1 reduce-scatter.3
  279.6 36.8 reduce-scatter.5
  352.0 25.4 reduce-scatter.7

commit v5 on v4

--- a/solution.py
+++ b/solution.py
@@ -742,8 +742,8 @@
             value = jnp.pad(value, ((0, ROWS - SEQ), (0, 0)))
             return jnp.concatenate([value, swap(value)])
 
-        inputs = both_images(after(tokens, *square_one))
-        down = both_images(after(cotangent, *square_one))
+        inputs = both_images(after(tokens, around[1]))
+        down = both_images(after(cotangent, around[1]))
         line_two = lax.all_gather(shard_two, "z", axis=0)
         line_three = lax.all_gather(after(shard_three, *line_one), "z", axis=0)
         share = ln1_gain.shape[0]

time: 404 us -> 386 us (0.955)
  local copies, waits for them, and re-layouts: 81.4 us -> 71.8 us
  waiting for transfers between devices: 60.5 us -> 51.6 us
    ppermute x62, waiting for transfers between devices: 60.4 us -> 51.4 us  [send(): return lax.ppermute(value, ALL, perm)]
  transfers between devices with their start and end apart: 67 -> 67, of which waited for: 21 -> 18; matrix products, arithmetic and copies ran while one was open for 13% -> 12% of each run, Pallas kernels for 29% -> 30%
where the time goes in v5:
time: 386 us; the launch traced here: 381 us
  Pallas kernels  121 us (31%)
  starting transfers between devices  92 us (24%)
  local copies, waits for them, and re-layouts  71.8 us (19%)
  waiting for transfers between devices  51.6 us (13%)
  matrix products  19.6 us (5%)
  between operations  15.6 us (4%)
  other arithmetic  9.44 us (2%)
    ppermute x62, starting transfers between devices, send(): return lax.ppermute(value, ALL, perm)  91.8 us
    pallas_call x21, Pallas kernels, call(): pl.pallas_call(kernel, grid=grid, in_specs=[pl.BlockSpec(block, at) for b...  74.1 us
    unnamed x175, local copies, waits for them, and re-layouts  53.6 us
    ppermute x62, waiting for transfers between devices, send(): return lax.ppermute(value, ALL, perm)  51.4 us
    dot_general x6, matrix products, dot(): return lax.dot_general(left, right, dims, preferred_element_type=F32)  19.6 us
    pallas_call x2, Pallas kernels, attend_back(): pl.pallas_call(kernel, grid=(2,), in_specs=[pl.BlockSpec(*image(3 * width...  19.4 us
    pallas_call x14, Pallas kernels, place(): pl.pallas_call(kernel, grid_spec=pltpu.PrefetchScalarGridSpec(num_scalar_...  18 us
    pallas_call x8, Pallas kernels, prefetched(): pl.pallas_call(kernel, grid_spec=pltpu.PrefetchScalarGridSpec(num_scalar_...  9.04 us
  transfers between devices with their start and end apart: 67, of which 18 were waited for; matrix products, arithmetic and copies ran while one was open for 12% of the time, Pallas kernels for 30%

profile of v5, /device:TPU:1, one launch (start us, length us, event | category | flops | bytes accessed | tf_op | source)
XLA Modules:
  0.0 380.7 jit_solution(3961583562618013461)
XLA Ops:
  9.0 4.7 %collective-permute-start = (bf16[64,2048]{1,0:T(8,128)(2,1)S(1)}, bf16[64,2048]{1,0:T(8,128)(2,1)S(1)}, u32[]{:S(2)}, u32[]{:S(2)}) collective-permute-start(bf16[64,2048]{1,0:T(8,128)(2,1)S(1)} %shard_map.245), channel_id=1, source_target_pairs={{0,0},{1,2},{2,1},{3,3},{4,4},{5,6},{6,5},{7,7},{8,8},{9,10},{10,9... | collective-permute-start | bytes 786440 | tf_op jit(solution)/shard_map/ppermute | solution.py:595
  23.1 4.1 %concatenate.197 = bf16[384]{0:T(512)(128)(2,1)S(1)} concatenate(bf16[32]{0:T(256)(128)(2,1)} %param.15, bf16[32]{0:T(256)(128)(2,1)} %param.16, bf16[32]{0:T(256)(128)(2,1)} %param.21, bf16[32]{0:T(256)(128)(2,1)} %param.22, bf16[32]{0:T(256)(128)(2,1)} %param.20, bf16[32]{0:T(256)(128)(2,1)} %param.26, bf16[64]{0:T(256)(128)(2,1)S(1)} %reshape.528, bf16[128]{0:T(256)(128)(2,1)S(1)} %reshape.529), dimensions={0} | concatenate | bytes 1536 | tf_op jit(solution)/shard_map/concatenate | solution.py:708
  39.1 8.1 %collective-permute-done.6 = bf16[64,2048]{1,0:T(8,128)(2,1)S(1)} collective-permute-done((bf16[64,2048]{1,0:T(8,128)(2,1)S(1)}, bf16[64,2048]{1,0:T(8,128)(2,1)S(1)}, u32[]{:S(2)}, u32[]{:S(2)}) %collective-permute-start.6) | collective-permute-done | bytes 262176 | tf_op jit(solution)/shard_map/ppermute | solution.py:595
  57.1 4.7 %collective-permute-done.9 = bf16[2,2,2,2,384]{4,3,1,0,2:T(2,128)(2,1)S(1)} collective-permute-done((bf16[2,2,2,2,384]{4,3,1,0,2:T(2,128)(2,1)S(1)}, bf16[2,2,2,2,384]{4,3,1,0,2:T(2,128)(2,1)S(1)}, u32[]{:S(2)}, u32[]{:S(2)}) %collective-permute-start.9) | collective-permute-done | bytes 12320 | tf_op jit(solution)/shard_map/ppermute | solution.py:595
  80.9 9.8 %collective-permute-done.12.refs_1_ = bf16[4,2,64,1024]{3,2,1,0:T(8,128)(2,1)} collective-permute-done((bf16[4,2,64,1024]{3,2,1,0:T(8,128)(2,1)}, bf16[4,2,64,1024]{3,2,1,0:T(8,128)(2,1)}, u32[]{:S(2)}, u32[]{:S(2)}) %collective-permute-start.12) | collective-permute-done | bytes 1048608 | tf_op jit(solution)/shard_map/ppermute | solution.py:595
  96.6 6.3 %shard_map.252 = (bf16[1184,256]{1,0:T(8,128)(2,1)S(1)}, bf16[2,4,592,592]{3,2,1,0:T(8,128)(2,1)S(1)}) custom-call(bf16[1184,768]{1,0:T(8,128)(2,1)S(1)} %fusion.10.qkv_ref), custom_call_target="tpu_custom_call" | custom-call | flops 1048576 | bytes 262144 | tf_op jit(solution)/shard_map/pallas_call | solution.py:39
  121.8 6.4 %shard_map.256 = (bf16[1184,256]{1,0:T(8,128)(2,1)S(1)}, bf16[2,4,592,592]{3,2,1,0:T(8,128)(2,1)S(1)}) custom-call(bf16[1184,768]{1,0:T(8,128)(2,1)S(1)} %fusion.11.qkv_ref), custom_call_target="tpu_custom_call" | custom-call | flops 1048576 | bytes 262144 | tf_op jit(solution)/shard_map/pallas_call | solution.py:39
  133.1 5.4 %collective-permute-start.19 = (bf16[1184,384]{1,0:T(8,128)(2,1)S(1)}, bf16[1184,384]{1,0:T(8,128)(2,1)S(1)}, u32[]{:S(2)}, u32[]{:S(2)}) collective-permute-start(bf16[1184,384]{1,0:T(8,128)(2,1)S(1)} %get-tuple-element.174.refs_0_), channel_id=1, source_target_pairs={{0,2},{1,3},{2,0},{3,1},{4,6},{5,7},{6,4},{7,5},{8,10},{9,11},{10,... | collective-permute-start | bytes 2727944 | tf_op jit(solution)/shard_map/ppermute | solution.py:595
  147.9 4.6 %fusion.4 = (bf16[1184,1024]{1,0:T(8,128)(2,1)S(1)}, bf16[1184,1024]{1,0:T(8,128)(2,1)S(1)}) fusion(f32[1024]{0:T(1024)S(1)} %get-tuple-element.315, bf16[1184,1024]{1,0:T(8,128)(2,1)S(1)} %get-tuple-element.200, bf16[1024,1024]{1,0:T(8,128)(2,1)S(1)} %bitcast.113), kind=kOutput, calls=%fused_computation.6 | convolution fusion | flops 2497576960 | bytes 9375744 | tf_op jit(solution)/shard_map/dot_general | solution.py:35
  152.5 4.6 %fusion.9 = (bf16[1184,1024]{1,0:T(8,128)(2,1)S(1)}, bf16[1184,1024]{1,0:T(8,128)(2,1)S(1)}) fusion(f32[1024]{0:T(1024)S(1)} %get-tuple-element.314, bf16[1184,1024]{1,0:T(8,128)(2,1)S(1)} %get-tuple-element.200, bf16[1024,1024]{1,0:T(8,128)(2,1)S(1)} %bitcast.115), kind=kOutput, calls=%fused_computation.11 | convolution fusion | flops 2497576960 | bytes 9375744 | tf_op jit(solution)/shard_map/dot_general | solution.py:35
  175.9 5.6 %shard_map.270 = (bf16[1184,384]{1,0:T(8,128)(2,1)S(1)}, bf16[1184,384]{1,0:T(8,128)(2,1)S(1)}, bf16[1184,256]{1,0:T(8,128)(2,1)S(1)}) custom-call(bf16[1184,1024]{1,0:T(8,128)(2,1)S(1)} %get-tuple-element.191.refs_0_, bf16[1184,1024]{1,0:T(8,128)(2,1)S(1)} %get-tuple-element.192.refs_1_, bf16[1024,1024]{1,0:T(8,128)(2,1)S(1)} %bitcast.114, ...), custom_call_target="tpu_custom_call" | custom-call | flops 1048576 | bytes 262144 | tf_op jit(solution)/shard_map/pallas_call | solution.py:39
  181.6 4.5 %collective-permute-start.31 = (bf16[1184,384]{1,0:T(8,128)(2,1)S(1)}, bf16[1184,384]{1,0:T(8,128)(2,1)S(1)}, u32[]{:S(2)}, u32[]{:S(2)}) collective-permute-start(bf16[1184,384]{1,0:T(8,128)(2,1)S(1)} %get-tuple-element.193.refs_0_), channel_id=1, source_target_pairs={{0,2},{1,3},{2,0},{3,1},{4,6},{5,7},{6,4},{7,5},{8,10},{9,11},{10,... | collective-permute-start | bytes 2727944 | tf_op jit(solution)/shard_map/ppermute | solution.py:595
  200.1 4.4 %shard_map.273 = (f32[592,1024]{1,0:T(8,128)S(1)}, bf16[1184,1024]{1,0:T(8,128)(2,1)S(1)}, f32[8,1024]{1,0:T(8,128)S(1)}) custom-call(f32[1184,1024]{1,0:T(8,128)S(1)} %get-tuple-element.177.resid_ref, bf16[1184,1024]{1,0:T(8,128)(2,1)S(1)} %pad_maximum_fusion.1.rows_ref.down_ref, f32[8,1024]{1,0:T(8,128)S(1)} %pad_convert_fusion.vec_ref, ...), custom_call_target="tpu_custom_call" | custom-call | flops 1048576 | bytes 262144 | tf_op jit(solution)/shard_map/pallas_call | solution.py:39
  217.2 9.7 %shard_map.275 = (bf16[1184,768]{1,0:T(8,128)(2,1)S(1)}, f32[8,768]{1,0:T(8,128)S(1)}) custom-call(bf16[1184,768]{1,0:T(8,128)(2,1)S(1)} %copy-done.34, bf16[2,4,592,592]{3,2,1,0:T(8,128)(2,1)S(1)} %copy-done.42, bf16[1184,1024]{1,0:T(8,128)(2,1)S(1)} %copy-done.4, bf16[1024,1024]{1,0:T(8,128)(2,1)S(1)} %bitcast.95), custom_call_target="tpu_custom_call" | custom-call | flops 1048576 | bytes 262144 | tf_op jit(solution)/shard_map/pallas_call | solution.py:170
  227.5 4.2 %shard_map.276 = (bf16[1024,512]{1,0:T(8,128)(2,1)S(1)}, bf16[1024,512]{1,0:T(8,128)(2,1)S(1)}) custom-call(bf16[1184,1024]{1,0:T(8,128)(2,1)S(1)} %copy-done.15, bf16[1184,768]{1,0:T(8,128)(2,1)S(1)} %get-tuple-element.242.qkv_ref.refs_0_, bf16[1184,1024]{1,0:T(8,128)(2,1)S(1)} %copy-done.4, bf16[1184,256]{1,0:T(8,128)(2,1)S(1)} %copy-done.47), custom_call_target="tpu_custom_call" | custom-call | flops 1048576 | bytes 262144 | tf_op jit(solution)/shard_map/pallas_call | solution.py:39
  247.4 9.7 %shard_map.280 = (bf16[1184,768]{1,0:T(8,128)(2,1)S(1)}, f32[8,768]{1,0:T(8,128)S(1)}) custom-call(bf16[1184,768]{1,0:T(8,128)(2,1)S(1)} %copy-done.32, bf16[2,4,592,592]{3,2,1,0:T(8,128)(2,1)S(1)} %copy-done.40, bf16[1184,1024]{1,0:T(8,128)(2,1)S(1)} %copy-done.4, bf16[1024,1024]{1,0:T(8,128)(2,1)S(1)} %bitcast.99), custom_call_target="tpu_custom_call" | custom-call | flops 1048576 | bytes 262144 | tf_op jit(solution)/shard_map/pallas_call | solution.py:170
  262.0 4.1 %collective-permute-done.39.refs_0_ = bf16[4,64,512]{2,1,0:T(8,128)(2,1)S(1)} collective-permute-done((bf16[4,64,512]{2,1,0:T(8,128)(2,1)}, bf16[4,64,512]{2,1,0:T(8,128)(2,1)S(1)}, u32[]{:S(2)}, u32[]{:S(2)}) %collective-permute-start.39) | collective-permute-done | bytes 262176 | tf_op jit(solution)/shard_map/ppermute | solution.py:595
  272.2 4.2 %shard_map.283 = (bf16[1024,512]{1,0:T(8,128)(2,1)S(1)}, bf16[1024,512]{1,0:T(8,128)(2,1)S(1)}) custom-call(bf16[1184,1024]{1,0:T(8,128)(2,1)S(1)} %copy-done.16, bf16[1184,768]{1,0:T(8,128)(2,1)S(1)} %copy-done.38, bf16[1184,1024]{1,0:T(8,128)(2,1)S(1)} %copy-done.4, bf16[1184,256]{1,0:T(8,128)(2,1)S(1)} %get-tuple-element.173.refs_1_.mixed_ref), custom_call_target="tpu_custom_call" | custom-call | flops 1048576 | bytes 262144 | tf_op jit(solution)/shard_map/pallas_call | solution.py:39
  280.4 5.7 %shard_map.285 = (bf16[592,1024]{1,0:T(8,128)(2,1)S(1)}, bf16[592,384]{1,0:T(8,128)(2,1)}, bf16[592,384]{1,0:T(8,128)(2,1)}, bf16[592,256]{1,0:T(8,128)(2,1)}) custom-call(bf16[1184,768]{1,0:T(8,128)(2,1)S(1)} %copy-done.36, bf16[1184,768]{1,0:T(8,128)(2,1)S(1)} %copy-done.38, bf16[1024,1024]{1,0:T(8,128)(2,1)S(1)} %bitcast.96, bf16[1024,1024]{1,0:T(8,128)(2,1)S(1)} %bitcast.100), custom_call_target="tpu_custom_call" | custom-call | flops 1048576 | bytes 262144 | tf_op jit(solution)/shard_map/pallas_call | solution.py:39
  292.1 16.5 %collective-permute-start.43 = (bf16[592,384]{1,0:T(8,128)(2,1)}, bf16[592,384]{1,0:T(8,128)(2,1)}, u32[]{:S(2)}, u32[]{:S(2)}) collective-permute-start(bf16[592,384]{1,0:T(8,128)(2,1)} %get-tuple-element.245), channel_id=1, source_target_pairs={{0,2},{1,3},{2,0},{3,1},{4,6},{5,7},{6,4},{7,5},{8,10},{9,11},{10,... | collective-permute-start | bytes 1363976 | tf_op jit(solution)/shard_map/ppermute | solution.py:595
  319.2 4.7 %shard_map.288 = (f32[577,1024]{1,0:T(8,128)}, f32[8,1024]{1,0:T(8,128)S(1)}) custom-call(bf16[592,1024]{1,0:T(8,128)(2,1)S(1)} %copy-done.49, bf16[1184,1024]{1,0:T(8,128)(2,1)S(1)} %copy-done.2, f32[592,1024]{1,0:T(8,128)S(1)} %copy-done.44, f32[8,1024]{1,0:T(8,128)S(1)} %copy-done.51, bf16[592,384]{1,0:T(8,128)(2,1)} %collective-permute-done.43.refs_0_, ...), custom_call_target="tpu_custom_call" | custom-call | flops 1048576 | bytes 262144 | tf_op jit(solution)/shard_map/pallas_call | solution.py:39
  326.9 6.1 %collective-permute-start.61 = (bf16[64,2048]{1,0:T(8,128)(2,1)S(1)}, bf16[64,2048]{1,0:T(8,128)(2,1)S(1)}, u32[]{:S(2)}, u32[]{:S(2)}) collective-permute-start(bf16[64,2048]{1,0:T(8,128)(2,1)S(1)} %bitcast.160), channel_id=1, source_target_pairs={{0,0},{1,2},{2,1},{3,3},{4,4},{5,6},{6,5},{7,7},{8,8},{9,10},{10,9... | collective-permute-start | bytes 786440 | tf_op jit(solution)/shard_map/ppermute | solution.py:595
  339.3 6.0 %collective-permute-start.58 = (f32[1,9216]{1,0:T(1,128)S(1)}, f32[1,9216]{1,0:T(1,128)S(1)}, u32[]{:S(2)}, u32[]{:S(2)}) collective-permute-start(f32[1,9216]{1,0:T(1,128)S(1)} %add.241), channel_id=1, source_target_pairs={{0,2},{1,3},{2,0},{3,1},{4,6},{5,7},{6,4},{7,5},{8,10},{9,11},{10,... | collective-permute-start | bytes 110600 | tf_op jit(solution)/shard_map/ppermute | solution.py:595
  353.0 6.7 %shard_map.289 = (bf16[592,1024]{1,0:T(8,128)(2,1)S(1)}, bf16[592,384]{1,0:T(8,128)(2,1)}, bf16[592,384]{1,0:T(8,128)(2,1)}, bf16[592,256]{1,0:T(8,128)(2,1)}) custom-call(bf16[1184,1024]{1,0:T(8,128)(2,1)S(1)} %copy-done.24, bf16[1184,1024]{1,0:T(8,128)(2,1)S(1)} %copy-done.26, bf16[1024,1024]{1,0:T(8,128)(2,1)S(1)} %bitcast.102, ...), custom_call_target="tpu_custom_call" | custom-call | flops 1048576 | bytes 262144 | tf_op jit(solution)/shard_map/pallas_call | solution.py:39
  (415 shorter events, 214.4 us)
Async XLA Ops:
  7.2 70.1 %all-gather.5.cloned.1.call-start = ((), (), s32[]{:S(2)}) async-start(), calls=%async_computation.6 | async-start | bytes 1310720 | tf_op jit(solution)/shard_map/all_gather | solution.py:747
  39.0 68.6 %all-gather.7.cloned.1.call-start = ((), (), s32[]{:S(2)}) async-start(), calls=%async_computation.7 | async-start | bytes 1310720 | tf_op jit(solution)/shard_map/all_gather | solution.py:748
  67.2 23.5 %collective-permute-start.12 = (bf16[4,2,64,1024]{3,2,1,0:T(8,128)(2,1)}, bf16[4,2,64,1024]{3,2,1,0:T(8,128)(2,1)}, u32[]{:S(2)}, u32[]{:S(2)}) collective-permute-start(bf16[4,2,64,1024]{3,2,1,0:T(8,128)(2,1)} %shard_map.249.refs_0_), channel_id=1, source_target_pairs={{0,1},{1,0},{2,3},{3,2},{4,5},{5,4},{6,7},{7,6},{8,9},{9,8},{10,11... | collective-permute-start | bytes 3145736 | tf_op jit(solution)/shard_map/ppermute | solution.py:595
  69.8 199.2 %reduce-scatter.4.cloned.1.call-start = ((), (), s32[]{:S(2)}) async-start(), calls=%async_computation.3 | async-start | bytes 1310720 | tf_op jit(solution)/shard_map/reduce_scatter | solution.py:702
  69.9 38.9 %collective-permute-start.18 = (bf16[4,2,64,1024]{3,2,1,0:T(8,128)(2,1)S(1)}, bf16[4,2,64,1024]{3,2,1,0:T(8,128)(2,1)}, u32[]{:S(2)}, u32[]{:S(2)}) collective-permute-start(bf16[4,2,64,1024]{3,2,1,0:T(8,128)(2,1)S(1)} %shard_map.250.refs_0_), channel_id=1, source_target_pairs={{0,4},{1,5},{2,6},{3,7},{4,0},{5,1},{6,2},{7,3},{8,12},{9,13},{10,... | collective-permute-start | bytes 3145736 | tf_op jit(solution)/shard_map/ppermute | solution.py:595
  79.5 33.8 %collective-permute-start.15 = (bf16[4,64,1024]{2,1,0:T(8,128)(2,1)}, bf16[4,64,1024]{2,1,0:T(8,128)(2,1)}, u32[]{:S(2)}, u32[]{:S(2)}) collective-permute-start(bf16[4,64,1024]{2,1,0:T(8,128)(2,1)} %get-tuple-element.157.refs_0_), channel_id=1, source_target_pairs={{0,4},{1,5},{2,6},{3,7},{4,0},{5,1},{6,2},{7,3},{8,12},{9,13},{10,... | collective-permute-start | bytes 1572872 | tf_op jit(solution)/shard_map/ppermute | solution.py:595
  80.9 35.3 %collective-permute-start.17 = (bf16[4,64,1024]{2,1,0:T(8,128)(2,1)}, bf16[4,64,1024]{2,1,0:T(8,128)(2,1)}, u32[]{:S(2)}, u32[]{:S(2)}) collective-permute-start(bf16[4,64,1024]{2,1,0:T(8,128)(2,1)} %get-tuple-element.158.refs_0_), channel_id=1, source_target_pairs={{0,1},{1,0},{2,3},{3,2},{4,5},{5,4},{6,7},{7,6},{8,9},{9,8},{10,11... | collective-permute-start | bytes 1572872 | tf_op jit(solution)/shard_map/ppermute | solution.py:595
  108.9 29.6 %collective-permute-start.25 = (bf16[4,64,1024]{2,1,0:T(8,128)(2,1)S(1)}, bf16[4,64,1024]{2,1,0:T(8,128)(2,1)S(1)}, u32[]{:S(2)}, u32[]{:S(2)}) collective-permute-start(bf16[4,64,1024]{2,1,0:T(8,128)(2,1)S(1)} %get-tuple-element.164.refs_0_), channel_id=1, source_target_pairs={{0,4},{1,5},{2,6},{3,7},{4,0},{5,1},{6,2},{7,3},{8,12},{9,13},{10,... | collective-permute-start | bytes 1572872 | tf_op jit(solution)/shard_map/ppermute | solution.py:595
  109.7 28.9 %collective-permute-start.26 = (bf16[4,64,1024]{2,1,0:T(8,128)(2,1)S(1)}, bf16[4,64,1024]{2,1,0:T(8,128)(2,1)S(1)}, u32[]{:S(2)}, u32[]{:S(2)}) collective-permute-start(bf16[4,64,1024]{2,1,0:T(8,128)(2,1)S(1)} %get-tuple-element.165.refs_0_), channel_id=1, source_target_pairs={{0,1},{1,0},{2,3},{3,2},{4,5},{5,4},{6,7},{7,6},{8,9},{9,8},{10,11... | collective-permute-start | bytes 1572872 | tf_op jit(solution)/shard_map/ppermute | solution.py:595
  118.2 27.9 %collective-permute-start.22 = (bf16[4,2,64,1024]{3,2,1,0:T(8,128)(2,1)S(1)}, bf16[4,2,64,1024]{3,2,1,0:T(8,128)(2,1)S(1)}, u32[]{:S(2)}, u32[]{:S(2)}) collective-permute-start(bf16[4,2,64,1024]{3,2,1,0:T(8,128)(2,1)S(1)} %shard_map.253.refs_0_), channel_id=1, source_target_pairs={{0,1},{1,0},{2,3},{3,2},{4,5},{5,4},{6,7},{7,6},{8,9},{9,8},{10,11... | collective-permute-start | bytes 3145736 | tf_op jit(solution)/shard_map/ppermute | solution.py:595
  118.2 28.8 %collective-permute-start.23 = (bf16[4,2,64,1024]{3,2,1,0:T(8,128)(2,1)S(1)}, bf16[4,2,64,1024]{3,2,1,0:T(8,128)(2,1)S(1)}, u32[]{:S(2)}, u32[]{:S(2)}) collective-permute-start(bf16[4,2,64,1024]{3,2,1,0:T(8,128)(2,1)S(1)} %shard_map.254.refs_0_), channel_id=1, source_target_pairs={{0,4},{1,5},{2,6},{3,7},{4,0},{5,1},{6,2},{7,3},{8,12},{9,13},{10,... | collective-permute-start | bytes 3145736 | tf_op jit(solution)/shard_map/ppermute | solution.py:595
  142.7 25.3 %collective-permute-start.27 = (bf16[4,2,64,1024]{3,2,1,0:T(8,128)(2,1)S(1)}, bf16[4,2,64,1024]{3,2,1,0:T(8,128)(2,1)S(1)}, u32[]{:S(2)}, u32[]{:S(2)}) collective-permute-start(bf16[4,2,64,1024]{3,2,1,0:T(8,128)(2,1)S(1)} %shard_map.264.refs_0_), channel_id=1, source_target_pairs={{0,1},{1,0},{2,3},{3,2},{4,5},{5,4},{6,7},{7,6},{8,9},{9,8},{10,11... | collective-permute-start | bytes 3145736 | tf_op jit(solution)/shard_map/ppermute | solution.py:595
  142.7 25.2 %collective-permute-start.28 = (bf16[4,2,64,1024]{3,2,1,0:T(8,128)(2,1)S(1)}, bf16[4,2,64,1024]{3,2,1,0:T(8,128)(2,1)S(1)}, u32[]{:S(2)}, u32[]{:S(2)}) collective-permute-start(bf16[4,2,64,1024]{3,2,1,0:T(8,128)(2,1)S(1)} %shard_map.265.refs_0_), channel_id=1, source_target_pairs={{0,4},{1,5},{2,6},{3,7},{4,0},{5,1},{6,2},{7,3},{8,12},{9,13},{10,... | collective-permute-start | bytes 3145736 | tf_op jit(solution)/shard_map/ppermute | solution.py:595
  165.8 22.8 %collective-permute-start.24 = (bf16[4,2,64,1024]{3,2,1,0:T(8,128)(2,1)S(1)}, bf16[4,2,64,1024]{3,2,1,0:T(8,128)(2,1)S(1)}, u32[]{:S(2)}, u32[]{:S(2)}) collective-permute-start(bf16[4,2,64,1024]{3,2,1,0:T(8,128)(2,1)S(1)} %get-tuple-element.182), channel_id=1, source_target_pairs={{0,1},{1,0},{2,3},{3,2},{4,5},{5,4},{6,7},{7,6},{8,9},{9,8},{10,11... | collective-permute-start | bytes 3145736 | tf_op jit(solution)/shard_map/ppermute | solution.py:595
  167.4 21.7 %collective-permute-start.29 = (bf16[4,2,64,1024]{3,2,1,0:T(8,128)(2,1)S(1)}, bf16[4,2,64,1024]{3,2,1,0:T(8,128)(2,1)S(1)}, u32[]{:S(2)}, u32[]{:S(2)}) collective-permute-start(bf16[4,2,64,1024]{3,2,1,0:T(8,128)(2,1)S(1)} %get-tuple-element.186), channel_id=1, source_target_pairs={{0,4},{1,5},{2,6},{3,7},{4,0},{5,1},{6,2},{7,3},{8,12},{9,13},{10,... | collective-permute-start | bytes 3145736 | tf_op jit(solution)/shard_map/ppermute | solution.py:595
  209.7 100.8 %reduce-scatter.6.cloned.1.call-start = ((), (), s32[]{:S(2)}) async-start(), calls=%async_computation.4 | async-start | bytes 1310720 | tf_op jit(solution)/shard_map/reduce_scatter | solution.py:702
  209.7 24.2 %collective-permute-start.36 = (bf16[4,2,64,1024]{3,2,1,0:T(8,128)(2,1)}, bf16[4,2,64,1024]{3,2,1,0:T(8,128)(2,1)S(1)}, u32[]{:S(2)}, u32[]{:S(2)}) collective-permute-start(bf16[4,2,64,1024]{3,2,1,0:T(8,128)(2,1)} %copy-done.76), channel_id=1, source_target_pairs={{0,1},{1,0},{2,3},{3,2},{4,5},{5,4},{6,7},{7,6},{8,9},{9,8},{10,11... | collective-permute-start | bytes 3145736 | tf_op jit(solution)/shard_map/ppermute | solution.py:595
  210.1 23.9 %collective-permute-start.37 = (bf16[4,2,64,1024]{3,2,1,0:T(8,128)(2,1)}, bf16[4,2,64,1024]{3,2,1,0:T(8,128)(2,1)S(1)}, u32[]{:S(2)}, u32[]{:S(2)}) collective-permute-start(bf16[4,2,64,1024]{3,2,1,0:T(8,128)(2,1)} %copy-done.75), channel_id=1, source_target_pairs={{0,4},{1,5},{2,6},{3,7},{4,0},{5,1},{6,2},{7,3},{8,12},{9,13},{10,... | collective-permute-start | bytes 3145736 | tf_op jit(solution)/shard_map/ppermute | solution.py:595
  235.4 23.6 %collective-permute-start.40 = (bf16[4,64,1024]{2,1,0:T(8,128)(2,1)S(1)}, bf16[4,64,1024]{2,1,0:T(8,128)(2,1)S(1)}, u32[]{:S(2)}, u32[]{:S(2)}) collective-permute-start(bf16[4,64,1024]{2,1,0:T(8,128)(2,1)S(1)} %get-tuple-element.225), channel_id=1, source_target_pairs={{0,4},{1,5},{2,6},{3,7},{4,0},{5,1},{6,2},{7,3},{8,12},{9,13},{10,... | collective-permute-start | bytes 1572872 | tf_op jit(solution)/shard_map/ppermute | solution.py:595
  236.0 23.0 %collective-permute-start.41 = (bf16[4,64,1024]{2,1,0:T(8,128)(2,1)S(1)}, bf16[4,64,1024]{2,1,0:T(8,128)(2,1)S(1)}, u32[]{:S(2)}, u32[]{:S(2)}) collective-permute-start(bf16[4,64,1024]{2,1,0:T(8,128)(2,1)S(1)} %get-tuple-element.231), channel_id=1, source_target_pairs={{0,1},{1,0},{2,3},{3,2},{4,5},{5,4},{6,7},{7,6},{8,9},{9,8},{10,11... | collective-permute-start | bytes 1572872 | tf_op jit(solution)/shard_map/ppermute | solution.py:595
  260.6 101.5 %reduce-scatter.8.cloned.1.call-start = ((), (), s32[]{:S(2)}) async-start(), calls=%async_computation.5 | async-start | bytes 1310720 | tf_op jit(solution)/shard_map/reduce_scatter | solution.py:702
  292.1 24.2 %collective-permute-start.43 = (bf16[592,384]{1,0:T(8,128)(2,1)}, bf16[592,384]{1,0:T(8,128)(2,1)}, u32[]{:S(2)}, u32[]{:S(2)}) collective-permute-start(bf16[592,384]{1,0:T(8,128)(2,1)} %get-tuple-element.245), channel_id=1, source_target_pairs={{0,2},{1,3},{2,0},{3,1},{4,6},{5,7},{6,4},{7,5},{8,10},{9,11},{10,... | collective-permute-start | bytes 1363976 | tf_op jit(solution)/shard_map/ppermute | solution.py:595
  339.3 22.6 %collective-permute-start.58 = (f32[1,9216]{1,0:T(1,128)S(1)}, f32[1,9216]{1,0:T(1,128)S(1)}, u32[]{:S(2)}, u32[]{:S(2)}) collective-permute-start(f32[1,9216]{1,0:T(1,128)S(1)} %add.241), channel_id=1, source_target_pairs={{0,2},{1,3},{2,0},{3,1},{4,6},{5,7},{6,4},{7,5},{8,10},{9,11},{10,... | collective-permute-start | bytes 110600 | tf_op jit(solution)/shard_map/ppermute | solution.py:595
  346.1 20.7 %collective-permute-start.60 = (bf16[64,2048]{1,0:T(8,128)(2,1)}, bf16[64,2048]{1,0:T(8,128)(2,1)}, u32[]{:S(2)}, u32[]{:S(2)}) collective-permute-start(bf16[64,2048]{1,0:T(8,128)(2,1)} %bitcast.37), channel_id=1, source_target_pairs={{0,0},{1,2},{2,1},{3,3},{4,4},{5,6},{6,5},{7,7},{8,8},{9,10},{10,9... | collective-permute-start | bytes 786440 | tf_op jit(solution)/shard_map/ppermute | solution.py:595
  (124 other events, 1133.7 us)
Sparse Core Ops, SparseCore 0:
  39.1 27.8 all-gather.4
  69.9 26.4 all-gather.6
  209.8 28.8 reduce-scatter.3
  260.7 36.7 reduce-scatter.5
  333.1 27.0 reduce-scatter.7
